TPU v7x, 32 devices: a whole 2x2x4 slice. The times are simulated.
32 devices in a mesh: section: 2 (over x), dp: 8 (over z, y), tensor: 2 (over core).
Axes of the slice: x: 2, y: 2, z: 4, core: 2. Of those that a mesh axis runs over, the one named last changes fastest.
Arguments:
- tokens: bfloat16 [8192, 768], P(('dp', 'tensor')), may hold values from -6 to 6
- segment_ids: int32 [32, 256], P('dp'), may hold values from 0 to 3, never falling along the last dimension, each value on 1 to 128 neighbouring positions
- out_cotangent: bfloat16 [8192, 768], P(('dp', 'tensor')), may hold values from -6 to 6
- w_qkv: bfloat16 [2, 768, 3, 768], P('section', None, None, 'tensor'), may hold values from -0.21875 to 0.21875
- qv_bias: bfloat16 [2, 2, 768], P('section', None, 'tensor'), may hold values from -3 to 3
- w_out: bfloat16 [2, 768, 768], P('section', 'tensor'), may hold values from -0.875 to 0.875
- w_up: bfloat16 [2, 768, 3072], P('section', None, 'tensor'), may hold values from -0.21875 to 0.21875
- up_bias: bfloat16 [2, 3072], P('section', 'tensor'), may hold values from -3 to 3
- w_down: bfloat16 [2, 3072, 768], P('section', 'tensor'), may hold values from -0.15625 to 0.15625
- add_bias: float32 [2, 2, 768], P('section'), may hold values from -3 to 3
- norm_gain: float32 [2, 2, 768], P('section'), may hold values from 0.5 to 1.5
- norm_bias: float32 [2, 2, 768], P('section'), may hold values from -3 to 3
Outputs:
- layer_outputs: bfloat16 [2, 8192, 768], P('section', ('dp', 'tensor'))
- input_grads: float32 [2, 8192, 768], P('section', ('dp', 'tensor'))
- grad_w_qkv: float32 [2, 768, 3, 768], P('section', None, None, 'tensor')
- grad_qv_bias: float32 [2, 2, 768], P('section', None, 'tensor')
- grad_w_out: float32 [2, 768, 768], P('section', 'tensor')
- grad_w_up: float32 [2, 768, 3072], P('section', None, 'tensor')
- grad_up_bias: float32 [2, 3072], P('section', 'tensor')
- grad_w_down: float32 [2, 3072, 768], P('section', 'tensor')
- grad_add_bias: float32 [2, 2, 768], P('section', None, 'tensor')
- grad_norm_gain: float32 [2, 2, 768], P('section', None, 'tensor')
- grad_norm_bias: float32 [2, 2, 768], P('section', None, 'tensor')
Inputs may be any that keep to these rules, and one draw needn't show every extreme that they name: `segment_ids`: along each packed sequence the numbers never fall; each number covers 1 to 128 rows; rows attend only to rows with the same number in the same sequence.
All inputs are finite; a program needn't handle non-finite values.
Results may differ from a plain program's by a relative error of at most 0.02.
Values may be sent and summed in bfloat16 or wider, within the bound.
A program may use at most 192 MiB of HBM per device.

v0:
```python
from functools import partial

import jax
import jax.numpy as jnp
from jax import lax
from jax.sharding import PartitionSpec as P

HEAD_DIM = 64
MICRO = 2


norm_eps = 1e-12
masked_score = -1e30


def as_sent(shard):
    return jax.tree.map(lambda a: a.astype(jnp.bfloat16) if a.dtype == jnp.float32 else a, shard)


def shifted(value, axis, steps):
    count = lax.axis_size(axis)
    initial, last = (max(0, -steps), min(count, count - steps))
    return lax.ppermute(value, axis, [(source, source + steps) for source in range(initial, last)])


def gelu_exact(pre_active):
    return jax.nn.gelu(pre_active, approximate=False)


def layer_norm(residual, gain_row, shift_row):
    centered = residual - jnp.mean(residual, axis=-1, keepdims=True)
    scaled = lax.rsqrt(jnp.mean(centered * centered, axis=-1, keepdims=True) + norm_eps)
    normed = centered * scaled
    return (normed * gain_row + shift_row, normed, scaled)


def norm_back(grad_output, normed, scaled, gain_row):
    weighted = grad_output * gain_row
    grad_input = scaled * (
        weighted
        - jnp.mean(weighted, axis=-1, keepdims=True)
        - normed * jnp.mean(weighted * normed, axis=-1, keepdims=True)
    )
    return (grad_input, jnp.sum(grad_output * normed, axis=0), jnp.sum(grad_output, axis=0))


def score_block(query_rows, key_rows, seg_block):
    scores = jnp.einsum(
        "sqhe,skhe->shqk", query_rows, key_rows, preferred_element_type=jnp.float32
    ) * HEAD_DIM ** (-0.5)
    same_pair = (seg_block[:, :, None] == seg_block[:, None, :])[:, None]
    return jnp.where(same_pair, scores, masked_score)


def attend(query_rows, key_rows, value_rows, seg_block):
    scores = score_block(query_rows, key_rows, seg_block)
    largest = jnp.max(scores, axis=-1, keepdims=True)
    totals = jnp.sum(jnp.exp(scores - largest), axis=-1, keepdims=True)
    log_total = largest + jnp.log(totals)
    weights = jnp.exp(scores - log_total).astype(jnp.bfloat16)
    mixed_heads = jnp.einsum(
        "shqk,skhe->sqhe", weights, value_rows, preferred_element_type=jnp.float32
    )
    return (mixed_heads, log_total)


def attend_back(query_rows, key_rows, value_rows, seg_block, log_total, grad_mixed):
    weights = jnp.exp(score_block(query_rows, key_rows, seg_block) - log_total)
    grad_values = jnp.einsum(
        "shqk,sqhe->skhe",
        weights.astype(jnp.bfloat16),
        grad_mixed,
        preferred_element_type=jnp.float32,
    )
    grad_weights = jnp.einsum(
        "sqhe,skhe->shqk", grad_mixed, value_rows, preferred_element_type=jnp.float32
    )
    centre = jnp.sum(weights * grad_weights, axis=-1, keepdims=True)
    grad_scores = (weights * (grad_weights - centre)).astype(jnp.bfloat16)
    score_scale = HEAD_DIM ** (-0.5)
    grad_query = (
        jnp.einsum("shqk,skhe->sqhe", grad_scores, key_rows, preferred_element_type=jnp.float32)
        * score_scale
    )
    grad_keys = (
        jnp.einsum("shqk,sqhe->skhe", grad_scores, query_rows, preferred_element_type=jnp.float32)
        * score_scale
    )
    return (grad_query, grad_keys, grad_values)


def layer_forward(token_rows, seg_block, params):
    w_qkv, qv_bias, w_out, w_up, up_bias, w_down, add_bias, norm_gain, norm_bias = params
    model_width = w_qkv.shape[0]
    column_count = w_qkv.shape[-1]
    head_count = column_count // HEAD_DIM
    local_count = token_rows.shape[0]
    full_rows = jax.tree.map(
        lambda part, own: part.astype(own.dtype),
        lax.all_gather(as_sent(token_rows), "tensor", axis=0, tiled=True),
        token_rows,
    )
    projected = jnp.dot(
        full_rows, w_qkv.reshape(model_width, 3 * column_count), preferred_element_type=jnp.float32
    )
    projected = projected.reshape(-1, 3, column_count)
    head_shape = (seg_block.shape[0], seg_block.shape[1], head_count, HEAD_DIM)
    query_rows = (projected[:, 0] + qv_bias[0]).astype(jnp.bfloat16).reshape(head_shape)
    key_rows = projected[:, 1].astype(jnp.bfloat16).reshape(head_shape)
    value_rows = (projected[:, 2] + qv_bias[1]).astype(jnp.bfloat16).reshape(head_shape)
    mixed_heads, log_total = attend(query_rows, key_rows, value_rows, seg_block)
    mixed_heads = mixed_heads.reshape(-1, column_count).astype(jnp.bfloat16)
    attended = lax.psum_scatter(
        jnp.dot(
            lax.slice_in_dim(mixed_heads, 0, lax.axis_size("tensor") * local_count, axis=0),
            w_out,
            preferred_element_type=jnp.float32,
        ),
        "tensor",
        scatter_dimension=0,
        tiled=True,
    )
    residual = token_rows.astype(jnp.float32) + attended + add_bias[0]
    hidden, normed_one, scaled_one = layer_norm(residual, norm_gain[0], norm_bias[0])
    hidden_low = hidden.astype(jnp.bfloat16)
    full_hidden = lax.all_gather(hidden_low, "tensor", axis=0, tiled=True)
    pre_active = jnp.dot(full_hidden, w_up, preferred_element_type=jnp.float32) + up_bias
    active = gelu_exact(pre_active).astype(jnp.bfloat16)
    branch_out = lax.psum_scatter(
        jnp.dot(
            lax.slice_in_dim(active, 0, local_count * lax.axis_size("tensor"), axis=0),
            w_down,
            preferred_element_type=jnp.float32,
        ).astype(jnp.bfloat16),
        "tensor",
        scatter_dimension=0,
        tiled=True,
    ).astype(jnp.float32)
    residual_two = hidden + branch_out + add_bias[1]
    output, normed_two, scaled_two = layer_norm(residual_two, norm_gain[1], norm_bias[1])
    saved = (
        full_rows,
        query_rows,
        key_rows,
        value_rows,
        seg_block,
        log_total,
        mixed_heads,
        full_hidden,
        pre_active,
        active,
        normed_one,
        scaled_one,
        normed_two,
        scaled_two,
    )
    return (output, saved)


def layer_backward(grad_output, saved, params):
    (
        full_rows,
        query_rows,
        key_rows,
        value_rows,
        seg_block,
        log_total,
        mixed_heads,
        full_hidden,
        pre_active,
        active,
        normed_one,
        scaled_one,
        normed_two,
        scaled_two,
    ) = saved
    w_qkv, qv_bias, w_out, w_up, up_bias, w_down, add_bias, norm_gain, norm_bias = params
    model_width = w_qkv.shape[0]
    column_count = w_qkv.shape[-1]
    local_count = grad_output.shape[0]
    grad_two, grad_gain_two, grad_shift_two = norm_back(
        grad_output, normed_two, scaled_two, norm_gain[1]
    )
    branch_grad = grad_two.astype(jnp.bfloat16)
    full_branch = lax.all_gather(branch_grad, "tensor", axis=0, tiled=True)
    grad_down = jnp.einsum("mf,md->fd", active, full_branch, preferred_element_type=jnp.float32)
    grad_active = jnp.einsum("md,fd->mf", full_branch, w_down, preferred_element_type=jnp.float32)
    _, gelu_pull = jax.vjp(gelu_exact, pre_active)
    grad_pre = gelu_pull(grad_active)[0]
    grad_up_bias = jnp.sum(grad_pre, axis=0)
    grad_pre_low = grad_pre.astype(jnp.bfloat16)
    grad_up = jnp.einsum("md,mf->df", full_hidden, grad_pre_low, preferred_element_type=jnp.float32)
    grad_hidden = lax.psum_scatter(
        jnp.einsum(
            "mf,df->md",
            lax.slice_in_dim(grad_pre_low, 0, local_count * lax.axis_size("tensor"), axis=0),
            w_up,
            preferred_element_type=jnp.float32,
        ).astype(jnp.bfloat16),
        "tensor",
        scatter_dimension=0,
        tiled=True,
    ).astype(jnp.float32)
    grad_hidden = grad_hidden + grad_two
    grad_one, grad_gain_one, grad_shift_one = norm_back(
        grad_hidden, normed_one, scaled_one, norm_gain[0]
    )
    attn_grad = grad_one.astype(jnp.bfloat16)
    full_attn = lax.all_gather(attn_grad, "tensor", axis=0, tiled=True)
    grad_out_weight = jnp.einsum(
        "mc,md->cd", mixed_heads, full_attn, preferred_element_type=jnp.float32
    )
    grad_mixed = jnp.einsum("md,cd->mc", full_attn, w_out, preferred_element_type=jnp.float32)
    grad_mixed = grad_mixed.astype(jnp.bfloat16).reshape(query_rows.shape)
    grad_query, grad_keys, grad_values = attend_back(
        query_rows, key_rows, value_rows, seg_block, log_total, grad_mixed
    )
    grad_query = grad_query.astype(jnp.bfloat16).reshape(-1, column_count)
    grad_keys = grad_keys.astype(jnp.bfloat16).reshape(-1, column_count)
    grad_values = grad_values.astype(jnp.bfloat16).reshape(-1, column_count)
    grad_proj = jnp.stack([grad_query, grad_keys, grad_values], axis=1).reshape(
        -1, 3 * column_count
    )
    grad_qv = jnp.stack(
        [
            jnp.sum(grad_query.astype(jnp.float32), axis=0),
            jnp.sum(grad_values.astype(jnp.float32), axis=0),
        ]
    )
    grad_qkv = jnp.einsum(
        "md,mc->dc", full_rows, grad_proj, preferred_element_type=jnp.float32
    ).reshape(model_width, 3, column_count)
    flat_qkv = w_qkv.reshape(model_width, 3 * column_count)
    grad_rows = lax.psum_scatter(
        jnp.einsum(
            "mc,dc->md",
            lax.slice_in_dim(grad_proj, 0, local_count * lax.axis_size("tensor"), axis=0),
            flat_qkv,
            preferred_element_type=jnp.float32,
        ).astype(jnp.bfloat16),
        "tensor",
        scatter_dimension=0,
        tiled=True,
    ).astype(jnp.float32)
    grad_rows = grad_rows + grad_one
    grad_add = jnp.stack([jnp.sum(grad_one, axis=0), jnp.sum(grad_two, axis=0)])
    grad_gain = jnp.stack([grad_gain_one, grad_gain_two])
    grad_shift = jnp.stack([grad_shift_one, grad_shift_two])
    return (
        grad_rows,
        (
            grad_qkv,
            grad_qv,
            grad_out_weight,
            grad_up,
            grad_up_bias,
            grad_down,
            grad_add,
            grad_gain,
            grad_shift,
        ),
    )


def pick_section(section_first, early_item, late_item):
    return jax.tree.map(partial(jnp.where, section_first), early_item, late_item)


def shards(
    tokens,
    segment_ids,
    out_cotangent,
    w_qkv,
    qv_bias,
    w_out,
    w_up,
    up_bias,
    w_down,
    add_bias,
    norm_gain,
    norm_bias,
):
    section_first = lax.axis_index("section") == 0
    tensor_count = lax.axis_size("tensor")
    model_width = tokens.shape[1]
    local_count = tokens.shape[0] // MICRO
    seq_length = segment_ids.shape[1]
    token_blocks = tokens.reshape(MICRO, local_count, model_width)
    cot_blocks = out_cotangent.reshape(MICRO, local_count, model_width)
    seg_groups = segment_ids.reshape(tensor_count, MICRO, -1, seq_length)
    params = (
        w_qkv[0],
        qv_bias[0],
        w_out[0],
        w_up[0],
        up_bias[0],
        w_down[0],
        add_bias[0],
        norm_gain[0],
        norm_bias[0],
    )
    seg_blocks = [seg_groups[:, number].reshape(-1, seq_length) for number in range(MICRO)]
    incoming = jnp.zeros((local_count, model_width), jnp.bfloat16)
    layer_blocks = [incoming for number in range(MICRO)]
    stored = []
    for step_index in range(MICRO + 1):
        own_block = min(step_index, MICRO - 1)
        prior_block = max(step_index - 1, 0)
        source_rows = jnp.where(section_first, token_blocks[own_block], incoming)
        seg_block = jnp.where(section_first, seg_blocks[own_block], seg_blocks[prior_block])
        result, saved = layer_forward(source_rows, seg_block, params)
        result_low = result.astype(jnp.bfloat16)
        for number in range(MICRO):
            landed = jnp.where(section_first, step_index == number, step_index - 1 == number)
            layer_blocks[number] = jnp.where(landed, result_low, layer_blocks[number])
        stored.append((source_rows, seg_block))
        if step_index < MICRO:
            incoming = shifted(result_low, "section", 1)
    returning = jnp.zeros((local_count, model_width), jnp.bfloat16)
    grad_blocks = [jnp.zeros((local_count, model_width), jnp.float32) for number in range(MICRO)]
    summed = None
    for step_index in range(MICRO + 1):
        own_block = min(step_index, MICRO - 1)
        early_step = max(step_index - 1, 0)
        late_step = min(step_index + 1, MICRO)
        active_step = jnp.where(section_first, step_index >= 1, step_index < MICRO)
        grad_output = jnp.where(section_first, returning, cot_blocks[own_block]).astype(jnp.float32)
        chosen = pick_section(section_first, stored[early_step], stored[late_step])
        _, saved = layer_forward(chosen[0], chosen[1], params)
        grad_rows, grads = layer_backward(grad_output, saved, params)
        grads = jax.tree.map(
            partial(jnp.where, active_step), grads, jax.tree.map(jnp.zeros_like, grads)
        )
        summed = grads if summed is None else jax.tree.map(jnp.add, summed, grads)
        for number in range(MICRO):
            landed = jnp.where(section_first, step_index - 1 == number, step_index == number)
            grad_blocks[number] = jnp.where(landed, grad_rows, grad_blocks[number])
        if step_index < MICRO:
            returning = shifted(grad_rows.astype(jnp.bfloat16), "section", -1)
    (
        grad_qkv,
        grad_qv,
        grad_out_weight,
        grad_up,
        grad_up_bias,
        grad_down,
        grad_add,
        grad_gain,
        grad_shift,
    ) = summed
    grad_add, grad_gain, grad_shift = (
        lax.psum_scatter(grad_add, "tensor", scatter_dimension=1, tiled=True),
        lax.psum_scatter(grad_gain, "tensor", scatter_dimension=1, tiled=True),
        lax.psum_scatter(grad_shift, "tensor", scatter_dimension=1, tiled=True),
    )
    totals = (
        lax.psum(grad_qkv.astype(jnp.bfloat16), "dp").astype(jnp.float32),
        lax.psum(grad_qv.astype(jnp.bfloat16), "dp").astype(jnp.float32),
        lax.psum(grad_out_weight.astype(jnp.bfloat16), "dp").astype(jnp.float32),
        lax.psum(grad_up.astype(jnp.bfloat16), "dp").astype(jnp.float32),
        lax.psum(grad_up_bias.astype(jnp.bfloat16), "dp").astype(jnp.float32),
        lax.psum(grad_down.astype(jnp.bfloat16), "dp").astype(jnp.float32),
        lax.psum(grad_add.astype(jnp.bfloat16), "dp").astype(jnp.float32),
        lax.psum(grad_gain.astype(jnp.bfloat16), "dp").astype(jnp.float32),
        lax.psum(grad_shift.astype(jnp.bfloat16), "dp").astype(jnp.float32),
    )
    layer_rows = jnp.concatenate(layer_blocks, axis=0)[None]
    input_rows = jnp.concatenate(grad_blocks, axis=0)[None]
    return (layer_rows, input_rows) + tuple((member[None] for member in totals))


def solution(mesh):
    return jax.shard_map(
        shards,
        mesh=mesh,
        in_specs=(
            P(("dp", "tensor"), None),
            P("dp", None),
            P(("dp", "tensor"), None),
            P("section", None, None, "tensor"),
            P("section", None, "tensor"),
            P("section", "tensor", None),
            P("section", None, "tensor"),
            P("section", "tensor"),
            P("section", "tensor", None),
            P("section", None, None),
            P("section", None, None),
            P("section", None, None),
        ),
        out_specs=(
            P("section", ("dp", "tensor"), None),
            P("section", ("dp", "tensor"), None),
            P("section", None, None, "tensor"),
            P("section", None, "tensor"),
            P("section", "tensor", None),
            P("section", None, "tensor"),
            P("section", "tensor"),
            P("section", "tensor", None),
            P("section", None, "tensor"),
            P("section", None, "tensor"),
            P("section", None, "tensor"),
        ),
        check_vma=False,
    )
```

profile of v0, /device:TPU:0, one launch (start us, length us, event | category | flops | bytes accessed | tf_op | source)
XLA Modules:
  0.0 888.1 jit_solution(15020476119399507771)
XLA Ops:
  10.9 3.8 copy.247
  14.7 2.7 fusion.102
  30.9 3.1 fusion.174
  36.5 11.6 %reduce-scatter.28.cloned.1.call-done = f32[256,768]{1,0:T(8,128)} async-done(((f32[512,768]{1,0:T(8,128)}), f32[256,768]{1,0:T(8,128)}) %reduce-scatter.28.cloned.1.call-update) | async-done | bytes 786448 | tf_op jit(solution)/shard_map/reduce_scatter | solution.py:113
  52.5 2.7 all_gather.55
  55.2 11.5 %fusion.132 = bf16[512,768]{1,0:T(8,128)(2,1)} fusion(bf16[1,1536,768]{2,1,0:T(8,128)(2,1)} %param.20, bf16[512,768]{1,0:T(8,128)(2,1)} %all_gather.55, bf16[1,768,1536]{2,1,0:T(8,128)(2,1)S(1)} %copy-done, f32[1536]{0:T(1024)S(1)} %convert_reduce_fusion.9), kind=kOutput, calls=%fused_computation.214 | convolution fusion | flops 2468216832 | bytes 6297600 | tf_op jit(solution)/shard_map/dot_general | solution.py:130
  66.8 9.5 %reduce-scatter.30.cloned.1.call-done = bf16[256,768]{1,0:T(8,128)(2,1)} async-done(((bf16[512,768]{1,0:T(8,128)(2,1)}), bf16[256,768]{1,0:T(8,128)(2,1)}) %reduce-scatter.30.cloned.1.call-update) | async-done | bytes 393232 | tf_op jit(solution)/shard_map/reduce_scatter | solution.py:129
  78.7 3.8 collective-permute-start
  83.3 8.0 collective-permute-done
  92.1 2.6 all_gather.56
  115.7 3.0 fusion.175
  121.2 3.0 all_gather.62
  124.1 3.0 fusion.94
  131.5 2.5 squeeze.41
  151.3 9.2 %reduce-scatter.44.cloned.1.call-done = f32[256,768]{1,0:T(8,128)} async-done(((f32[512,768]{1,0:T(8,128)}), f32[256,768]{1,0:T(8,128)}) %reduce-scatter.44.cloned.1.call-update) | async-done | bytes 786448 | tf_op jit(solution)/shard_map/reduce_scatter | solution.py:113
  166.9 9.7 %multiply_convert_fusion.4 = (bf16[512,1536]{1,0:T(8,128)(2,1)S(1)}, f32[512,1536]{1,0:T(8,128)}, f32[512,1536]{1,0:T(8,128)}) fusion(f32[1536]{0:T(1024)S(1)} %copy-done.165, bf16[512,768]{1,0:T(8,128)(2,1)S(1)} %all_gather.63, bf16[1,768,1536]{2,1,0:T(8,128)(2,1)S(1)} %copy-done), kind=kOutput, calls=%fused_computation.52 | convolution fusion | flops 1259864064 | bytes 11016192 | tf_op jit(solution)/shard_map/dot_general | solution.py:127
  180.2 4.3 all_gather.57
  184.5 11.5 %fusion.135 = bf16[512,768]{1,0:T(8,128)(2,1)} fusion(bf16[1,1536,768]{2,1,0:T(8,128)(2,1)} %param.20, bf16[512,768]{1,0:T(8,128)(2,1)} %all_gather.57, bf16[1,768,1536]{2,1,0:T(8,128)(2,1)S(1)} %copy-done, f32[1536]{0:T(1024)} %copy-done.164), kind=kOutput, calls=%fused_computation.215 | convolution fusion | flops 2468216832 | bytes 6297600 | tf_op jit(solution)/shard_map/dot_general | solution.py:130
  196.1 9.5 %reduce-scatter.34.cloned.1.call-done = bf16[256,768]{1,0:T(8,128)(2,1)} async-done(((bf16[512,768]{1,0:T(8,128)(2,1)}), bf16[256,768]{1,0:T(8,128)(2,1)}) %reduce-scatter.34.cloned.1.call-update) | async-done | bytes 393232 | tf_op jit(solution)/shard_map/reduce_scatter | solution.py:129
  205.7 3.5 fusion.441
  210.8 3.6 collective-permute-start.1
  215.2 8.0 collective-permute-done.1
  224.8 2.6 all_gather.58
  244.5 3.1 fusion.176
  253.9 3.0 fusion.92
  260.5 2.6 squeeze.43
  267.6 2.6 squeeze.88
  277.1 2.8 all_gather.60
  279.9 3.0 fusion.96
  304.2 2.6 fusion.206
  311.6 5.1 fusion.458
  328.2 3.5 reduce-scatter.48.cloned.1.call-done
  331.8 4.6 multiply_reduce_fusion.5
  346.6 3.7 convert_reduce_fusion.7
  371.3 3.6 convolution_convert_fusion.2
  374.9 2.8 all_gather.69
  377.7 10.7 %multiply_convert_fusion.1 = (bf16[512,1536]{1,0:T(8,128)(2,1)S(1)}, f32[512,1536]{1,0:T(8,128)}, f32[512,1536]{1,0:T(8,128)}) fusion(f32[1536]{0:T(1024)} %copy-done.164, bf16[512,768]{1,0:T(8,128)(2,1)S(1)} %all_gather.69, bf16[1,768,1536]{2,1,0:T(8,128)(2,1)S(1)} %copy-done), kind=kOutput, calls=%fused_computation.30 | convolution fusion | flops 1259864064 | bytes 11016192 | tf_op jit(solution)/shard_map/dot_general | solution.py:127
  393.3 11.1 %multiply_convert_fusion.5 = (bf16[512,1536]{1,0:T(8,128)(2,1)S(1)}, f32[512,1536]{1,0:T(8,128)}, f32[512,1536]{1,0:T(8,128)}) fusion(f32[1536]{0:T(1024)} %copy-done.164, bf16[512,768]{1,0:T(8,128)(2,1)} %all_gather.61, bf16[1,768,1536]{2,1,0:T(8,128)(2,1)S(1)} %copy-done), kind=kOutput, calls=%fused_computation.68 | convolution fusion | flops 1259864064 | bytes 11016192 | tf_op jit(solution)/shard_map/dot_general | solution.py:127
  409.7 11.5 %fusion.138 = bf16[512,768]{1,0:T(8,128)(2,1)} fusion(bf16[1,1536,768]{2,1,0:T(8,128)(2,1)} %param.20, bf16[512,768]{1,0:T(8,128)(2,1)} %all_gather.59, bf16[1,768,1536]{2,1,0:T(8,128)(2,1)S(1)} %copy-done, f32[1536]{0:T(1024)} %copy-done.164), kind=kOutput, calls=%fused_computation.216 | convolution fusion | flops 2468216832 | bytes 6297600 | tf_op jit(solution)/shard_map/dot_general | solution.py:130
  424.7 6.3 reduce-scatter.38.cloned.1.call-done
  431.0 4.4 fusion.437
  442.8 2.9 fusion.457
  449.2 8.6 reduce-scatter.52.cloned.1.call-done
  457.9 2.6 multiply_reduce_fusion.4
  472.3 3.7 convert_reduce_fusion.5
  495.2 3.6 convolution_convert_fusion.1
  501.6 5.3 fusion.459
  506.9 3.6 fusion.235
  510.5 3.0 fusion.180
  513.6 2.6 select_select_fusion.1
  517.8 11.5 %collective-permute-done.3 = bf16[256,768]{1,0:T(8,128)(2,1)S(1)} collective-permute-done((bf16[256,768]{1,0:T(8,128)(2,1)S(1)}, bf16[256,768]{1,0:T(8,128)(2,1)S(1)}, u32[]{:S(2)}, u32[]{:S(2)}) %collective-permute-start.3) | collective-permute-done | bytes 393248 | tf_op jit(solution)/shard_map/ppermute | solution.py:23
  533.8 5.1 fusion.456
  548.6 5.4 fusion.460
  554.0 3.6 fusion.232
  559.3 3.0 fusion.178
  575.1 4.4 convert_reduce_fusion.3
  600.4 3.6 convolution_convert_fusion
  604.1 6.2 fusion.48
  610.3 5.5 fusion.49
  617.1 2.6 fusion.122
  632.5 39.2 %all-reduce = (bf16[1,2,384]{2,1,0:T(2,128)(2,1)S(1)}, bf16[1,1536]{1,0:T(2,128)(2,1)S(1)}, bf16[1,2,384]{2,1,0:T(2,128)(2,1)S(1)}, bf16[1,2,384]{2,1,0:T(2,128)(2,1)S(1)}, bf16[1,2,384]{2,1,0:T(2,128)(2,1)S(1)}) all-reduce(bf16[1,2,384]{2,1,0:T(2,128)(2,1)S(1)} %fusion.319, ...), channel_id=1, replica_groups=mesh['section'=2,'dp'=8,'tensor'=2] {'dp'}, use_global_device_ids=true, to_apply=%region_76.77 | all-reduce | flops 4608 | bytes 18432 | tf_op jit(solution)/shard_map/psum | solution.py:358
  677.5 193.3 %all-reduce.4.cloned.1.call-done = (bf16[1,768,3,384]{3,1,2,0:T(8,128)(2,1)}, bf16[1,384,768]{2,1,0:T(8,128)(2,1)}, bf16[1,768,1536]{2,1,0:T(8,128)(2,1)}, bf16[1,1536,768]{2,1,0:T(8,128)(2,1)}) async-done(((bf16[1,768,3,384]{3,1,2,0:T(8,128)(2,1)}, bf16[1,384,768]{2,1,0:T(8,128)(2,1)}, bf16[1,768,1536]{2,1,0:T(8,128)(2,1)}, bf16[1,1536,768]{2,1,0:T(8,128)(2,1)}), (bf16[1,768,3,384]{3,1,2,0:T(8,128)(2,1)}, ...) | async-done | bytes 7077904 | tf_op jit(solution)/shard_map/psum | solution.py:357
  870.7 4.6 broadcast_in_dim.226
  875.4 2.5 broadcast_in_dim.230
  (718 shorter events, 325.3 us)
Async XLA Ops:
  7.2 48.0 %copy-start = (bf16[1,768,1536]{2,1,0:T(8,128)(2,1)S(1)}, bf16[1,768,1536]{2,1,0:T(8,128)(2,1)}, u32[]{:S(2)}) copy-start(bf16[1,768,1536]{2,1,0:T(8,128)(2,1)} %param.18) | copy-start | bytes 7077892
  7.2 40.9 %reduce-scatter.28.cloned.1.call-start = ((), (), s32[]{:S(2)}) async-start(), calls=%async_computation.21 | async-start | bytes 2359296 | tf_op jit(solution)/shard_map/reduce_scatter | solution.py:113
  36.2 40.1 %reduce-scatter.30.cloned.1.call-start = ((), (), s32[]{:S(2)}) async-start(), calls=%async_computation.22 | async-start | bytes 1179648 | tf_op jit(solution)/shard_map/reduce_scatter | solution.py:129
  36.3 18.9 %copy-start.164 = (f32[1536]{0:T(1024)}, f32[1536]{0:T(1024)S(1)}, u32[]{:S(2)}) copy-start(f32[1536]{0:T(1024)S(1)} %convert_reduce_fusion.9) | copy-start | bytes 18436
  36.4 40.0 %copy-start.129 = (f32[768]{0:T(1024)}, f32[768]{0:T(1024)S(1)}, u32[]{:S(2)}) copy-start(f32[768]{0:T(1024)S(1)} %get-tuple-element.42) | copy-start | bytes 9220
  36.5 39.9 %copy-start.114 = (f32[768]{0:T(1024)}, f32[768]{0:T(1024)S(1)}, u32[]{:S(2)}) copy-start(f32[768]{0:T(1024)S(1)} %get-tuple-element.41) | copy-start | bytes 9220
  36.5 42.0 %copy-start.126 = (f32[768]{0:T(1024)}, f32[768]{0:T(1024)S(1)}, u32[]{:S(2)}) copy-start(f32[768]{0:T(1024)S(1)} %get-tuple-element.40) | copy-start | bytes 9220
  66.7 15.8 %copy-start.143 = (s32[2,1,1,256]{3,1,0,2:T(1,128)S(1)}, s32[2,1,1,256]{3,1,0,2:T(1,128)}, u32[]{:S(2)}) copy-start(s32[2,1,1,256]{3,1,0,2:T(1,128)} %get-tuple-element.135) | copy-start | bytes 6148
  66.7 15.8 %copy-start.146 = (s32[2,1,1,256]{3,1,0,2:T(1,128)S(1)}, s32[2,1,1,256]{3,1,0,2:T(1,128)}, u32[]{:S(2)}) copy-start(s32[2,1,1,256]{3,1,0,2:T(1,128)} %copy-done.145) | copy-start | bytes 6148
  66.8 82.7 %reduce-scatter.32.cloned.1.call-start = ((), (), s32[]{:S(2)}) async-start(), calls=%async_computation.23 | async-start | bytes 2359296 | tf_op jit(solution)/shard_map/reduce_scatter | solution.py:113
  76.3 15.0 %copy-start.19 = (bf16[512,768]{1,0:T(8,128)(2,1)S(1)}, bf16[512,768]{1,0:T(8,128)(2,1)}, u32[]{:S(2)}) copy-start(bf16[512,768]{1,0:T(8,128)(2,1)} %param.12) | copy-start | bytes 2359300
  78.2 13.9 %copy-start.26 = (f32[256,768]{1,0:T(8,128)}, f32[256,768]{1,0:T(8,128)S(1)}, u32[]{:S(2)}) copy-start(f32[256,768]{1,0:T(8,128)S(1)} %get-tuple-element.98) | copy-start | bytes 2359300
  78.2 16.5 %copy-start.7 = (bf16[1,768,3,384]{1,3,2,0:T(8,128)(2,1)S(1)}, bf16[1,768,3,384]{1,3,2,0:T(8,128)(2,1)}, u32[]{:S(2)}) copy-start(bf16[1,768,3,384]{1,3,2,0:T(8,128)(2,1)} %copy.247) | copy-start | bytes 5308420
  78.7 12.6 %collective-permute-start = (bf16[256,768]{1,0:T(8,128)(2,1)S(1)}, bf16[256,768]{1,0:T(8,128)(2,1)S(1)}, u32[]{:S(2)}, u32[]{:S(2)}) collective-permute-start(bf16[256,768]{1,0:T(8,128)(2,1)S(1)} %add_convert_fusion.5), channel_id=1, source_target_pairs={{0,16},{1,17},{2,18},{3,19},{4,20},{5,21},{6,22},{7,23},{8,24},{9,... | collective-permute-start | bytes 1179656 | tf_op jit(solution)/shard_map/ppermute | solution.py:23
  120.9 39.5 %reduce-scatter.44.cloned.1.call-start = ((), (), s32[]{:S(2)}) async-start(), calls=%async_computation.29 | async-start | bytes 2359296 | tf_op jit(solution)/shard_map/reduce_scatter | solution.py:113
  121.1 24.2 %copy-start.58 = (pred[2,256,256]{1,2,0:T(8,128)(4,1)}, pred[2,256,256]{1,2,0:T(8,128)(4,1)S(1)}, u32[]{:S(2)}) copy-start(pred[2,256,256]{1,2,0:T(8,128)(4,1)S(1)} %broadcast_compare_fusion.1) | copy-start | bytes 393220
  149.3 46.8 %reduce-scatter.46.cloned.1.call-start = ((), (), s32[]{:S(2)}) async-start(), calls=%async_computation.30 | async-start | bytes 1179648 | tf_op jit(solution)/shard_map/reduce_scatter | solution.py:129
  162.4 43.3 %copy-start.9 = (f32[256,768]{1,0:T(8,128)}, f32[256,768]{1,0:T(8,128)S(1)}, u32[]{:S(2)}) copy-start(f32[256,768]{1,0:T(8,128)S(1)} %get-tuple-element.82) | copy-start | bytes 2359300
  166.9 9.8 %copy-start.67 = (bf16[512,768]{1,0:T(8,128)(2,1)}, bf16[512,768]{1,0:T(8,128)(2,1)S(1)}, u32[]{:S(2)}) copy-start(bf16[512,768]{1,0:T(8,128)(2,1)S(1)} %all_gather.63) | copy-start | bytes 2359300
  166.9 11.0 %copy-start.173 = (bf16[1,1536,768]{2,1,0:T(8,128)(2,1)S(1)}, bf16[1,1536,768]{2,1,0:T(8,128)(2,1)}, u32[]{:S(2)}) copy-start(bf16[1,1536,768]{2,1,0:T(8,128)(2,1)} %param.20) | copy-start | bytes 7077892
  180.1 25.5 %reduce-scatter.34.cloned.1.call-start = ((), (), s32[]{:S(2)}) async-start(), calls=%async_computation.24 | async-start | bytes 1179648 | tf_op jit(solution)/shard_map/reduce_scatter | solution.py:129
  196.1 124.3 %reduce-scatter.36.cloned.1.call-start = ((), (), s32[]{:S(2)}) async-start(), calls=%async_computation.25 | async-start | bytes 2359296 | tf_op jit(solution)/shard_map/reduce_scatter | solution.py:113
  205.7 17.5 %copy-start.20 = (bf16[512,768]{1,0:T(8,128)(2,1)S(1)}, bf16[512,768]{1,0:T(8,128)(2,1)}, u32[]{:S(2)}) copy-start(bf16[512,768]{1,0:T(8,128)(2,1)} %param.12) | copy-start | bytes 2359300
  209.2 18.2 %copy-start.8 = (bf16[1,768,3,384]{1,3,2,0:T(8,128)(2,1)S(1)}, bf16[1,768,3,384]{1,3,2,0:T(8,128)(2,1)}, u32[]{:S(2)}) copy-start(bf16[1,768,3,384]{1,3,2,0:T(8,128)(2,1)} %copy.247) | copy-start | bytes 5308420
  210.8 13.3 %copy-start.105 = (bf16[256,768]{1,0:T(8,128)(2,1)}, bf16[256,768]{1,0:T(8,128)(2,1)S(1)}, u32[]{:S(2)}) copy-start(bf16[256,768]{1,0:T(8,128)(2,1)S(1)} %get-tuple-element.92) | copy-start | bytes 1179652
  210.8 12.5 %collective-permute-start.1 = (bf16[256,768]{1,0:T(8,128)(2,1)S(1)}, bf16[256,768]{1,0:T(8,128)(2,1)S(1)}, u32[]{:S(2)}, u32[]{:S(2)}) collective-permute-start(bf16[256,768]{1,0:T(8,128)(2,1)S(1)} %get-tuple-element.92), channel_id=1, source_target_pairs={{0,16},{1,17},{2,18},{3,19},{4,20},{5,21},{6,22},{7,23},{8,24},{9,... | collective-permute-start | bytes 1179656 | tf_op jit(solution)/shard_map/ppermute | solution.py:23
  249.9 72.5 %reduce-scatter.56.cloned.1.call-start = ((), (), s32[]{:S(2)}) async-start(), calls=%async_computation.35 | async-start | bytes 2359296 | tf_op jit(solution)/shard_map/reduce_scatter | solution.py:113
  260.5 9.7 %copy-start.56 = (pred[2,256,256]{1,2,0:T(8,128)(4,1)S(1)}, pred[2,256,256]{1,2,0:T(8,128)(4,1)}, u32[]{:S(2)}) copy-start(pred[2,256,256]{1,2,0:T(8,128)(4,1)} %broadcast_compare_fusion) | copy-start | bytes 393220
  276.9 45.5 %reduce-scatter.40.cloned.1.call-start = ((), (), s32[]{:S(2)}) async-start(), calls=%async_computation.27 | async-start | bytes 2359296 | tf_op jit(solution)/shard_map/reduce_scatter | solution.py:113
  277.1 21.6 %copy-start.60 = (pred[2,256,256]{1,2,0:T(8,128)(4,1)}, pred[2,256,256]{1,2,0:T(8,128)(4,1)S(1)}, u32[]{:S(2)}) copy-start(pred[2,256,256]{1,2,0:T(8,128)(4,1)S(1)} %broadcast_compare_fusion.2) | copy-start | bytes 393220
  302.6 29.2 %reduce-scatter.48.cloned.1.call-start = ((), (), s32[]{:S(2)}) async-start(), calls=%async_computation.31 | async-start | bytes 1179648 | tf_op jit(solution)/shard_map/reduce_scatter | solution.py:193
  302.6 8.9 %copy-start.174 = (bf16[1,1536,768]{2,1,0:T(8,128)(2,1)S(1)}, bf16[1,1536,768]{2,1,0:T(8,128)(2,1)}, u32[]{:S(2)}) copy-start(bf16[1,1536,768]{2,1,0:T(8,128)(2,1)} %param.20) | copy-start | bytes 7077892
  302.6 8.9 %copy-start.180 = (f32[512,1536]{1,0:T(8,128)S(1)}, f32[512,1536]{1,0:T(8,128)}, u32[]{:S(2)}) copy-start(f32[512,1536]{1,0:T(8,128)} %get-tuple-element.80) | copy-start | bytes 9437188
  320.2 101.1 %reduce-scatter.50.cloned.1.call-start = ((), (), s32[]{:S(2)}) async-start(), calls=%async_computation.32 | async-start | bytes 1179648 | tf_op jit(solution)/shard_map/reduce_scatter | solution.py:234
  374.9 49.8 %reduce-scatter.58.cloned.1.call-start = ((), (), s32[]{:S(2)}) async-start(), calls=%async_computation.36 | async-start | bytes 1179648 | tf_op jit(solution)/shard_map/reduce_scatter | solution.py:129
  377.7 10.7 %copy-start.62 = (bf16[512,768]{1,0:T(8,128)(2,1)}, bf16[512,768]{1,0:T(8,128)(2,1)S(1)}, u32[]{:S(2)}) copy-start(bf16[512,768]{1,0:T(8,128)(2,1)S(1)} %all_gather.69) | copy-start | bytes 2359300
  377.7 10.7 %copy-start.108 = (bf16[256,768]{1,0:T(8,128)(2,1)S(1)}, bf16[256,768]{1,0:T(8,128)(2,1)}, u32[]{:S(2)}) copy-start(bf16[256,768]{1,0:T(8,128)(2,1)} %get-tuple-element.126) | copy-start | bytes 1179652
  377.7 13.2 %copy-start.175 = (bf16[1,1536,768]{2,1,0:T(8,128)(2,1)S(1)}, bf16[1,1536,768]{2,1,0:T(8,128)(2,1)}, u32[]{:S(2)}) copy-start(bf16[1,1536,768]{2,1,0:T(8,128)(2,1)} %param.20) | copy-start | bytes 7077892
  393.3 31.4 %reduce-scatter.42.cloned.1.call-start = ((), (), s32[]{:S(2)}) async-start(), calls=%async_computation.28 | async-start | bytes 1179648 | tf_op jit(solution)/shard_map/reduce_scatter | solution.py:129
  393.3 11.1 %copy-start.107 = (bf16[256,768]{1,0:T(8,128)(2,1)S(1)}, bf16[256,768]{1,0:T(8,128)(2,1)}, u32[]{:S(2)}) copy-start(bf16[256,768]{1,0:T(8,128)(2,1)} %get-tuple-element.125) | copy-start | bytes 1179652
  393.3 13.6 %copy-start.176 = (bf16[1,1536,768]{2,1,0:T(8,128)(2,1)S(1)}, bf16[1,1536,768]{2,1,0:T(8,128)(2,1)}, u32[]{:S(2)}) copy-start(bf16[1,1536,768]{2,1,0:T(8,128)(2,1)} %param.20) | copy-start | bytes 7077892
  409.2 21.8 %reduce-scatter.38.cloned.1.call-start = ((), (), s32[]{:S(2)}) async-start(), calls=%async_computation.26 | async-start | bytes 1179648 | tf_op jit(solution)/shard_map/reduce_scatter | solution.py:129
  421.2 36.6 %reduce-scatter.52.cloned.1.call-start = ((), (), s32[]{:S(2)}) async-start(), calls=%async_computation.33 | async-start | bytes 1179648 | tf_op jit(solution)/shard_map/reduce_scatter | solution.py:193
  423.3 13.4 %collective-permute-start.2 = (bf16[256,768]{1,0:T(8,128)(2,1)}, bf16[256,768]{1,0:T(8,128)(2,1)}, u32[]{:S(2)}, u32[]{:S(2)}) collective-permute-start(bf16[256,768]{1,0:T(8,128)(2,1)} %fusion.259), channel_id=1, source_target_pairs={{16,0},{17,1},{18,2},{19,3},{20,4},{21,5},{22,6},{23,7},{24,8},{25... | collective-permute-start | bytes 1179656 | tf_op jit(solution)/shard_map/ppermute | solution.py:23
  431.0 11.8 %copy-start.182 = (f32[512,1536]{1,0:T(8,128)S(1)}, f32[512,1536]{1,0:T(8,128)}, u32[]{:S(2)}) copy-start(f32[512,1536]{1,0:T(8,128)} %get-tuple-element.150) | copy-start | bytes 9437188
  446.8 11.0 %copy-start.135 = (f32[256]{0:T(256)S(1)}, f32[256]{0:T(256)}, u32[]{:S(2)}) copy-start(f32[256]{0:T(256)} %copy-done.134) | copy-start | bytes 3076
  446.9 11.0 %copy-start.139 = (f32[256]{0:T(256)S(1)}, f32[256]{0:T(256)}, u32[]{:S(2)}) copy-start(f32[256]{0:T(256)} %add_rsqrt_fusion.5) | copy-start | bytes 3076
  449.2 64.3 %reduce-scatter.54.cloned.1.call-start = ((), (), s32[]{:S(2)}) async-start(), calls=%async_computation.34 | async-start | bytes 1179648 | tf_op jit(solution)/shard_map/reduce_scatter | solution.py:234
  457.9 9.3 %copy-start.15 = (bf16[1,384,768]{2,1,0:T(8,128)(2,1)S(1)}, bf16[1,384,768]{2,1,0:T(8,128)(2,1)}, u32[]{:S(2)}) copy-start(bf16[1,384,768]{2,1,0:T(8,128)(2,1)} %param.17) | copy-start | bytes 1769476
  462.9 9.4 %copy-start.61 = (pred[2,256,256]{1,2,0:T(8,128)(4,1)S(1)}, pred[2,256,256]{1,2,0:T(8,128)(4,1)}, u32[]{:S(2)}) copy-start(pred[2,256,256]{1,2,0:T(8,128)(4,1)} %copy-done.60) | copy-start | bytes 393220
  462.9 9.4 %copy-start.120 = (f32[2,6,256]{2,1,0:T(8,128)S(1)}, f32[2,6,256]{2,1,0:T(8,128)}, u32[]{:S(2)}) copy-start(f32[2,6,256]{2,1,0:T(8,128)} %copy-done.119) | copy-start | bytes 36868
  498.8 63.5 %reduce-scatter.60.cloned.1.call-start = ((), (), s32[]{:S(2)}) async-start(), calls=%async_computation.37 | async-start | bytes 1179648 | tf_op jit(solution)/shard_map/reduce_scatter | solution.py:193
  513.5 15.7 %copy-start.82 = (bf16[512,768]{1,0:T(8,128)(2,1)S(1)}, bf16[512,768]{1,0:T(8,128)(2,1)}, u32[]{:S(2)}) copy-start(bf16[512,768]{1,0:T(8,128)(2,1)} %param.14) | copy-start | bytes 2359300
  516.2 13.1 %collective-permute-start.3 = (bf16[256,768]{1,0:T(8,128)(2,1)S(1)}, bf16[256,768]{1,0:T(8,128)(2,1)S(1)}, u32[]{:S(2)}, u32[]{:S(2)}) collective-permute-start(bf16[256,768]{1,0:T(8,128)(2,1)S(1)} %get-tuple-element.112), channel_id=1, source_target_pairs={{16,0},{17,1},{18,2},{19,3},{20,4},{21,5},{22,6},{23,7},{24,8},{25... | collective-permute-start | bytes 1179656 | tf_op jit(solution)/shard_map/ppermute | solution.py:23
  517.5 16.3 %copy-start.178 = (bf16[1,1536,768]{2,1,0:T(8,128)(2,1)S(1)}, bf16[1,1536,768]{2,1,0:T(8,128)(2,1)}, u32[]{:S(2)}) copy-start(bf16[1,1536,768]{2,1,0:T(8,128)(2,1)} %param.20) | copy-start | bytes 7077892
  517.5 16.3 %copy-start.179 = (f32[512,1536]{1,0:T(8,128)S(1)}, f32[512,1536]{1,0:T(8,128)}, u32[]{:S(2)}) copy-start(f32[512,1536]{1,0:T(8,128)} %get-tuple-element.67) | copy-start | bytes 9437188
  542.5 86.9 %reduce-scatter.68.cloned.1.call-start = ((), (), s32[]{:S(2)}) async-start(), calls=%async_computation.41 | async-start | bytes 589824
  565.7 9.4 %copy-start.57 = (pred[2,256,256]{1,2,0:T(8,128)(4,1)S(1)}, pred[2,256,256]{1,2,0:T(8,128)(4,1)}, u32[]{:S(2)}) copy-start(pred[2,256,256]{1,2,0:T(8,128)(4,1)} %broadcast_compare_fusion) | copy-start | bytes 393220
  565.7 9.4 %copy-start.116 = (f32[2,6,256]{2,1,0:T(8,128)S(1)}, f32[2,6,256]{2,1,0:T(8,128)}, u32[]{:S(2)}) copy-start(f32[2,6,256]{2,1,0:T(8,128)} %copy-done.115) | copy-start | bytes 36868
  585.2 45.2 %reduce-scatter.66.cloned.1.call-start = ((), (), s32[]{:S(2)}) async-start(), calls=%async_computation.40 | async-start | bytes 589824
  587.7 43.7 %reduce-scatter.64.cloned.1.call-start = ((), (), s32[]{:S(2)}) async-start(), calls=%async_computation.39 | async-start | bytes 589824
  598.2 76.4 %reduce-scatter.62.cloned.1.call-start = ((), (), s32[]{:S(2)}) async-start(), calls=%async_computation.38 | async-start | bytes 1179648 | tf_op jit(solution)/shard_map/reduce_scatter | solution.py:234
  604.0 266.8 %all-reduce.4.cloned.1.call-start = ((), (), s32[]{:S(2)}) async-start(), calls=%async_computation.42 | async-start | bytes 14155776 | tf_op jit(solution)/shard_map/psum | solution.py:357
  619.7 54.9 %copy-start.30 = (f32[256,768]{1,0:T(8,128)S(1)}, f32[256,768]{1,0:T(8,128)}, u32[]{:S(2)}) copy-start(f32[256,768]{1,0:T(8,128)} %copy-done.29) | copy-start | bytes 2359300
  (145 other events, 484.7 us)
Sparse Core Ops, SparseCore 0:
  36.4 11.6 reduce-scatter.27
  66.9 9.4 reduce-scatter.29
  121.1 10.9 reduce-scatter.31
  149.5 10.9 reduce-scatter.43
  180.3 9.4 reduce-scatter.45
  196.2 9.4 reduce-scatter.33
  250.0 10.9 reduce-scatter.35
  277.0 11.9 reduce-scatter.55
  302.7 12.0 reduce-scatter.39
  320.3 11.4 reduce-scatter.47
  375.0 9.4 reduce-scatter.49
  393.4 9.3 reduce-scatter.57
  409.3 9.4 reduce-scatter.41
  421.6 9.3 reduce-scatter.37
  449.3 8.5 reduce-scatter.51
  498.9 9.3 reduce-scatter.53
  542.6 8.6 reduce-scatter.59
  585.3 8.1 reduce-scatter.67
  595.7 8.9 reduce-scatter.65
  606.9 8.9 reduce-scatter.63
  618.1 9.3 reduce-scatter.61
  633.2 237.5 all-reduce.3
where the time goes:
time: 899 us; the launch traced here: 888 us
  waiting for transfers between devices  281 us (31%)
  matrix products  221 us (25%)
  local copies, waits for them, and re-layouts  176 us (20%)
  other arithmetic  94.6 us (11%)
  blocking collectives  86.4 us (10%)
  between operations  16.7 us (2%)
  starting transfers between devices  12.2 us (1%)
    psum x1, waiting for transfers between devices, shards(): lax.psum(grad_qkv.astype(jnp.bfloat16), 'dp').astype(jnp.float32)  193 us
    dot_general x6, matrix products, layer_forward(): jnp.dot(lax.slice_in_dim(active, 0, local_count * lax.axis_size('tensor')...  41.4 us
    unnamed x387, local copies, waits for them, and re-layouts  39.7 us
    psum x1, blocking collectives, shards(): lax.psum(grad_qv.astype(jnp.bfloat16), 'dp').astype(jnp.float32)  39.2 us
    dot_general x3, matrix products, layer_forward(): jnp.dot(full_hidden, w_up, preferred_element_type=jnp.float32) + up_bias  31.6 us
    ppermute x4, waiting for transfers between devices, shifted(): lax.ppermute(value, axis, [(source, source + steps) for source in range(i...  28.7 us
    reduce_scatter x6, waiting for transfers between devices, layer_forward(): lax.psum_scatter(jnp.dot(lax.slice_in_dim(active, 0, local_count * lax.ax...  25.4 us
    reduce_scatter x6, waiting for transfers between devices, layer_forward(): lax.psum_scatter(jnp.dot(lax.slice_in_dim(mixed_heads, 0, lax.axis_size('...  20.8 us
  transfers between devices with their start and end apart: 26, of which 12 were waited for; matrix products, arithmetic and copies ran while one was open for 26% of the time, Pallas kernels for 0%

commit v1 on v0

v1 whole, which is shorter than its diff:
```python
from functools import partial

import jax
import jax.numpy as jnp
from jax import lax
from jax.experimental import pallas as pl
from jax.experimental.pallas import tpu as pltpu
from jax.sharding import PartitionSpec as P

HEAD_DIM = 64
norm_eps = 1e-12
masked_score = -1e30
MESH = pl.DeviceIdType.MESH
F32 = jnp.float32
BF16 = jnp.bfloat16


def mm(a, b):
    return lax.dot_general(a, b, (((1,), (0,)), ((), ())), preferred_element_type=F32)


def mm_nt(a, b):
    return lax.dot_general(a, b, (((1,), (1,)), ((), ())), preferred_element_type=F32)


def mm_tn(a, b):
    return lax.dot_general(a, b, (((0,), (0,)), ((), ())), preferred_element_type=F32)


def ds(start, size, align=None):
    return pl.ds(pl.multiple_of(start, align or size), size)


def row_mean(v):
    return jnp.sum(v, axis=-1, keepdims=True) * (1.0 / v.shape[-1])


def main_kernel(
    D, FF, S,
    tok, cot, segk, segq, wq_in, wo_in, wu_in, wd_in, bq_in, bu_in, vec,
    lo, ig, gq, go, gu, gd, gsq, gsu, gsv,
    wq, wo, wu, wd, bq, bu,
    X, QKV, O, N1, N2, Hr, U, GP, R, dB, dA, dOs, dQKV,
    r1s, r2s, Hf, Zf, bias, dY, YB, IGB, IGF, T1, T2, T3,
    rq, ro, ru, rd, sq, su, sv, sqr, sur, svr,
    lsem, wsend, wrecv, rsend, rrecv, gsend, grecv, osem,
):
    s = lax.axis_index("section")
    d = lax.axis_index("dp")
    c = lax.axis_index("tensor")
    other = 1 - c
    core_peer = (s, d, other)
    x_peer = (1 - s, d, c)
    half_d, half_f, half_q = D // 2, FF // 2, 3 * D // 2
    pairs = D // 128
    lo_pairs = pairs // 2

    barrier = pltpu.get_barrier_semaphore()
    pl.semaphore_signal(barrier, inc=1, device_id=core_peer, device_id_type=MESH)
    pl.semaphore_signal(barrier, inc=1, device_id=x_peer, device_id_type=MESH)

    def places(k):
        return [
            (wq_in, wq.at[:, ds(k * half_q, half_q, 128)]),
            (bq_in, bq.at[:, ds(k * half_q, half_q, 128)]),
            (wo_in, wo.at[ds(k * half_d, half_d), :]),
            (bu_in, bu.at[:, ds(k * half_f, half_f, 128)]),
            (wu_in, wu.at[:, ds(k * half_f, half_f, 128)]),
            (wd_in, wd.at[ds(k * half_f, half_f), :]),
        ]

    own_places = places(c)
    local = [pltpu.make_async_copy(src, dst, lsem.at[i]) for i, (src, dst) in enumerate(own_places)]
    remote = [
        pltpu.make_async_remote_copy(src, dst, wsend.at[i], wrecv.at[i], device_id=core_peer, device_id_type=MESH)
        for i, (src, dst) in enumerate(own_places)
    ]
    tok_copy = pltpu.make_async_copy(tok, X, lsem.at[6])
    cot_copy = pltpu.make_async_copy(cot, dY, lsem.at[7])

    @pl.when(s == 0)
    def _():
        tok_copy.start()

    @pl.when(s == 1)
    def _():
        cot_copy.start()

    local[0].start()
    local[1].start()
    pl.semaphore_wait(barrier, 2)
    for i in range(6):
        remote[i].start()
        if i >= 2:
            local[i].start()

    def need(*which):
        for i in which:
            local[i].wait()
            remote[i].wait_recv()

    for q in range(2):
        bias[q] = jnp.where(segk[q] == segq[q], 0.0, masked_score)
    sq[...] = jnp.zeros_like(sq)
    su[...] = jnp.zeros_like(su)
    sv[...] = jnp.zeros_like(sv)
    lane = lax.broadcasted_iota(jnp.int32, (1, 128), 1)
    first_scaled = jnp.where(lane < HEAD_DIM, 0.125, 0.0).astype(BF16)
    second_scaled = jnp.where(lane < HEAD_DIM, 0.0, 0.125).astype(BF16)
    first_half = jnp.where(lane < HEAD_DIM, 1.0, 0.0).astype(BF16)
    second_half = jnp.where(lane < HEAD_DIM, 0.0, 1.0).astype(BF16)

    def relay(m):
        rows = ds(m * S, S)
        return pltpu.make_async_remote_copy(YB.at[rows], X.at[rows], rsend.at[m], rrecv.at[m], device_id=x_peer, device_id_type=MESH)

    def relay_back(m):
        rows = ds(m * S, S)
        return pltpu.make_async_remote_copy(IGB.at[rows], dY.at[rows], rsend.at[m], rrecv.at[m], device_id=x_peer, device_id_type=MESH)

    def pair_columns(p):
        base = (p // lo_pairs) * half_q + (p % lo_pairs) * 128
        return ds(base, 128), ds(base + half_d, 128), ds(base + 2 * half_d, 128)

    def normed(z, which):
        centered = z - row_mean(z)
        scaled = lax.rsqrt(row_mean(centered * centered) + norm_eps)
        n = centered * scaled
        return n, scaled, n * vec[2 + which : 3 + which, :] + vec[4 + which : 5 + which, :]

    def forward(t, m):
        rows = ds(m * S, S)

        @pl.when(t == 0)
        def _():
            @pl.when(s == 0)
            def _():
                tok_copy.wait()
            need(0, 1)

        @pl.when(s == 1)
        def _():
            relay(m).wait_recv()

        def qkv_tile(i, _):
            cols = ds(i * 256, 256)
            QKV[rows, cols] = (mm(X[rows, :], wq[:, cols]) + bq[0:1, cols]).astype(BF16)
            return 0

        lax.fori_loop(0, 3 * D // 256, qkv_tile, 0)

        def attend(p, _):
            qc, kc, vc = pair_columns(p)
            q2, k2, v2 = QKV[rows, qc], QKV[rows, kc], QKV[rows, vc]
            vt = v2.T
            outs = []
            for h, mask in enumerate((first_scaled, second_scaled)):
                st = mm_nt(k2 * mask, q2) + bias[m]
                e = jnp.exp(st - jnp.max(st, axis=0, keepdims=True))
                r = (e * (1.0 / jnp.sum(e, axis=0, keepdims=True))).astype(BF16)
                R[ds((m * pairs + p) * 2 * S + h * S, S), :] = r
                outs.append(mm(vt[h * HEAD_DIM : (h + 1) * HEAD_DIM], r))
            O[rows, ds(p * 128, 128)] = jnp.concatenate(outs, axis=0).T.astype(BF16)
            return 0

        lax.fori_loop(0, pairs, attend, 0)

        @pl.when(t == 0)
        def _():
            need(2)

        def out_tile(i, _):
            cols = ds(i * 256, 256)
            Zf[:, cols] = mm(O[rows, :], wo[:, cols]) + X[rows, cols].astype(F32) + vec[0:1, cols]
            return 0

        lax.fori_loop(0, D // 256, out_tile, 0)
        n, r, h = normed(Zf[...], 0)
        N1[rows, :] = n.astype(BF16)
        r1s[rows, :] = jnp.broadcast_to(r, (S, 128))
        Hf[...] = h
        Hr[rows, :] = h.astype(BF16)

        @pl.when(t == 0)
        def _():
            need(3, 4)

        def up_tile(i, _):
            cols = ds(i * 256, 256)
            g = mm(Hr[rows, :], wu[:, cols]) + bu[0:1, cols]
            cdf = 0.5 + 0.5 * lax.erf(g * 0.7071067811865476)
            U[rows, cols] = (g * cdf).astype(BF16)
            GP[rows, cols] = (cdf + g * (0.3989422804014327 * jnp.exp(g * g * -0.5))).astype(BF16)
            return 0

        lax.fori_loop(0, FF // 256, up_tile, 0)

        @pl.when(t == 0)
        def _():
            need(5)

        def down_tile(i, _):
            cols = ds(i * 256, 256)
            Zf[:, cols] = mm(U[rows, :], wd[:, cols]) + Hf[:, cols] + vec[1:2, cols]
            return 0

        lax.fori_loop(0, D // 256, down_tile, 0)
        n, r, y = normed(Zf[...], 1)
        N2[rows, :] = n.astype(BF16)
        r2s[rows, :] = jnp.broadcast_to(r, (S, 128))
        YB[rows, :] = y.astype(BF16)
        pltpu.make_async_copy(YB.at[rows], lo.at[rows], osem.at[m]).start()

        @pl.when(s == 0)
        def _():
            relay(m).start()

    def column_sum(v):
        return jnp.sum(v, axis=0, keepdims=True)

    def norm_back(dy, n, r, which):
        e = dy * vec[2 + which : 3 + which, :]
        dz = r * (e - row_mean(e) - n * row_mean(e * n))
        sv[0 + which : 1 + which, :] += column_sum(dz)
        sv[2 + which : 3 + which, :] += column_sum(dy * n)
        sv[4 + which : 5 + which, :] += column_sum(dy)
        return dz

    def backward(t, m):
        rows = ds(m * S, S)

        @pl.when(s == 0)
        def _():
            relay_back(m).wait_recv()

        @pl.when((s == 1) & (m == 0))
        def _():
            cot_copy.wait()

        dz2 = norm_back(dY[rows, :].astype(F32), N2[rows, :].astype(F32), r2s[rows, 0:1], 1)
        Zf[...] = dz2
        dB[rows, :] = dz2.astype(BF16)

        def down_back(i, _):
            cols = ds(i * 256, 256)
            dg = mm_nt(dB[rows, :], wd[cols, :]) * GP[rows, cols].astype(F32)
            su[0:1, cols] += column_sum(dg)
            GP[rows, cols] = dg.astype(BF16)
            return 0

        lax.fori_loop(0, FF // 256, down_back, 0)

        def up_back(i, _):
            cols = ds(i * 256, 256)
            Hf[:, cols] = mm_nt(GP[rows, :], wu[cols, :]) + Zf[:, cols]
            return 0

        lax.fori_loop(0, D // 256, up_back, 0)
        dz1 = norm_back(Hf[...], N1[rows, :].astype(F32), r1s[rows, 0:1], 0)
        Zf[...] = dz1
        dA[rows, :] = dz1.astype(BF16)

        def out_back(i, _):
            cols = ds(i * 256, 256)
            dOs[:, cols] = mm_nt(dA[rows, :], wo[cols, :]).astype(BF16)
            return 0

        lax.fori_loop(0, D // 256, out_back, 0)

        def attend_back(p, _):
            qc, kc, vc = pair_columns(p)
            q2, k2, v2 = QKV[rows, qc], QKV[rows, kc], QKV[rows, vc]
            do2 = dOs[:, ds(p * 128, 128)]
            kt = k2.T
            dk, dv, dqt = 0.0, 0.0, []
            for h, (scaled, half) in enumerate(((first_scaled, first_half), (second_scaled, second_half))):
                r = R[ds((m * pairs + p) * 2 * S + h * S, S), :]
                drt = mm_nt(v2 * half, do2)
                rf = r.astype(F32)
                w = rf * drt
                dst = (w - rf * jnp.sum(w, axis=0, keepdims=True)).astype(BF16)
                dk += mm(dst, q2 * scaled)
                dv += mm(r, do2 * half)
                dqt.append(mm(kt[h * HEAD_DIM : (h + 1) * HEAD_DIM], dst))
            dq = (jnp.concatenate(dqt, axis=0) * 0.125).T.astype(BF16)
            dvb = dv.astype(BF16)
            dQKV[rows, qc] = dq
            dQKV[rows, kc] = dk.astype(BF16)
            dQKV[rows, vc] = dvb
            sq[0:1, qc] += column_sum(dq.astype(F32))
            sq[0:1, vc] += column_sum(dvb.astype(F32))
            return 0

        lax.fori_loop(0, pairs, attend_back, 0)

        def in_back(i, _):
            cols = ds(i * 256, 256)
            dx = mm_nt(dQKV[rows, :], wq[cols, :]) + Zf[:, cols]
            IGF[rows, cols] = dx
            IGB[rows, cols] = dx.astype(BF16)
            return 0

        lax.fori_loop(0, D // 256, in_back, 0)
        pltpu.make_async_copy(IGF.at[rows], ig.at[rows], osem.at[2 + m]).start()

        @pl.when(s == 1)
        def _():
            relay_back(m).start()

    def step(t, _):
        back = jnp.where(s == 0, t // 2, t % 2)
        m = jnp.where(s == 0, t % 2, t // 2)

        @pl.when(back == 0)
        def _():
            forward(t, m)

        @pl.when(back == 1)
        def _():
            backward(t, m)

        return 0

    lax.fori_loop(0, 4, step, 0)
    for i in range(6):
        remote[i].wait_send()

    def grads_down(k, mine):
        def tile(i, _):
            rows = ds(k * half_f + i * 256, 256)
            g = mm(U[:, rows].T, dB[...])
            if mine:
                g = g + rd[ds(i * 256, 256), :].astype(F32)
            wd[rows, :] = g.astype(BF16)
            return 0
        lax.fori_loop(0, half_f // 256, tile, 0)

    def grads_up(k, mine):
        def tile(i, _):
            cols = ds(k * half_f + i * 256, 256)
            g = mm(T1[...], GP[:, cols])
            if mine:
                g = g + ru[:, ds(i * 256, 256)].astype(F32)
            wu[:, cols] = g.astype(BF16)
            return 0
        lax.fori_loop(0, half_f // 256, tile, 0)

    def grads_out(k, mine):
        rows = ds(k * half_d, half_d)
        g = mm(T2[rows, :], dA[...])
        if mine:
            g = g + ro[...].astype(F32)
        wo[rows, :] = g.astype(BF16)

    def grads_qkv(k, mine):
        def tile(i, _):
            cols = ds(k * half_q + i * 384, 384, 128)
            g = mm(T3[...], dQKV[:, cols])
            if mine:
                g = g + rq[:, ds(i * 384, 384)].astype(F32)
            wq[:, cols] = g.astype(BF16)
            return 0
        lax.fori_loop(0, half_q // 384, tile, 0)

    slices = [
        (wd.at[ds(other * half_f, half_f), :], rd),
        (wu.at[:, ds(other * half_f, half_f, 128)], ru),
        (wo.at[ds(other * half_d, half_d), :], ro),
        (wq.at[:, ds(other * half_q, half_q, 128)], rq),
        (sq, sqr), (su, sur), (sv, svr),
    ]
    exchange = [
        pltpu.make_async_remote_copy(src, dst, gsend.at[i], grecv.at[i], device_id=core_peer, device_id_type=MESH)
        for i, (src, dst) in enumerate(slices)
    ]
    for i in (4, 5, 6):
        exchange[i].start()
    T1[...] = Hr[...].T
    T2[...] = O[...].T
    T3[...] = X[...].T
    for i, work in enumerate((grads_down, grads_up, grads_out, grads_qkv)):
        work(other, False)
        exchange[i].start()
    results = [
        (wd.at[ds(c * half_f, half_f), :], gd),
        (wu.at[:, ds(c * half_f, half_f, 128)], gu),
        (wo.at[ds(c * half_d, half_d), :], go),
        (wq.at[:, ds(c * half_q, half_q, 128)], gq),
        (sq, gsq), (su, gsu), (sv, gsv),
    ]
    results = [pltpu.make_async_copy(src, dst, osem.at[4 + i]) for i, (src, dst) in enumerate(results)]
    for i, work in enumerate((grads_down, grads_up, grads_out, grads_qkv)):
        exchange[i].wait_recv()
        work(c, True)
        results[i].start()
    for i, (mine, theirs) in ((4, (sq, sqr)), (5, (su, sur)), (6, (sv, svr))):
        exchange[i].wait()
        mine[...] += theirs[...]
        results[i].start()
    for i in range(4):
        exchange[i].wait_send()
    for i in range(7):
        results[i].wait()
    for m in range(2):
        rows = ds(m * S, S)
        pltpu.make_async_copy(YB.at[rows], lo.at[rows], osem.at[m]).wait()
        pltpu.make_async_copy(IGF.at[rows], ig.at[rows], osem.at[2 + m]).wait()

    @pl.when(s == 0)
    def _():
        for m in range(2):
            relay(m).wait_send()

    @pl.when(s == 1)
    def _():
        for m in range(2):
            relay_back(m).wait_send()


def main_call(tok, cot, segk, segq, wq, wo, wu, wd, bq, bu, vec, S):
    rows, D = tok.shape
    FF = 2 * wu.shape[1]
    hd, hf, hq = D // 2, FF // 2, 3 * D // 2
    any_spec = pl.BlockSpec(memory_space=pl.ANY)
    vm_spec = pl.BlockSpec(memory_space=pltpu.VMEM)
    sds = jax.ShapeDtypeStruct
    V = pltpu.VMEM
    out_shape = (
        sds((rows, D), BF16), sds((rows, D), F32),
        sds((D, hq), BF16), sds((hd, D), BF16), sds((D, hf), BF16), sds((hf, D), BF16),
        sds((8, 2 * hq), F32), sds((8, FF), F32), sds((8, D), F32),
    )
    scratch = [
        V((D, 2 * hq), BF16), V((D, D), BF16), V((D, FF), BF16), V((FF, D), BF16), V((8, 2 * hq), F32), V((8, FF), F32),
        V((rows, D), BF16), V((rows, 3 * D), BF16), V((rows, D), BF16), V((rows, D), BF16), V((rows, D), BF16), V((rows, D), BF16),
        V((rows, FF), BF16), V((rows, FF), BF16), V((2 * (D // HEAD_DIM) * S, S), BF16),
        V((rows, D), BF16), V((rows, D), BF16), V((S, D), BF16), V((rows, 3 * D), BF16),
        V((rows, 128), F32), V((rows, 128), F32), V((S, D), F32), V((S, D), F32), V((2, S, S), F32),
        V((rows, D), BF16), V((rows, D), BF16), V((rows, D), BF16), V((rows, D), F32),
        V((D, rows), BF16), V((D, rows), BF16), V((D, rows), BF16),
        V((D, hq), BF16), V((hd, D), BF16), V((D, hf), BF16), V((hf, D), BF16),
        V((8, 2 * hq), F32), V((8, FF), F32), V((8, D), F32), V((8, 2 * hq), F32), V((8, FF), F32), V((8, D), F32),
        pltpu.SemaphoreType.DMA((8,)), pltpu.SemaphoreType.DMA((6,)), pltpu.SemaphoreType.DMA((6,)),
        pltpu.SemaphoreType.DMA((2,)), pltpu.SemaphoreType.DMA((2,)),
        pltpu.SemaphoreType.DMA((7,)), pltpu.SemaphoreType.DMA((7,)), pltpu.SemaphoreType.DMA((11,)),
    ]
    return pl.pallas_call(
        partial(main_kernel, D, FF, S),
        out_shape=out_shape,
        in_specs=[any_spec, any_spec, vm_spec, vm_spec] + [any_spec] * 6 + [vm_spec],
        out_specs=(any_spec,) * 9,
        scratch_shapes=scratch,
        compiler_params=pltpu.CompilerParams(collective_id=0, has_side_effects=True, vmem_limit_bytes=60 * 2**20),
        name="layer_pass",
    )(tok, cot, segk, segq, wq, wo, wu, wd, bq, bu, vec)


def shards(tokens, segment_ids, out_cotangent, w_qkv, qv_bias, w_out, w_up, up_bias, w_down, add_bias, norm_gain, norm_bias):
    c = lax.axis_index("tensor")
    D = tokens.shape[1]
    hd = D // 2
    S = segment_ids.shape[1]
    seqs = tokens.shape[0] // S
    seg = lax.dynamic_slice_in_dim(segment_ids, c * seqs, seqs, axis=0)
    vec = jnp.concatenate([add_bias[0], norm_gain[0], norm_bias[0], jnp.zeros((2, D), F32)], axis=0)
    qv = qv_bias[0].astype(F32)
    bq = jnp.concatenate([qv[0], jnp.zeros((hd,), F32), qv[1]])
    bq = jnp.broadcast_to(bq[None], (8, 3 * hd))
    bu = jnp.broadcast_to(up_bias.astype(F32), (8, up_bias.shape[1]))
    lo, ig, gq, go, gu, gd, gsq, gsu, gsv = main_call(
        tokens, out_cotangent, seg[:, :, None], seg[:, None, :],
        w_qkv[0].reshape(D, 3 * hd), w_out[0], w_up[0], w_down[0], bq, bu, vec, S,
    )
    def own(v, size):
        return lax.dynamic_slice_in_dim(v, c * size, size, axis=-1)
    sq = own(gsq[0], 3 * hd)
    small = [jnp.concatenate([sq[:hd], sq[2 * hd :]]), own(gsu[0], up_bias.shape[1]), own(gsv[:6], hd).reshape(-1)]
    tot = lax.psum(tuple(v.astype(BF16) for v in (gq, go, gu, gd, *small)), "dp")
    gq, go, gu, gd, gqv, gub, gsv = (v.astype(F32) for v in tot)
    gsv = gsv.reshape(6, hd)
    return (
        lo[None], ig[None],
        gq.reshape(1, D, 3, hd), gqv.reshape(1, 2, hd), go[None], gu[None], gub[None], gd[None],
        gsv[None, 0:2], gsv[None, 2:4], gsv[None, 4:6],
    )


def solution(mesh):
    return jax.shard_map(
        shards,
        mesh=mesh,
        in_specs=(
            P(("dp", "tensor"), None), P("dp", None), P(("dp", "tensor"), None),
            P("section", None, None, "tensor"), P("section", None, "tensor"), P("section", "tensor", None),
            P("section", None, "tensor"), P("section", "tensor"), P("section", "tensor", None),
            P("section", None, None), P("section", None, None), P("section", None, None),
        ),
        out_specs=(
            P("section", ("dp", "tensor"), None), P("section", ("dp", "tensor"), None),
            P("section", None, None, "tensor"), P("section", None, "tensor"), P("section", "tensor", None),
            P("section", None, "tensor"), P("section", "tensor"), P("section", "tensor", None),
            P("section", None, "tensor"), P("section", None, "tensor"), P("section", None, "tensor"),
        ),
        check_vma=False,
    )
```

time: 899 us -> 413 us (0.46); the launches traced: 888 us -> 412 us
  matrix products: 221 us -> 0 us
  local copies, waits for them, and re-layouts: 176 us -> 20.4 us
  Pallas kernels: 0 us -> 135 us
  waiting for transfers between devices: 281 us -> 193 us
  other arithmetic: 94.6 us -> 10.9 us
  blocking collectives: 86.4 us -> 39.4 us
  starting transfers between devices: 12.2 us -> 0.04 us
    dot_general x69 -> x0, matrix products: 221 us -> none  [the longest x6 41.4 us: layer_forward(): jnp.dot(lax.slice_in_dim(active, 0, local_count * lax.axis_size('tensor')...]
    pallas_call x0 -> x1, Pallas kernels: none -> 135 us  [main_call(): pl.pallas_call(partial(main_kernel, D, FF, S), out_shape=out_shape, in_sp...]
    reduce_scatter x18 -> x0, waiting for transfers between devices: 58.4 us -> none  [the longest x6 25.4 us: layer_forward(): lax.psum_scatter(jnp.dot(lax.slice_in_dim(active, 0, local_count * lax.ax...]
    reduce_sum x33 -> x0, other arithmetic: 47.7 us -> none  [the longest x8 18 us: layer_norm(): centered = residual - jnp.mean(residual, axis=-1, keepdims=True)]
    all_gather x18 -> x0, blocking collectives: 47.2 us -> none  [the longest x6 17.2 us: layer_forward(): full_hidden = lax.all_gather(hidden_low, 'tensor', axis=0, tiled=True)]
    slice x34 -> x9, local copies, waits for them, and re-layouts: 42.4 us -> 3.6 us  [the longest x1 0.9 us: shards(): gsu[0]]
    convert_element_type x26 -> x3, local copies, waits for them, and re-layouts: 32.8 us -> 0.03 us  [shards(): v.astype(BF16)]
    unnamed x387 -> x26, local copies, waits for them, and re-layouts: 39.7 us -> 7.93 us
  transfers between devices with their start and end apart: 26 -> 1, of which waited for: 12 -> 1; matrix products, arithmetic and copies ran while one was open for 26% -> 1% of each run, Pallas kernels for 0% -> 0%
where the time goes in v1:
time: 413 us; the launch traced here: 412 us
  waiting for transfers between devices  193 us (47%)
  Pallas kernels  135 us (33%)
  blocking collectives  39.4 us (10%)
  local copies, waits for them, and re-layouts  20.4 us (5%)
  between operations  14.2 us (3%)
  other arithmetic  10.9 us (3%)
    psum x1, waiting for transfers between devices, shards(): lax.psum(tuple((v.astype(BF16) for v in (gq, go, gu, gd, *small))), 'dp')  193 us
    pallas_call x1, Pallas kernels, main_call(): pl.pallas_call(partial(main_kernel, D, FF, S), out_shape=out_shape, in_sp...  135 us
    psum x1, blocking collectives, shards(): lax.psum(tuple((v.astype(BF16) for v in (gq, go, gu, gd, *small))), 'dp')  39.4 us
  transfers between devices with their start and end apart: 1, of which 1 were waited for; matrix products, arithmetic and copies ran while one was open for 1% of the time, Pallas kernels for 0%

profile of v1, /device:TPU:0, one launch (start us, length us, event | category | flops | bytes accessed | tf_op | source)
XLA Modules:
  0.0 412.4 jit_solution(3023183375071847333)
XLA Ops:
  7.2 0.0 copy-start
  7.2 0.0 all-reduce.4.cloned.1.call-start
  7.2 0.6 copy-done
  7.9 0.9 copy.26.segk
  8.7 0.6 broadcast_in_dim.62.segq
  9.3 0.7 convert_element_type.27
  10.0 2.6 copy.25
  12.7 0.0 copy-start.6
  12.7 0.0 copy-start.8
  12.7 0.0 copy-start.9
  12.7 0.0 copy-start.10
  12.7 2.2 copy.27.wq_in
  14.9 0.0 copy-done.6
  15.0 0.1 pad.5.clone
  15.0 0.0 copy-done.8
  15.1 0.0 copy-done.9
  15.1 0.0 copy-done.10
  15.1 0.7 maximum_maximum_fusion.vec
  15.8 0.6 broadcast_in_dim.64.bq_in
  16.4 0.6 broadcast_in_dim.67.bu_in
  17.0 134.8 %layer_pass.1 = (bf16[512,768]{1,0:T(8,128)(2,1)}, f32[512,768]{1,0:T(8,128)}, bf16[768,1152]{1,0:T(8,128)(2,1)}, bf16[384,768]{1,0:T(8,128)(2,1)}, bf16[768,153...) custom-call(bf16[512,768]{1,0:T(8,128)(2,1)} %tok.1, ...), custom_call_target="tpu_custom_call" | custom-call | tf_op jit(solution)/shard_map/layer_pass/pallas_call | solution.py:447
  151.8 3.9 copy.28
  155.7 0.0 copy-start.7
  155.7 0.0 all-reduce.4.cloned.1.call-update
  155.7 0.9 slice.75
  156.7 0.0 copy-done.7
  156.7 0.9 slice.80
  157.7 39.4 %all-reduce = (bf16[2304]{0:T(1024)(128)(2,1)S(1)}, bf16[1,2,384]{2,1,0:T(2,128)(2,1)S(1)}, bf16[1,1536]{1,0:T(2,128)(2,1)S(1)}) all-reduce(bf16[2304]{0:T(1024)(128)(2,1)S(1)} %convert_element_type.31, bf16[1,2,384]{2,1,0:T(2,128)(2,1)S(1)} %reshape.82, ...), channel_id=1, replica_groups=mesh['section'=2,'dp'=8,'tensor'=2] {'dp'}, use_global_device_ids=true, to_apply=%region_6.0 | all-reduce | flops 4608 | bytes 18432 | tf_op jit(solution)/shard_map/psum | solution.py:478
  197.1 0.6 slice.83
  197.7 0.6 slice.85
  198.3 0.6 slice.87
  198.9 0.6 broadcast_in_dim.76
  199.5 0.6 reshape.83
  200.0 192.6 %all-reduce.4.cloned.1.call-done = (bf16[1,768,3,384]{1,3,2,0:T(8,128)(2,1)}, bf16[1,384,768]{2,1,0:T(8,128)(2,1)}, bf16[1,768,1536]{2,1,0:T(8,128)(2,1)}, bf16[1,1536,768]{2,1,0:T(8,128)(2,1)}) async-done(((bf16[1,768,3,384]{1,3,2,0:T(8,128)(2,1)}, bf16[1,384,768]{2,1,0:T(8,128)(2,1)}, bf16[1,768,1536]{2,1,0:T(8,128)(2,1)}, bf16[1,1536,768]{2,1,0:T(8,128)(2,1)}), (bf16[1,768,3,384]{1,3,2,0:T(8,128)(2,1)}, ...) | async-done | bytes 7077904 | tf_op jit(solution)/shard_map/psum | solution.py:478
  392.6 0.0 copy-start.1
  392.7 4.6 %broadcast_in_dim.74 = f32[1,768,1536]{2,1,0:T(8,128)} convert(bf16[1,768,1536]{2,1,0:T(8,128)(2,1)} %get-tuple-element.49) | non-fusion elementwise | flops 1179648 | bytes 7077888 | tf_op jit(solution)/shard_map/broadcast_in_dim | solution.py:483
  397.3 0.0 copy-done.1
  397.3 0.0 copy-start.2
  397.3 2.5 broadcast_in_dim.78
  399.8 0.0 copy-done.2
  399.8 0.0 copy-start.5
  399.9 0.0 copy-start.4
  399.9 2.6 copy.29
  402.5 0.0 copy-start.3
  402.5 0.0 copy-done.5
  402.5 1.1 broadcast_in_dim.72
  403.6 0.0 copy-done.4
  403.6 0.9 copy.36
  404.4 0.0 copy-done.3
  404.4 1.1 copy.37
  (16 shorter events, 0.2 us)
Async XLA Ops:
  7.2 0.7 copy-start
  7.2 385.5 %all-reduce.4.cloned.1.call-start = ((), (), s32[]{:S(2)}) async-start(), calls=%async_computation | async-start | bytes 14155776 | tf_op jit(solution)/shard_map/psum | solution.py:478
  12.7 2.3 copy-start.6
  12.7 2.4 copy-start.8
  12.7 2.4 copy-start.9
  12.7 2.4 copy-start.10
  155.7 1.0 copy-start.7
  392.6 4.7 %copy-start.1 = (bf16[1,1536,768]{2,1,0:T(8,128)(2,1)S(1)}, bf16[1,1536,768]{2,1,0:T(8,128)(2,1)}, u32[]{:S(2)}) copy-start(bf16[1,1536,768]{2,1,0:T(8,128)(2,1)} %get-tuple-element.50) | copy-start | bytes 7077892
  397.3 2.5 copy-start.2
  399.8 2.6 copy-start.5
  399.9 3.7 copy-start.4
  402.5 2.0 copy-start.3
Sparse Core Ops, SparseCore 0:
  155.8 236.7 all-reduce.3

commit v2 on v1

--- a/solution.py
+++ b/solution.py
@@ -10,6 +10,9 @@
 HEAD_DIM = 64
 norm_eps = 1e-12
 masked_score = -1e30
+LINE = 4
+BUCKETS = 12
+A_ROWS = 512
 MESH = pl.DeviceIdType.MESH
 F32 = jnp.float32
 BF16 = jnp.bfloat16
@@ -35,15 +38,285 @@
     return jnp.sum(v, axis=-1, keepdims=True) * (1.0 / v.shape[-1])
 
 
+class Line:
+    def __init__(self, red, base, size, landing, sems):
+        self.red, self.base, self.size, self.landing, self.sems = red, base, size, landing, sems
+
+    def own(self, b, j):
+        return ds(self.base(b) + j * self.size, self.size, 16)
+
+    def slot(self, b, j):
+        return ds((b * (LINE + 1) + j) * self.size, self.size, 16)
+
+    def sum_up(self, b, j):
+        r = self.red
+        return r.remote(r.G.at[self.own(b, j)], self.landing.at[self.slot(b, j)], b, self.sems + j, r.above)
+
+    def sum_down(self, b, j):
+        r = self.red
+        place = jnp.where(j == r.z - 1, LINE, j)
+        return r.remote(r.G.at[self.own(b, j)], self.landing.at[self.slot(b, place)], b, self.sems + LINE + j, r.below)
+
+    def from_above(self, b, j):
+        r = self.red
+        place = jnp.where(j == r.z, LINE, j)
+        return r.remote(r.G.at[self.own(b, j)], self.landing.at[self.slot(b, place)], b, self.sems + LINE + j, r.below)
+
+    def out_up(self, b, j, own=False):
+        r = self.red
+        return r.remote(r.place(own).at[self.own(b, j)], r.out.at[self.own(b, j)], b, self.sems + 2 * LINE + j, r.above)
+
+    def out_down(self, b, j, own=False):
+        r = self.red
+        return r.remote(r.place(own).at[self.own(b, j)], r.out.at[self.own(b, j)], b, self.sems + 3 * LINE + j, r.below)
+
+    def add(self, b, j, *places):
+        G = self.red.G
+        rows = self.own(b, j)
+        total = G[rows, :].astype(F32)
+        for place in places:
+            total = total + self.landing[self.slot(b, place), :].astype(F32)
+        G[rows, :] = total.astype(BF16)
+
+    def begin(self, b):
+        z = self.red.z
+
+        @pl.when(z == 0)
+        def _():
+            for i in range(LINE - 1):
+                self.sum_up(b, LINE - 1 - i).start()
+
+        @pl.when(z == LINE - 1)
+        def _():
+            for i in range(LINE - 1):
+                self.sum_down(b, i).start()
+
+    def pass_on(self, b, i):
+        z = self.red.z
+        end = LINE - 1 - z
+        up, down = LINE - 2 - i + z, 1 + i - end
+
+        @pl.when((up > z) & (up < LINE) & (z > 0))
+        def _():
+            self.sum_up(b, up).wait_recv()
+            self.add(b, up, up)
+            self.sum_up(b, up).start()
+
+        @pl.when((down < z) & (down >= 0) & (end > 0))
+        def _():
+            self.from_above(b, down).wait_recv()
+            self.add(b, down, down)
+            self.sum_down(b, down).start()
+
+    def finish_own(self, b):
+        z = self.red.z
+
+        @pl.when(z > 0)
+        def _():
+            self.sum_up(b, z).wait_recv()
+
+        @pl.when(z < LINE - 1)
+        def _():
+            self.from_above(b, z).wait_recv()
+
+        @pl.when(z == 0)
+        def _():
+            self.add(b, 0, LINE)
+
+        @pl.when(z == LINE - 1)
+        def _():
+            self.add(b, LINE - 1, LINE - 1)
+
+        @pl.when((z > 0) & (z < LINE - 1))
+        def _():
+            self.add(b, z, z, LINE)
+
+    def spread(self, b):
+        z = self.red.z
+
+        @pl.when(z < LINE - 1)
+        def _():
+            self.out_up(b, z, True).start()
+
+        @pl.when(z > 0)
+        def _():
+            self.out_down(b, z, True).start()
+
+        self.keep(b).start()
+
+    def keep(self, b):
+        r = self.red
+        rows = self.own(b, r.z)
+        return pltpu.make_async_copy(r.G.at[rows], r.out.at[rows], r.csem.at[b, self.sems // (4 * LINE)])
+
+    def spread_on(self, b, i):
+        z = self.red.z
+
+        @pl.when(z - i >= 0)
+        def _():
+            self.out_up(b, z - i).wait_recv()
+
+            @pl.when(z < LINE - 1)
+            def _():
+                self.out_up(b, z - i).start()
+
+        @pl.when(z + i < LINE)
+        def _():
+            self.out_down(b, z + i).wait_recv()
+
+            @pl.when(z > 0)
+            def _():
+                self.out_down(b, z + i).start()
+
+    def drain(self, b):
+        z = self.red.z
+        for j in range(LINE):
+            @pl.when(j > z)
+            def _():
+                self.sum_up(b, j).wait_send()
+
+            @pl.when(j < z)
+            def _():
+                self.sum_down(b, j).wait_send()
+
+            @pl.when((j <= z) & (z < LINE - 1))
+            def _():
+                self.out_up(b, j).wait_send()
+
+            @pl.when((j >= z) & (z > 0))
+            def _():
+                self.out_down(b, j).wait_send()
+
+
+class Reduction:
+    stages = 9
+
+    def __init__(self, D, s, d, c, G, out, LA1, LA, LB, LS, SM, SML, asend, arecv, ssend, srecv, csem):
+        self.out, self.csem = out, csem
+        self.G, self.LA1, self.LS, self.SM, self.SML = G, LA1, LS, SM, SML
+        self.asend, self.arecv, self.ssend, self.srecv = asend, arecv, ssend, srecv
+        self.z, self.y = d // 2, d % 2
+        self.s, self.d, self.c = s, d, c
+        self.above = (s, jnp.minimum(d + 2, 2 * LINE - 1), c)
+        self.below = (s, jnp.maximum(d - 2, 0), c)
+        self.beside = (s, d + 1 - 2 * self.y, c)
+        self.half = A_ROWS // 2
+        self.D = D
+        self.a = Line(self, lambda b: b * D + self.y * self.half, self.half // LINE, LA, 0)
+        self.b = Line(self, lambda b: b * D + A_ROWS, (D - A_ROWS) // LINE, LB, 4 * LINE)
+        z = self.z
+        pair = z + 1 - 2 * (z % 2)
+        far = (z + 2) % 4
+        self.small_peers = [None, self.beside, (s, pair * 2 + self.y, c), (s, far * 2 + self.y, c)]
+
+    def place(self, own):
+        return self.G if own else self.out
+
+    def remote(self, src, dst, b, sem, to):
+        return pltpu.make_async_remote_copy(src, dst, self.asend.at[b, sem], self.arecv.at[b, sem], device_id=to, device_id_type=MESH)
+
+    def greet(self, barrier):
+        def hello(to):
+            pl.semaphore_signal(barrier, inc=1, device_id=to, device_id_type=MESH)
+        for to in self.small_peers[1:]:
+            hello(to)
+        @pl.when((self.z == 1))
+        def _():
+            hello(self.above)
+
+        @pl.when((self.z == 2))
+        def _():
+            hello(self.below)
+
+    def greetings(self):
+        return 3 + ((self.z == 1) | (self.z == 2)).astype(jnp.int32)
+
+    def small_copy(self, k):
+        return pltpu.make_async_remote_copy(self.SM, self.SML.at[k], self.ssend.at[k], self.srecv.at[k], device_id=self.small_peers[k], device_id_type=MESH)
+
+    def small_start(self, k):
+        self.small_copy(k).start()
+
+    def small_finish(self, k):
+        self.small_copy(k).wait()
+        self.SM[...] += self.SML[k]
+
+    def give_side(self, b):
+        rows = ds(b * self.D + (1 - self.y) * self.half, self.half, 16)
+        return self.remote(self.G.at[rows], self.LA1.at[ds(b * self.half, self.half, 16)], b, 8 * LINE, self.beside)
+
+    def share_side(self, b):
+        rows = ds(b * self.D + self.y * self.half, self.half, 16)
+        return self.remote(self.out.at[rows], self.out.at[rows], b, 8 * LINE + 1, self.beside)
+
+    def swap(self, b):
+        size = self.b.size
+        return self.remote(self.G.at[self.b.own(b, self.z)], self.LS.at[ds(b * size, size, 16)], b, 8 * LINE + 2, self.beside)
+
+    def stage(self, k, b):
+        A, B = self.a, self.b
+        if k == 0:
+            self.give_side(b).start()
+            B.begin(b)
+        elif k == 1:
+            B.pass_on(b, 0)
+            self.give_side(b).wait_recv()
+            rows = ds(b * self.D + self.y * self.half, self.half, 16)
+            land = ds(b * self.half, self.half, 16)
+            self.G[rows, :] = (self.G[rows, :].astype(F32) + self.LA1[land, :].astype(F32)).astype(BF16)
+            A.begin(b)
+        elif k == 2:
+            B.pass_on(b, 1)
+            A.pass_on(b, 0)
+        elif k == 3:
+            B.finish_own(b)
+            self.swap(b).start()
+            A.pass_on(b, 1)
+        elif k == 4:
+            A.finish_own(b)
+            A.spread(b)
+            size = B.size
+            self.swap(b).wait()
+            rows, land = B.own(b, self.z), ds(b * size, size, 16)
+            self.G[rows, :] = (self.G[rows, :].astype(F32) + self.LS[land, :].astype(F32)).astype(BF16)
+            B.spread(b)
+        elif k <= 7:
+            A.spread_on(b, k - 4)
+            B.spread_on(b, k - 4)
+            if k == 7:
+                A.keep(b).wait()
+                self.share_side(b).start()
+        else:
+            self.share_side(b).wait_recv()
+
+    def slot(self, tau):
+        for k in range(self.stages - 1, -1, -1):
+            b = tau - k
+
+            @pl.when((b >= 0) & (b < BUCKETS))
+            def _():
+                self.stage(k, b)
+
+    def drain(self):
+        def one(b, _):
+            self.a.drain(b)
+            self.b.drain(b)
+            self.give_side(b).wait_send()
+            self.share_side(b).wait_send()
+            self.b.keep(b).wait()
+            return 0
+        lax.fori_loop(0, BUCKETS, one, 0)
+
+
 def main_kernel(
-    D, FF, S,
+    D, FF, S, grid,
     tok, cot, segk, segq, wq_in, wo_in, wu_in, wd_in, bq_in, bu_in, vec,
-    lo, ig, gq, go, gu, gd, gsq, gsu, gsv,
+    lo, ig, gall, gsm,
     wq, wo, wu, wd, bq, bu,
     X, QKV, O, N1, N2, Hr, U, GP, R, dB, dA, dOs, dQKV,
-    r1s, r2s, Hf, Zf, bias, dY, YB, IGB, IGF, T1, T2, T3,
-    rq, ro, ru, rd, sq, su, sv, sqr, sur, svr,
-    lsem, wsend, wrecv, rsend, rrecv, gsend, grecv, osem,
+    r1s, r2s, Hf, Zf, bias, dY, YB, IGB, IGF,
+    sq, su, sv, SM, SML, G, LA1, LA, LB, LS,
+    lsem, wsend, wrecv, rsend, rrecv, gsend, grecv, osem, ssend, srecv, asend, arecv, csem,
 ):
     s = lax.axis_index("section")
     d = lax.axis_index("dp")
@@ -58,6 +331,9 @@
     barrier = pltpu.get_barrier_semaphore()
     pl.semaphore_signal(barrier, inc=1, device_id=core_peer, device_id_type=MESH)
     pl.semaphore_signal(barrier, inc=1, device_id=x_peer, device_id_type=MESH)
+    if grid:
+        ring = Reduction(D, s, d, c, G, gall, LA1, LA, LB, LS, SM, SML, asend, arecv, ssend, srecv, csem)
+        ring.greet(barrier)
 
     def places(k):
         return [
@@ -88,7 +364,7 @@
 
     local[0].start()
     local[1].start()
-    pl.semaphore_wait(barrier, 2)
+    pl.semaphore_wait(barrier, 2 + ring.greetings() if grid else 2)
     for i in range(6):
         remote[i].start()
         if i >= 2:
@@ -325,82 +601,141 @@
     for i in range(6):
         remote[i].wait_send()
 
-    def grads_down(k, mine):
-        def tile(i, _):
-            rows = ds(k * half_f + i * 256, 256)
-            g = mm(U[:, rows].T, dB[...])
-            if mine:
-                g = g + rd[ds(i * 256, 256), :].astype(F32)
-            wd[rows, :] = g.astype(BF16)
-            return 0
-        lax.fori_loop(0, half_f // 256, tile, 0)
-
-    def grads_up(k, mine):
-        def tile(i, _):
-            cols = ds(k * half_f + i * 256, 256)
-            g = mm(T1[...], GP[:, cols])
-            if mine:
-                g = g + ru[:, ds(i * 256, 256)].astype(F32)
-            wu[:, cols] = g.astype(BF16)
-            return 0
-        lax.fori_loop(0, half_f // 256, tile, 0)
-
-    def grads_out(k, mine):
-        rows = ds(k * half_d, half_d)
-        g = mm(T2[rows, :], dA[...])
-        if mine:
-            g = g + ro[...].astype(F32)
-        wo[rows, :] = g.astype(BF16)
-
-    def grads_qkv(k, mine):
-        def tile(i, _):
-            cols = ds(k * half_q + i * 384, 384, 128)
-            g = mm(T3[...], dQKV[:, cols])
-            if mine:
-                g = g + rq[:, ds(i * 384, 384)].astype(F32)
-            wq[:, cols] = g.astype(BF16)
-            return 0
-        lax.fori_loop(0, half_q // 384, tile, 0)
-
-    slices = [
-        (wd.at[ds(other * half_f, half_f), :], rd),
-        (wu.at[:, ds(other * half_f, half_f, 128)], ru),
-        (wo.at[ds(other * half_d, half_d), :], ro),
-        (wq.at[:, ds(other * half_q, half_q, 128)], rq),
-        (sq, sqr), (su, sur), (sv, svr),
-    ]
-    exchange = [
-        pltpu.make_async_remote_copy(src, dst, gsend.at[i], grecv.at[i], device_id=core_peer, device_id_type=MESH)
-        for i, (src, dst) in enumerate(slices)
-    ]
-    for i in (4, 5, 6):
-        exchange[i].start()
-    T1[...] = Hr[...].T
-    T2[...] = O[...].T
-    T3[...] = X[...].T
-    for i, work in enumerate((grads_down, grads_up, grads_out, grads_qkv)):
-        work(other, False)
-        exchange[i].start()
-    results = [
-        (wd.at[ds(c * half_f, half_f), :], gd),
-        (wu.at[:, ds(c * half_f, half_f, 128)], gu),
-        (wo.at[ds(c * half_d, half_d), :], go),
-        (wq.at[:, ds(c * half_q, half_q, 128)], gq),
-        (sq, gsq), (su, gsu), (sv, gsv),
-    ]
-    results = [pltpu.make_async_copy(src, dst, osem.at[4 + i]) for i, (src, dst) in enumerate(results)]
-    for i, work in enumerate((grads_down, grads_up, grads_out, grads_qkv)):
-        exchange[i].wait_recv()
-        work(c, True)
-        results[i].start()
-    for i, (mine, theirs) in ((4, (sq, sqr)), (5, (su, sur)), (6, (sv, svr))):
-        exchange[i].wait()
-        mine[...] += theirs[...]
-        results[i].start()
+    W = D // 2
+
+    def grad_tiles(k, kind, i):
+        if kind == "down" or kind == "out":
+            rows = ds(k * half_f + i * W, W, 128) if kind == "down" else ds(k * half_d, W)
+            if kind == "out":
+                return [across(1, k * half_d, W, dA[:, q * W : (q + 1) * W]) for q in range(2)]
+            left = U[:, rows].T
+            return [mm(left, dB[:, q * W : (q + 1) * W]) for q in range(2)]
+        cols = ds(k * (half_f if kind == "up" else half_q) + i * W, W, 128)
+        i, right = (0, GP) if kind == "up" else (2, dQKV)
+        return [across(i, q * W, W, right[:, cols]) for q in range(2)]
+
+    first = {"down": 0, "up": 4, "qkv": 8, "out": 11}
+
+    def halves(k, kind, i):
+        if kind == "down":
+            return [wd.at[ds(k * half_f + i * W, W), q * W : (q + 1) * W] for q in range(2)]
+        if kind == "out":
+            return [wo.at[ds(k * half_d, W), q * W : (q + 1) * W] for q in range(2)]
+        cols = ds(k * (half_f if kind == "up" else half_q) + i * W, W, 128)
+        ref = wu if kind == "up" else wq
+        return [ref.at[q * W : (q + 1) * W, cols] for q in range(2)]
+
+    def exchange(kind, i):
+        b = first[kind] + i
+        return [
+            pltpu.make_async_remote_copy(part, G.at[ds(b * D + q * W, W)], gsend.at[b, q], grecv.at[b, q], device_id=core_peer, device_id_type=MESH)
+            for q, part in enumerate(halves(other, kind, i))
+        ]
+
+    def give(kind, i):
+        tiles = grad_tiles(other, kind, i)
+        for q, copy in enumerate(exchange(kind, i)):
+            halves(other, kind, i)[q][...] = tiles[q].astype(BF16)
+            copy.start()
+
+    def keep(kind, i):
+        tiles = grad_tiles(c, kind, i)
+        b = first[kind] + i
+        for q, copy in enumerate(exchange(kind, i)):
+            copy.wait_recv()
+            rows = ds(b * D + q * W, W)
+            G[rows, :] = (tiles[q] + G[rows, :].astype(F32)).astype(BF16)
+
+    def slot(tau):
+        if grid:
+            ring.slot(tau)
+
+    for i in range(3):
+        SM[i : i + 1, :] = sq[0:1, i * D : (i + 1) * D]
     for i in range(4):
-        exchange[i].wait_send()
-    for i in range(7):
-        results[i].wait()
+        SM[3 + i : 4 + i, :] = su[0:1, i * D : (i + 1) * D]
+    SM[7:8, :] = jnp.zeros((1, D), F32)
+    SM[8:16, :] = sv[...]
+    small_core = pltpu.make_async_remote_copy(SM, SML.at[0], ssend.at[0], srecv.at[0], device_id=core_peer, device_id_type=MESH)
+    small_core.start()
+    for i, whole in enumerate((Hr, O, X)):
+        for m in range(2):
+            R[(2 * i + m) * D : (2 * i + m + 1) * D, :] = whole[m * S : (m + 1) * S, :].T
+
+    def across(i, start, size, right):
+        return sum(mm(R[ds((2 * i + m) * D + start, size, 128), :], right[m * S : (m + 1) * S]) for m in range(2))
+
+
+    def first_loop(i, _):
+        give("down", i)
+        return 0
+
+    def second_loop(i, _):
+        keep("down", i)
+        slot(i)
+        give("up", i)
+        return 0
+
+    def third_loop(i, _):
+        keep("up", i)
+        slot(4 + i)
+
+        @pl.when(i < 3)
+        def _():
+            give("qkv", i)
+
+        @pl.when(i == 3)
+        def _():
+            give("out", 0)
+
+        return 0
+
+    def fourth_loop(i, _):
+        @pl.when(i < 3)
+        def _():
+            keep("qkv", i)
+
+        @pl.when(i == 3)
+        def _():
+            keep("out", 0)
+
+        slot(8 + i)
+        return 0
+
+    lax.fori_loop(0, 4, first_loop, 0)
+    small_core.wait()
+    SM[...] += SML[0]
+    if grid:
+        ring.small_start(1)
+    lax.fori_loop(0, 4, second_loop, 0)
+    if grid:
+        ring.small_finish(1)
+        ring.small_start(2)
+    lax.fori_loop(0, 4, third_loop, 0)
+    if grid:
+        ring.small_finish(2)
+        ring.small_start(3)
+    lax.fori_loop(0, 4, fourth_loop, 0)
+    if grid:
+        ring.small_finish(3)
+
+        def last_loop(tau, _):
+            slot(tau)
+            return 0
+
+        lax.fori_loop(12, 12 + ring.stages - 1, last_loop, 0)
+        ring.drain()
+    if not grid:
+        result = pltpu.make_async_copy(G, gall, osem.at[4])
+        result.start()
+        result.wait()
+    small_result = pltpu.make_async_copy(SM, gsm, osem.at[5])
+    small_result.start()
+    for kind, n in (("down", 4), ("up", 4), ("qkv", 3), ("out", 1)):
+        for i in range(n):
+            for copy in exchange(kind, i):
+                copy.wait_send()
+    small_result.wait()
     for m in range(2):
         rows = ds(m * S, S)
         pltpu.make_async_copy(YB.at[rows], lo.at[rows], osem.at[m]).wait()
@@ -417,7 +752,7 @@
             relay_back(m).wait_send()
 
 
-def main_call(tok, cot, segk, segq, wq, wo, wu, wd, bq, bu, vec, S):
+def main_call(tok, cot, segk, segq, wq, wo, wu, wd, bq, bu, vec, S, grid):
     rows, D = tok.shape
     FF = 2 * wu.shape[1]
     hd, hf, hq = D // 2, FF // 2, 3 * D // 2
@@ -427,8 +762,7 @@
     V = pltpu.VMEM
     out_shape = (
         sds((rows, D), BF16), sds((rows, D), F32),
-        sds((D, hq), BF16), sds((hd, D), BF16), sds((D, hf), BF16), sds((hf, D), BF16),
-        sds((8, 2 * hq), F32), sds((8, FF), F32), sds((8, D), F32),
+        sds((BUCKETS * D, hd), BF16), sds((16, D), F32),
     )
     scratch = [
         V((D, 2 * hq), BF16), V((D, D), BF16), V((D, FF), BF16), V((FF, D), BF16), V((8, 2 * hq), F32), V((8, FF), F32),
@@ -437,18 +771,21 @@
         V((rows, D), BF16), V((rows, D), BF16), V((S, D), BF16), V((rows, 3 * D), BF16),
         V((rows, 128), F32), V((rows, 128), F32), V((S, D), F32), V((S, D), F32), V((2, S, S), F32),
         V((rows, D), BF16), V((rows, D), BF16), V((rows, D), BF16), V((rows, D), F32),
-        V((D, rows), BF16), V((D, rows), BF16), V((D, rows), BF16),
-        V((D, hq), BF16), V((hd, D), BF16), V((D, hf), BF16), V((hf, D), BF16),
-        V((8, 2 * hq), F32), V((8, FF), F32), V((8, D), F32), V((8, 2 * hq), F32), V((8, FF), F32), V((8, D), F32),
+        V((8, 2 * hq), F32), V((8, FF), F32), V((8, D), F32), V((16, D), F32), V((4, 16, D), F32),
+        V((BUCKETS * D, hd), BF16), V((BUCKETS * A_ROWS // 2, hd), BF16), V((BUCKETS * (A_ROWS // 2) // 4 * 5, hd), BF16),
+        V((BUCKETS * (D - A_ROWS) // 4 * 5, hd), BF16), V((BUCKETS * (D - A_ROWS) // 4, hd), BF16),
         pltpu.SemaphoreType.DMA((8,)), pltpu.SemaphoreType.DMA((6,)), pltpu.SemaphoreType.DMA((6,)),
         pltpu.SemaphoreType.DMA((2,)), pltpu.SemaphoreType.DMA((2,)),
-        pltpu.SemaphoreType.DMA((7,)), pltpu.SemaphoreType.DMA((7,)), pltpu.SemaphoreType.DMA((11,)),
+        pltpu.SemaphoreType.DMA((BUCKETS, 2)), pltpu.SemaphoreType.DMA((BUCKETS, 2)), pltpu.SemaphoreType.DMA((6,)),
+        pltpu.SemaphoreType.DMA((4,)), pltpu.SemaphoreType.DMA((4,)),
+        pltpu.SemaphoreType.DMA((BUCKETS, 8 * LINE + 3)), pltpu.SemaphoreType.DMA((BUCKETS, 8 * LINE + 3)),
+        pltpu.SemaphoreType.DMA((BUCKETS, 2)),
     ]
     return pl.pallas_call(
-        partial(main_kernel, D, FF, S),
+        partial(main_kernel, D, FF, S, grid),
         out_shape=out_shape,
         in_specs=[any_spec, any_spec, vm_spec, vm_spec] + [any_spec] * 6 + [vm_spec],
-        out_specs=(any_spec,) * 9,
+        out_specs=(any_spec,) * 4,
         scratch_shapes=scratch,
         compiler_params=pltpu.CompilerParams(collective_id=0, has_side_effects=True, vmem_limit_bytes=60 * 2**20),
         name="layer_pass",
@@ -467,17 +804,25 @@
     bq = jnp.concatenate([qv[0], jnp.zeros((hd,), F32), qv[1]])
     bq = jnp.broadcast_to(bq[None], (8, 3 * hd))
     bu = jnp.broadcast_to(up_bias.astype(F32), (8, up_bias.shape[1]))
-    lo, ig, gq, go, gu, gd, gsq, gsu, gsv = main_call(
+    grid = lax.axis_size("dp") == 2 * LINE
+    lo, ig, gall, gsm = main_call(
         tokens, out_cotangent, seg[:, :, None], seg[:, None, :],
-        w_qkv[0].reshape(D, 3 * hd), w_out[0], w_up[0], w_down[0], bq, bu, vec, S,
+        w_qkv[0].reshape(D, 3 * hd), w_out[0], w_up[0], w_down[0], bq, bu, vec, S, grid,
     )
     def own(v, size):
         return lax.dynamic_slice_in_dim(v, c * size, size, axis=-1)
-    sq = own(gsq[0], 3 * hd)
-    small = [jnp.concatenate([sq[:hd], sq[2 * hd :]]), own(gsu[0], up_bias.shape[1]), own(gsv[:6], hd).reshape(-1)]
-    tot = lax.psum(tuple(v.astype(BF16) for v in (gq, go, gu, gd, *small)), "dp")
-    gq, go, gu, gd, gqv, gub, gsv = (v.astype(F32) for v in tot)
-    gsv = gsv.reshape(6, hd)
+    if not grid:
+        gall, gsm = lax.psum(gall, "dp"), lax.psum(gsm, "dp")
+    F = up_bias.shape[1]
+    block = gall.astype(F32).reshape(BUCKETS, 2, hd, hd)
+    gd = block[0:4].transpose(0, 2, 1, 3).reshape(F, D)
+    gu = block[4:8].reshape(4, D, hd).transpose(1, 0, 2).reshape(D, F)
+    gq = block[8:11].reshape(3, D, hd).transpose(1, 0, 2)
+    go = block[11].transpose(1, 0, 2).reshape(hd, D)
+    sq = own(gsm[0:3].reshape(-1), 3 * hd)
+    gqv = jnp.concatenate([sq[:hd], sq[2 * hd :]])
+    gub = own(gsm[3:7].reshape(-1), F)
+    gsv = own(gsm[8:14], hd)
     return (
         lo[None], ig[None],
         gq.reshape(1, D, 3, hd), gqv.reshape(1, 2, hd), go[None], gu[None], gub[None], gd[None],

time: 413 us -> 330 us (0.80)
  waiting for transfers between devices: 193 us -> 0 us
  Pallas kernels: 135 us -> 271 us
  blocking collectives: 39.4 us -> 0 us
  local copies, waits for them, and re-layouts: 20.4 us -> 54.1 us
  between operations: 14.2 us -> 0.73 us
  other arithmetic: 10.9 us -> 2.82 us
    psum x1 -> x0, waiting for transfers between devices: 193 us -> none  [shards(): lax.psum(tuple((v.astype(BF16) for v in (gq, go, gu, gd, *small))), 'dp')]
    pallas_call x1, Pallas kernels: 135 us -> 271 us  [main_call(): pl.pallas_call(partial(main_kernel, D, FF, S, grid), out_shape=out_shape,...]
    psum x1 -> x0, blocking collectives: 39.4 us -> none  [shards(): lax.psum(tuple((v.astype(BF16) for v in (gq, go, gu, gd, *small))), 'dp')]
    another operation x1 -> x3, local copies, waits for them, and re-layouts: 0.01 us -> 15.6 us  [the longest x1 7.16 us: shards(): gd[None]]
    transpose x0 -> x3, local copies, waits for them, and re-layouts: none -> 14.2 us  [the longest x1 7.49 us: shards(): gu = block[4:8].reshape(4, D, hd).transpose(1, 0, 2).reshape(D, F)]
    broadcast_in_dim x4 -> x0, other arithmetic: 8.88 us -> none  [the longest x1 4.65 us: shards(): gu[None]]
    slice x8 -> x7, local copies, waits for them, and re-layouts: 3.58 us -> 12.1 us  [the longest x1 5.17 us: shards(): gd = block[0:4].transpose(0, 2, 1, 3).reshape(F, D)]
  transfers between devices with their start and end apart: 1 -> 0, of which waited for: 1 -> 0; matrix products, arithmetic and copies ran while one was open for 1% -> 0% of each run, Pallas kernels for 0% -> 0%
where the time goes in v2:
time: 330 us; the launch traced here: 329 us
  Pallas kernels  271 us (82%)
  local copies, waits for them, and re-layouts  54.1 us (16%)
    pallas_call x1, Pallas kernels, main_call(): pl.pallas_call(partial(main_kernel, D, FF, S, grid), out_shape=out_shape,...  271 us
    transpose x1, local copies, waits for them, and re-layouts, shards(): gu = block[4:8].reshape(4, D, hd).transpose(1, 0, 2).reshape(D, F)  7.49 us
    another operation x1, local copies, waits for them, and re-layouts, shards(): gd[None]  7.16 us

profile of v2, /device:TPU:0, one launch (start us, length us, event | category | flops | bytes accessed | tf_op | source)
XLA Modules:
  0.0 329.0 jit_solution(1575787074974141237)
XLA Ops:
  0.6 0.0 copy-start
  0.7 0.1 pad.5.clone
  0.7 0.6 copy-done
  1.3 0.6 broadcast_in_dim.47.segq
  1.9 0.7 convert_element_type.8
  2.7 0.7 convert_reduce_fusion
  3.4 1.4 maximum_maximum_fusion.vec
  4.8 0.6 broadcast_in_dim.49.bq_in
  5.4 0.6 broadcast_in_dim.52.bu_in
  6.0 0.9 copy.28.segk
  6.9 2.6 copy.27
  9.5 2.2 copy.29.wq_in
  11.7 271.4 %layer_pass.1 = (bf16[512,768]{1,0:T(8,128)(2,1)}, f32[512,768]{1,0:T(8,128)}, bf16[9216,384]{1,0:T(8,128)(2,1)}, f32[16,768]{1,0:T(8,128)}) custom-call(bf16[512,768]{1,0:T(8,128)(2,1)} %tok.1, bf16[512,768]{1,0:T(8,128)(2,1)} %cot.1, s32[2,256,1]{2,1,0:T(8,128)} %copy.28.segk, s32[2,1,256]{2,1,0:T(1,128)} %broadcast_in_dim.47.segq, ...), custom_call_target="tpu_custom_call" | custom-call | tf_op jit(solution)/shard_map/layer_pass/pallas_call | solution.py:784
  283.1 0.7 slice.58
  283.8 0.1 dynamic_slice.14
  283.9 0.6 broadcast_in_dim.56
  284.5 0.7 slice.53
  285.3 0.7 slice.61
  286.0 0.7 dynamic-slice_bitcast_fusion
  286.7 0.1 fusion.1
  286.8 0.6 reshape.57
  287.4 1.1 slice.68
  288.5 0.9 copy.30
  289.4 2.0 broadcast_in_dim_reshape.9
  291.4 3.5 %slice.67 = f32[2304,384]{1,0:T(8,128)} slice(bf16[9216,384]{1,0:T(8,128)(2,1)} %get-tuple-element.17), slice={[6144:8448], [0:384]} | slice | bytes 7077888 | tf_op jit(solution)/shard_map/slice | solution.py:820
  294.9 5.2 %fusion = (f32[3072,384]{1,0:T(8,128)S(1)}, f32[3072,384]{1,0:T(8,128)}) fusion(bf16[9216,384]{1,0:T(8,128)(2,1)} %get-tuple-element.17), kind=kLoop, calls=%fused_computation.10 | loop fusion | bytes 18874368 | tf_op jit(solution)/shard_map/slice | solution.py:818
  300.1 5.8 %copy.32 = f32[4,384,2,384]{3,2,1,0:T(2,128)} copy(f32[4,384,2,384]{3,1,2,0:T(8,128)S(1)} %bitcast.32) | data formatting | bytes 9437184 | tf_op jit(solution)/shard_map/transpose | solution.py:818
  305.8 7.2 %broadcast_in_dim_reshape.11 = f32[1,1536,768]{2,1,0:T(8,128)} reshape(f32[4,384,2,384]{3,2,1,0:T(2,128)} %copy.32) | data formatting | bytes 9437184 | tf_op jit(solution)/shard_map/broadcast_in_dim;reshape | solution.py:828
  313.0 7.5 %copy.31 = f32[768,4,384]{2,1,0:T(4,128)} copy(f32[768,4,384]{2,0,1:T(8,128)} %bitcast.31) | data formatting | bytes 9437184 | tf_op jit(solution)/shard_map/transpose | solution.py:819
  320.5 0.0 copy-start.2
  320.5 0.0 copy-start.1
  320.5 6.5 %broadcast_in_dim_reshape.10 = f32[1,768,1536]{2,1,0:T(8,128)} reshape(f32[768,4,384]{2,1,0:T(4,128)} %copy.31) | data formatting | bytes 9437184 | tf_op jit(solution)/shard_map/broadcast_in_dim;reshape | solution.py:828
  327.0 0.0 copy-done.2
  327.0 0.9 copy.35
  327.9 0.0 copy-done.1
  327.9 1.1 copy.36
  (9 shorter events, 0.1 us)
Async XLA Ops:
  0.6 0.7 copy-start
  320.5 6.5 %copy-start.2 = (bf16[512,768]{1,0:T(8,128)(2,1)S(1)}, bf16[512,768]{1,0:T(8,128)(2,1)}, u32[]{:S(2)}) copy-start(bf16[512,768]{1,0:T(8,128)(2,1)} %get-tuple-element.15) | copy-start | bytes 2359300
  320.5 7.4 %copy-start.1 = (f32[512,768]{1,0:T(8,128)S(1)}, f32[512,768]{1,0:T(8,128)}, u32[]{:S(2)}) copy-start(f32[512,768]{1,0:T(8,128)} %get-tuple-element.16) | copy-start | bytes 4718596

commit v3 on v2

--- a/solution.py
+++ b/solution.py
@@ -32,6 +32,21 @@
 
 def ds(start, size, align=None):
     return pl.ds(pl.multiple_of(start, align or size), size)
+
+
+def eights(v):
+    return jnp.sum(v.reshape(v.shape[0] // 8, 8, v.shape[1]), axis=0)
+
+
+def gelu_and_slope(g):
+    size = jnp.abs(g)
+    x = 1.0 + 0.2316419 * size
+    t = pl.reciprocal(x, approx=True)
+    t = t * (2.0 - x * t)
+    density = 0.3989422804014327 * jnp.exp2(g * g * -0.7213475204444817)
+    tail = ((((1.330274429 * t - 1.821255978) * t + 1.781477937) * t - 0.356563782) * t + 0.319381530) * t * density
+    cdf = jnp.where(g > 0.0, 1.0 - tail, tail)
+    return g * cdf, cdf + g * density
 
 
 def row_mean(v):
@@ -310,10 +325,10 @@
 
 def main_kernel(
     D, FF, S, grid,
-    tok, cot, segk, segq, wq_in, wo_in, wu_in, wd_in, bq_in, bu_in, vec,
+    tok, cot, seg, wq_in, qv_in, wo_in, wu_in, ub_in, wd_in, add_in, gain, shift,
     lo, ig, gall, gsm,
     wq, wo, wu, wd, bq, bu,
-    X, QKV, O, N1, N2, Hr, U, GP, R, dB, dA, dOs, dQKV,
+    X, QKV, O, N1, N2, Hr, U, GP, R, DST, dB, dA, dOs, dQKV,
     r1s, r2s, Hf, Zf, bias, dY, YB, IGB, IGF,
     sq, su, sv, SM, SML, G, LA1, LA, LB, LS,
     lsem, wsend, wrecv, rsend, rrecv, gsend, grecv, osem, ssend, srecv, asend, arecv, csem,
@@ -335,21 +350,16 @@
         ring = Reduction(D, s, d, c, G, gall, LA1, LA, LB, LS, SM, SML, asend, arecv, ssend, srecv, csem)
         ring.greet(barrier)
 
-    def places(k):
-        return [
-            (wq_in, wq.at[:, ds(k * half_q, half_q, 128)]),
-            (bq_in, bq.at[:, ds(k * half_q, half_q, 128)]),
-            (wo_in, wo.at[ds(k * half_d, half_d), :]),
-            (bu_in, bu.at[:, ds(k * half_f, half_f, 128)]),
-            (wu_in, wu.at[:, ds(k * half_f, half_f, 128)]),
-            (wd_in, wd.at[ds(k * half_f, half_f), :]),
-        ]
-
-    own_places = places(c)
-    local = [pltpu.make_async_copy(src, dst, lsem.at[i]) for i, (src, dst) in enumerate(own_places)]
+    weights = [(wq_in.at[j], wq.at[:, ds(c * half_q + j * half_d, half_d)]) for j in range(3)] + [
+        (wo_in, wo.at[ds(c * half_d, half_d), :]),
+        (wu_in, wu.at[:, ds(c * half_f, half_f, 128)]),
+        (wd_in, wd.at[ds(c * half_f, half_f), :]),
+    ]
+    biases = [bq.at[:, ds(c * half_q, half_q, 128)], bu.at[:, ds(c * half_f, half_f, 128)]]
+    local = [pltpu.make_async_copy(src, dst, lsem.at[i]) for i, (src, dst) in enumerate(weights)]
     remote = [
         pltpu.make_async_remote_copy(src, dst, wsend.at[i], wrecv.at[i], device_id=core_peer, device_id_type=MESH)
-        for i, (src, dst) in enumerate(own_places)
+        for i, (src, dst) in enumerate(weights + [(b, b) for b in biases])
     ]
     tok_copy = pltpu.make_async_copy(tok, X, lsem.at[6])
     cot_copy = pltpu.make_async_copy(cot, dY, lsem.at[7])
@@ -362,21 +372,19 @@
     def _():
         cot_copy.start()
 
-    local[0].start()
-    local[1].start()
+    for copy in local:
+        copy.start()
+    bq[:, ds(c * half_q, half_d)] = jnp.broadcast_to(qv_in[0:1, :].astype(F32), (8, half_d))
+    bq[:, ds(c * half_q + half_d, half_d)] = jnp.zeros((8, half_d), F32)
+    bq[:, ds(c * half_q + 2 * half_d, half_d)] = jnp.broadcast_to(qv_in[1:2, :].astype(F32), (8, half_d))
+    bu[:, ds(c * half_f, half_f)] = jnp.broadcast_to(ub_in[...].astype(F32), (8, half_f))
     pl.semaphore_wait(barrier, 2 + ring.greetings() if grid else 2)
-    for i in range(6):
+    for i in (0, 1, 2, 6, 7):
         remote[i].start()
-        if i >= 2:
-            local[i].start()
-
-    def need(*which):
-        for i in which:
-            local[i].wait()
-            remote[i].wait_recv()
 
     for q in range(2):
-        bias[q] = jnp.where(segk[q] == segq[q], 0.0, masked_score)
+        row = jnp.broadcast_to(seg[pl.ds(2 * c + q, 1), :].astype(F32), (S, S))
+        bias[q] = jnp.where(row.T == row, 0.0, masked_score)
     sq[...] = jnp.zeros_like(sq)
     su[...] = jnp.zeros_like(su)
     sv[...] = jnp.zeros_like(sv)
@@ -386,6 +394,12 @@
     first_half = jnp.where(lane < HEAD_DIM, 1.0, 0.0).astype(BF16)
     second_half = jnp.where(lane < HEAD_DIM, 0.0, 1.0).astype(BF16)
 
+    def need(*which):
+        for i in which:
+            if i < 6:
+                local[i].wait()
+            remote[i].wait_recv()
+
     def relay(m):
         rows = ds(m * S, S)
         return pltpu.make_async_remote_copy(YB.at[rows], X.at[rows], rsend.at[m], rrecv.at[m], device_id=x_peer, device_id_type=MESH)
@@ -398,11 +412,19 @@
         base = (p // lo_pairs) * half_q + (p % lo_pairs) * 128
         return ds(base, 128), ds(base + half_d, 128), ds(base + 2 * half_d, 128)
 
-    def normed(z, which):
-        centered = z - row_mean(z)
-        scaled = lax.rsqrt(row_mean(centered * centered) + norm_eps)
-        n = centered * scaled
-        return n, scaled, n * vec[2 + which : 3 + which, :] + vec[4 + which : 5 + which, :]
+    def normed(m, which, N, rs, finish):
+        def norm_rows(j, _):
+            near, rows = ds(j * 32, 32), ds(m * S + j * 32, 32)
+            z = Zf[near, :]
+            centered = z - row_mean(z)
+            scaled = lax.rsqrt(row_mean(centered * centered) + norm_eps)
+            n = centered * scaled
+            N[rows, :] = n.astype(BF16)
+            rs[rows, :] = jnp.broadcast_to(scaled, (32, 128))
+            finish(near, rows, n * gain[which : which + 1, :] + shift[which : which + 1, :])
+            return 0
+
+        lax.fori_loop(0, S // 32, norm_rows, 0, unroll=4)
 
     def forward(t, m):
         rows = ds(m * S, S)
@@ -412,7 +434,9 @@
             @pl.when(s == 0)
             def _():
                 tok_copy.wait()
-            need(0, 1)
+            need(0, 1, 2, 6, 7)
+            remote[3].start()
+            remote[4].start()
 
         @pl.when(s == 1)
         def _():
@@ -423,53 +447,56 @@
             QKV[rows, cols] = (mm(X[rows, :], wq[:, cols]) + bq[0:1, cols]).astype(BF16)
             return 0
 
-        lax.fori_loop(0, 3 * D // 256, qkv_tile, 0)
+        lax.fori_loop(0, 3 * D // 256, qkv_tile, 0, unroll=3)
 
         def attend(p, _):
             qc, kc, vc = pair_columns(p)
             q2, k2, v2 = QKV[rows, qc], QKV[rows, kc], QKV[rows, vc]
             vt = v2.T
+            weights = ds((m * pairs + p) * S, S)
             outs = []
             for h, mask in enumerate((first_scaled, second_scaled)):
-                st = mm_nt(k2 * mask, q2) + bias[m]
-                e = jnp.exp(st - jnp.max(st, axis=0, keepdims=True))
-                r = (e * (1.0 / jnp.sum(e, axis=0, keepdims=True))).astype(BF16)
-                R[ds((m * pairs + p) * 2 * S + h * S, S), :] = r
-                outs.append(mm(vt[h * HEAD_DIM : (h + 1) * HEAD_DIM], r))
+                kh = k2 * mask
+                for part in range(0, S, 128):
+                    st = mm_nt(kh, q2[part : part + 128, :]) + bias[m, :, part : part + 128]
+                    e = jnp.exp(st - jnp.max(st, axis=0, keepdims=True))
+                    R[weights, h * S + part : h * S + part + 128] = (e * (1.0 / jnp.sum(e, axis=0, keepdims=True))).astype(BF16)
+                outs.append(mm(vt[h * HEAD_DIM : (h + 1) * HEAD_DIM], R[weights, h * S : (h + 1) * S]))
             O[rows, ds(p * 128, 128)] = jnp.concatenate(outs, axis=0).T.astype(BF16)
             return 0
 
-        lax.fori_loop(0, pairs, attend, 0)
+        lax.fori_loop(0, pairs, attend, 0, unroll=2)
 
         @pl.when(t == 0)
         def _():
-            need(2)
+            need(3)
+            remote[5].start()
 
         def out_tile(i, _):
             cols = ds(i * 256, 256)
-            Zf[:, cols] = mm(O[rows, :], wo[:, cols]) + X[rows, cols].astype(F32) + vec[0:1, cols]
-            return 0
-
-        lax.fori_loop(0, D // 256, out_tile, 0)
-        n, r, h = normed(Zf[...], 0)
-        N1[rows, :] = n.astype(BF16)
-        r1s[rows, :] = jnp.broadcast_to(r, (S, 128))
-        Hf[...] = h
-        Hr[rows, :] = h.astype(BF16)
+            Zf[:, cols] = mm(O[rows, :], wo[:, cols]) + X[rows, cols].astype(F32) + add_in[0:1, cols]
+            return 0
+
+        lax.fori_loop(0, D // 256, out_tile, 0, unroll=3)
+
+        def first_done(near, rows, h):
+            Hf[near, :] = h
+            Hr[rows, :] = h.astype(BF16)
+
+        normed(m, 0, N1, r1s, first_done)
 
         @pl.when(t == 0)
         def _():
-            need(3, 4)
+            need(4)
 
         def up_tile(i, _):
             cols = ds(i * 256, 256)
-            g = mm(Hr[rows, :], wu[:, cols]) + bu[0:1, cols]
-            cdf = 0.5 + 0.5 * lax.erf(g * 0.7071067811865476)
-            U[rows, cols] = (g * cdf).astype(BF16)
-            GP[rows, cols] = (cdf + g * (0.3989422804014327 * jnp.exp(g * g * -0.5))).astype(BF16)
-            return 0
-
-        lax.fori_loop(0, FF // 256, up_tile, 0)
+            u, slope = gelu_and_slope(mm(Hr[rows, :], wu[:, cols]) + bu[0:1, cols])
+            U[rows, cols] = u.astype(BF16)
+            GP[rows, cols] = slope.astype(BF16)
+            return 0
+
+        lax.fori_loop(0, FF // 256, up_tile, 0, unroll=4)
 
         @pl.when(t == 0)
         def _():
@@ -477,32 +504,36 @@
 
         def down_tile(i, _):
             cols = ds(i * 256, 256)
-            Zf[:, cols] = mm(U[rows, :], wd[:, cols]) + Hf[:, cols] + vec[1:2, cols]
-            return 0
-
-        lax.fori_loop(0, D // 256, down_tile, 0)
-        n, r, y = normed(Zf[...], 1)
-        N2[rows, :] = n.astype(BF16)
-        r2s[rows, :] = jnp.broadcast_to(r, (S, 128))
-        YB[rows, :] = y.astype(BF16)
+            Zf[:, cols] = mm(U[rows, :], wd[:, cols]) + Hf[:, cols] + add_in[1:2, cols]
+            return 0
+
+        lax.fori_loop(0, D // 256, down_tile, 0, unroll=3)
+
+        def second_done(near, rows, y):
+            YB[rows, :] = y.astype(BF16)
+
+        normed(m, 1, N2, r2s, second_done)
         pltpu.make_async_copy(YB.at[rows], lo.at[rows], osem.at[m]).start()
 
         @pl.when(s == 0)
         def _():
             relay(m).start()
 
-    def column_sum(v):
-        return jnp.sum(v, axis=0, keepdims=True)
-
-    def norm_back(dy, n, r, which):
-        e = dy * vec[2 + which : 3 + which, :]
-        dz = r * (e - row_mean(e) - n * row_mean(e * n))
-        sv[0 + which : 1 + which, :] += column_sum(dz)
-        sv[2 + which : 3 + which, :] += column_sum(dy * n)
-        sv[4 + which : 5 + which, :] += column_sum(dy)
-        return dz
-
-    def backward(t, m):
+    def norm_back(m, which, get, N, rs, low):
+        def back_rows(j, sums):
+            near, rows = ds(j * 32, 32), ds(m * S + j * 32, 32)
+            dy, n = get(near, rows), N[rows, :].astype(F32)
+            e = dy * gain[which : which + 1, :]
+            dz = rs[rows, 0:1] * (e - row_mean(e) - n * row_mean(e * n))
+            Zf[near, :] = dz
+            low[rows, :] = dz.astype(BF16)
+            return sums[0] + eights(dz), sums[1] + eights(dy * n), sums[2] + eights(dy)
+
+        sums = lax.fori_loop(0, S // 32, back_rows, (jnp.zeros((8, D), F32),) * 3, unroll=2)
+        for i in range(3):
+            sv[2 * i + which] += sums[i]
+
+    def backward(t, m, last):
         rows = ds(m * S, S)
 
         @pl.when(s == 0)
@@ -513,61 +544,64 @@
         def _():
             cot_copy.wait()
 
-        dz2 = norm_back(dY[rows, :].astype(F32), N2[rows, :].astype(F32), r2s[rows, 0:1], 1)
-        Zf[...] = dz2
-        dB[rows, :] = dz2.astype(BF16)
+        norm_back(m, 1, lambda near, rows: dY[rows, :].astype(F32), N2, r2s, dB)
 
         def down_back(i, _):
             cols = ds(i * 256, 256)
             dg = mm_nt(dB[rows, :], wd[cols, :]) * GP[rows, cols].astype(F32)
-            su[0:1, cols] += column_sum(dg)
+            su[:, cols] += eights(dg)
             GP[rows, cols] = dg.astype(BF16)
             return 0
 
-        lax.fori_loop(0, FF // 256, down_back, 0)
+        lax.fori_loop(0, FF // 256, down_back, 0, unroll=4)
+        last(0)
 
         def up_back(i, _):
             cols = ds(i * 256, 256)
             Hf[:, cols] = mm_nt(GP[rows, :], wu[cols, :]) + Zf[:, cols]
             return 0
 
-        lax.fori_loop(0, D // 256, up_back, 0)
-        dz1 = norm_back(Hf[...], N1[rows, :].astype(F32), r1s[rows, 0:1], 0)
-        Zf[...] = dz1
-        dA[rows, :] = dz1.astype(BF16)
+        lax.fori_loop(0, D // 256, up_back, 0, unroll=3)
+        norm_back(m, 0, lambda near, rows: Hf[near, :], N1, r1s, dA)
+        last(1)
 
         def out_back(i, _):
             cols = ds(i * 256, 256)
             dOs[:, cols] = mm_nt(dA[rows, :], wo[cols, :]).astype(BF16)
             return 0
 
-        lax.fori_loop(0, D // 256, out_back, 0)
+        lax.fori_loop(0, D // 256, out_back, 0, unroll=3)
+        last(2)
 
         def attend_back(p, _):
             qc, kc, vc = pair_columns(p)
             q2, k2, v2 = QKV[rows, qc], QKV[rows, kc], QKV[rows, vc]
             do2 = dOs[:, ds(p * 128, 128)]
             kt = k2.T
-            dk, dv, dqt = 0.0, 0.0, []
-            for h, (scaled, half) in enumerate(((first_scaled, first_half), (second_scaled, second_half))):
-                r = R[ds((m * pairs + p) * 2 * S + h * S, S), :]
-                drt = mm_nt(v2 * half, do2)
-                rf = r.astype(F32)
-                w = rf * drt
-                dst = (w - rf * jnp.sum(w, axis=0, keepdims=True)).astype(BF16)
-                dk += mm(dst, q2 * scaled)
-                dv += mm(r, do2 * half)
-                dqt.append(mm(kt[h * HEAD_DIM : (h + 1) * HEAD_DIM], dst))
+            weights = ds((m * pairs + p) * S, S)
+            turn = p % 2
+            for h, half in enumerate((first_half, second_half)):
+                vh = v2 * half
+                for part in range(0, S, 128):
+                    cols = slice(h * S + part, h * S + part + 128)
+                    drt = mm_nt(vh, do2[part : part + 128, :])
+                    rf = R[weights, cols].astype(F32)
+                    DST[turn, :, cols] = (rf * (drt - jnp.sum(rf * drt, axis=0, keepdims=True))).astype(BF16)
+            dst = DST[turn]
+            dk = mm(dst, jnp.concatenate([q2 * first_scaled, q2 * second_scaled], axis=0))
+            dv = mm(R[weights, :], jnp.concatenate([do2 * first_half, do2 * second_half], axis=0))
+            dqt = [mm(kt[h * HEAD_DIM : (h + 1) * HEAD_DIM], dst[:, h * S : (h + 1) * S]) for h in range(2)]
             dq = (jnp.concatenate(dqt, axis=0) * 0.125).T.astype(BF16)
             dvb = dv.astype(BF16)
             dQKV[rows, qc] = dq
             dQKV[rows, kc] = dk.astype(BF16)
             dQKV[rows, vc] = dvb
-            sq[0:1, qc] += column_sum(dq.astype(F32))
-            sq[0:1, vc] += column_sum(dvb.astype(F32))
-            return 0
-
-        lax.fori_loop(0, pairs, attend_back, 0)
+            sq[:, qc] += eights(dq.astype(F32))
+            sq[:, vc] += eights(dvb.astype(F32))
+            return 0
+
+        lax.fori_loop(0, pairs, attend_back, 0, unroll=2)
+        last(3)
 
         def in_back(i, _):
             cols = ds(i * 256, 256)
@@ -576,43 +610,27 @@
             IGB[rows, cols] = dx.astype(BF16)
             return 0
 
-        lax.fori_loop(0, D // 256, in_back, 0)
+        lax.fori_loop(0, D // 256, in_back, 0, unroll=3)
         pltpu.make_async_copy(IGF.at[rows], ig.at[rows], osem.at[2 + m]).start()
 
         @pl.when(s == 1)
         def _():
             relay_back(m).start()
 
-    def step(t, _):
-        back = jnp.where(s == 0, t // 2, t % 2)
-        m = jnp.where(s == 0, t % 2, t // 2)
-
-        @pl.when(back == 0)
-        def _():
-            forward(t, m)
-
-        @pl.when(back == 1)
-        def _():
-            backward(t, m)
-
-        return 0
-
-    lax.fori_loop(0, 4, step, 0)
-    for i in range(6):
-        remote[i].wait_send()
-
     W = D // 2
 
+    def across(i, start, size, right):
+        return mm(R[ds(i * D + start, size, 128), :], right)
+
     def grad_tiles(k, kind, i):
-        if kind == "down" or kind == "out":
-            rows = ds(k * half_f + i * W, W, 128) if kind == "down" else ds(k * half_d, W)
-            if kind == "out":
-                return [across(1, k * half_d, W, dA[:, q * W : (q + 1) * W]) for q in range(2)]
-            left = U[:, rows].T
+        if kind == "down":
+            left = U[:, ds(k * half_f + i * W, W, 128)].T
             return [mm(left, dB[:, q * W : (q + 1) * W]) for q in range(2)]
+        if kind == "out":
+            return [across(1, k * half_d, W, dA[:, q * W : (q + 1) * W]) for q in range(2)]
         cols = ds(k * (half_f if kind == "up" else half_q) + i * W, W, 128)
-        i, right = (0, GP) if kind == "up" else (2, dQKV)
-        return [across(i, q * W, W, right[:, cols]) for q in range(2)]
+        which, right = (0, GP) if kind == "up" else (2, dQKV)
+        return [across(which, q * W, W, right[:, cols]) for q in range(2)]
 
     first = {"down": 0, "up": 4, "qkv": 8, "out": 11}
 
@@ -650,33 +668,72 @@
         if grid:
             ring.slot(tau)
 
+    def give_all_down():
+        def give_down(i, _):
+            give("down", i)
+            return 0
+
+        lax.fori_loop(0, 4, give_down, 0)
+
+    def step(t, _):
+        back = jnp.where(s == 0, t // 2, t % 2)
+        m = jnp.where(s == 0, t % 2, t // 2)
+
+        def last(i):
+            @pl.when((s == 0) & (m == 1))
+            def _():
+                if i == 0:
+                    give_all_down()
+                keep("down", i)
+                slot(i)
+
+        @pl.when(back == 0)
+        def _():
+            forward(t, m)
+
+        @pl.when(back == 1)
+        def _():
+            backward(t, m, last)
+
+        return 0
+
+    lax.fori_loop(0, 4, step, 0)
+
+    @pl.when(s == 1)
+    def _():
+        give_all_down()
+
+        def keep_down(i, _):
+            keep("down", i)
+            slot(i)
+            return 0
+
+        lax.fori_loop(0, 4, keep_down, 0)
+
+    for i, whole in enumerate((Hr, O, X)):
+        R[i * D : (i + 1) * D, :] = whole[...].T
+
+    def give_up(i, _):
+        give("up", i)
+        return 0
+
+    lax.fori_loop(0, 4, give_up, 0)
+
+    def total(v):
+        return jnp.sum(v, axis=0, keepdims=True)
+
     for i in range(3):
-        SM[i : i + 1, :] = sq[0:1, i * D : (i + 1) * D]
+        SM[i : i + 1, :] = total(sq[:, i * D : (i + 1) * D])
     for i in range(4):
-        SM[3 + i : 4 + i, :] = su[0:1, i * D : (i + 1) * D]
+        SM[3 + i : 4 + i, :] = total(su[:, i * D : (i + 1) * D])
     SM[7:8, :] = jnp.zeros((1, D), F32)
-    SM[8:16, :] = sv[...]
+    for i in range(6):
+        SM[8 + i : 9 + i, :] = total(sv[i])
+    SM[14:16, :] = jnp.zeros((2, D), F32)
     small_core = pltpu.make_async_remote_copy(SM, SML.at[0], ssend.at[0], srecv.at[0], device_id=core_peer, device_id_type=MESH)
     small_core.start()
-    for i, whole in enumerate((Hr, O, X)):
-        for m in range(2):
-            R[(2 * i + m) * D : (2 * i + m + 1) * D, :] = whole[m * S : (m + 1) * S, :].T
-
-    def across(i, start, size, right):
-        return sum(mm(R[ds((2 * i + m) * D + start, size, 128), :], right[m * S : (m + 1) * S]) for m in range(2))
-
-
-    def first_loop(i, _):
-        give("down", i)
-        return 0
-
-    def second_loop(i, _):
-        keep("down", i)
-        slot(i)
-        give("up", i)
-        return 0
-
-    def third_loop(i, _):
+
+    def keep_up(i, _):
         keep("up", i)
         slot(4 + i)
 
@@ -690,42 +747,39 @@
 
         return 0
 
-    def fourth_loop(i, _):
-        @pl.when(i < 3)
-        def _():
-            keep("qkv", i)
-
-        @pl.when(i == 3)
-        def _():
-            keep("out", 0)
-
-        slot(8 + i)
-        return 0
-
-    lax.fori_loop(0, 4, first_loop, 0)
+    lax.fori_loop(0, 4, keep_up, 0)
     small_core.wait()
     SM[...] += SML[0]
     if grid:
         ring.small_start(1)
-    lax.fori_loop(0, 4, second_loop, 0)
+
+    def keep_rest(i, _):
+        @pl.when(i < 3)
+        def _():
+            keep("qkv", i)
+
+        @pl.when(i == 3)
+        def _():
+            keep("out", 0)
+
+        slot(8 + i)
+        return 0
+
+    lax.fori_loop(0, 4, keep_rest, 0)
     if grid:
+        def last_slot(tau, _):
+            slot(tau)
+            return 0
+
         ring.small_finish(1)
         ring.small_start(2)
-    lax.fori_loop(0, 4, third_loop, 0)
-    if grid:
+        lax.fori_loop(12, 14, last_slot, 0)
         ring.small_finish(2)
         ring.small_start(3)
-    lax.fori_loop(0, 4, fourth_loop, 0)
-    if grid:
+        lax.fori_loop(14, BUCKETS + ring.stages - 1, last_slot, 0)
         ring.small_finish(3)
-
-        def last_loop(tau, _):
-            slot(tau)
-            return 0
-
-        lax.fori_loop(12, 12 + ring.stages - 1, last_loop, 0)
         ring.drain()
-    if not grid:
+    else:
         result = pltpu.make_async_copy(G, gall, osem.at[4])
         result.start()
         result.wait()
@@ -736,6 +790,8 @@
             for copy in exchange(kind, i):
                 copy.wait_send()
     small_result.wait()
+    for copy in remote:
+        copy.wait_send()
     for m in range(2):
         rows = ds(m * S, S)
         pltpu.make_async_copy(YB.at[rows], lo.at[rows], osem.at[m]).wait()
@@ -752,81 +808,112 @@
             relay_back(m).wait_send()
 
 
-def main_call(tok, cot, segk, segq, wq, wo, wu, wd, bq, bu, vec, S, grid):
+def main_call(grid, S, tok, cot, seg, wq, qv, wo, wu, ub, wd, add, gain, shift):
     rows, D = tok.shape
     FF = 2 * wu.shape[1]
-    hd, hf, hq = D // 2, FF // 2, 3 * D // 2
+    hd, hq = D // 2, 3 * D // 2
     any_spec = pl.BlockSpec(memory_space=pl.ANY)
     vm_spec = pl.BlockSpec(memory_space=pltpu.VMEM)
     sds = jax.ShapeDtypeStruct
-    V = pltpu.VMEM
-    out_shape = (
-        sds((rows, D), BF16), sds((rows, D), F32),
-        sds((BUCKETS * D, hd), BF16), sds((16, D), F32),
-    )
+    V, DMA = pltpu.VMEM, pltpu.SemaphoreType.DMA
+    line_a, line_b = A_ROWS // 2 // LINE, (D - A_ROWS) // LINE
     scratch = [
         V((D, 2 * hq), BF16), V((D, D), BF16), V((D, FF), BF16), V((FF, D), BF16), V((8, 2 * hq), F32), V((8, FF), F32),
         V((rows, D), BF16), V((rows, 3 * D), BF16), V((rows, D), BF16), V((rows, D), BF16), V((rows, D), BF16), V((rows, D), BF16),
-        V((rows, FF), BF16), V((rows, FF), BF16), V((2 * (D // HEAD_DIM) * S, S), BF16),
+        V((rows, FF), BF16), V((rows, FF), BF16), V((2 * (D // 128) * S, 2 * S), BF16), V((2, S, 2 * S), BF16),
         V((rows, D), BF16), V((rows, D), BF16), V((S, D), BF16), V((rows, 3 * D), BF16),
         V((rows, 128), F32), V((rows, 128), F32), V((S, D), F32), V((S, D), F32), V((2, S, S), F32),
         V((rows, D), BF16), V((rows, D), BF16), V((rows, D), BF16), V((rows, D), F32),
-        V((8, 2 * hq), F32), V((8, FF), F32), V((8, D), F32), V((16, D), F32), V((4, 16, D), F32),
-        V((BUCKETS * D, hd), BF16), V((BUCKETS * A_ROWS // 2, hd), BF16), V((BUCKETS * (A_ROWS // 2) // 4 * 5, hd), BF16),
-        V((BUCKETS * (D - A_ROWS) // 4 * 5, hd), BF16), V((BUCKETS * (D - A_ROWS) // 4, hd), BF16),
-        pltpu.SemaphoreType.DMA((8,)), pltpu.SemaphoreType.DMA((6,)), pltpu.SemaphoreType.DMA((6,)),
-        pltpu.SemaphoreType.DMA((2,)), pltpu.SemaphoreType.DMA((2,)),
-        pltpu.SemaphoreType.DMA((BUCKETS, 2)), pltpu.SemaphoreType.DMA((BUCKETS, 2)), pltpu.SemaphoreType.DMA((6,)),
-        pltpu.SemaphoreType.DMA((4,)), pltpu.SemaphoreType.DMA((4,)),
-        pltpu.SemaphoreType.DMA((BUCKETS, 8 * LINE + 3)), pltpu.SemaphoreType.DMA((BUCKETS, 8 * LINE + 3)),
-        pltpu.SemaphoreType.DMA((BUCKETS, 2)),
+        V((8, 2 * hq), F32), V((8, FF), F32), V((6, 8, D), F32), V((16, D), F32), V((4, 16, D), F32),
+        V((BUCKETS * D, hd), BF16), V((BUCKETS * A_ROWS // 2, hd), BF16), V((BUCKETS * line_a * (LINE + 1), hd), BF16),
+        V((BUCKETS * line_b * (LINE + 1), hd), BF16), V((BUCKETS * line_b, hd), BF16),
+        DMA((8,)), DMA((8,)), DMA((8,)), DMA((2,)), DMA((2,)),
+        DMA((BUCKETS, 2)), DMA((BUCKETS, 2)), DMA((6,)), DMA((4,)), DMA((4,)),
+        DMA((BUCKETS, 8 * LINE + 3)), DMA((BUCKETS, 8 * LINE + 3)), DMA((BUCKETS, 2)),
     ]
     return pl.pallas_call(
         partial(main_kernel, D, FF, S, grid),
-        out_shape=out_shape,
-        in_specs=[any_spec, any_spec, vm_spec, vm_spec] + [any_spec] * 6 + [vm_spec],
+        out_shape=(sds((rows, D), BF16), sds((rows, D), F32), sds((BUCKETS * D, hd), BF16), sds((16, D), F32)),
+        in_specs=[any_spec, any_spec, vm_spec, any_spec, vm_spec, any_spec, any_spec, vm_spec, any_spec, vm_spec, vm_spec, vm_spec],
         out_specs=(any_spec,) * 4,
         scratch_shapes=scratch,
         compiler_params=pltpu.CompilerParams(collective_id=0, has_side_effects=True, vmem_limit_bytes=60 * 2**20),
         name="layer_pass",
-    )(tok, cot, segk, segq, wq, wo, wu, wd, bq, bu, vec)
+    )(tok, cot, seg, wq, qv, wo, wu, ub, wd, add, gain, shift)
+
+
+def unpack_kernel(D, block, sums, gq, gqv, go, gu, gub, gd, ga, gg, gs):
+    b = pl.program_id(0)
+    c = lax.axis_index("tensor")
+    W = D // 2
+
+    @pl.when(b < 4)
+    def _():
+        for q in range(2):
+            gd[:, q * W : (q + 1) * W] = block[q * W : (q + 1) * W, :].astype(F32)
+
+    @pl.when((b >= 4) & (b < 8))
+    def _():
+        gu[...] = block[...].astype(F32)
+
+    @pl.when((b >= 8) & (b < 11))
+    def _():
+        gq[0] = block[...].astype(F32)
+
+    @pl.when(b == 11)
+    def _():
+        for q in range(2):
+            go[:, q * W : (q + 1) * W] = block[q * W : (q + 1) * W, :].astype(F32)
+        own = ds(c * W, W)
+        gqv[0:1, :] = sums[pl.ds(c, 1), own]
+        gqv[1:2, :] = sums[pl.ds(1 + c, 1), own]
+        for i in range(2):
+            gub[:, i * D : (i + 1) * D] = sums[pl.ds(3 + 2 * c + i, 1), :]
+            ga[i : i + 1, :] = sums[8 + i : 9 + i, own]
+            gg[i : i + 1, :] = sums[10 + i : 11 + i, own]
+            gs[i : i + 1, :] = sums[12 + i : 13 + i, own]
+
+
+def unpack_call(gall, gsm, D, FF):
+    W, F = D // 2, FF // 2
+    sds = jax.ShapeDtypeStruct
+
+    def whole(*shape):
+        return pl.BlockSpec(shape, lambda b: (0,) * len(shape))
+
+    return pl.pallas_call(
+        partial(unpack_kernel, D),
+        grid=(BUCKETS,),
+        in_specs=[pl.BlockSpec((D, W), lambda b: (b, 0)), whole(16, D)],
+        out_specs=(
+            pl.BlockSpec((1, D, W), lambda b: (jnp.clip(b - 8, 0, 2), 0, 0)), whole(2, W), whole(W, D),
+            pl.BlockSpec((D, W), lambda b: (0, jnp.clip(b - 4, 0, 3))), whole(1, F),
+            pl.BlockSpec((W, D), lambda b: (jnp.minimum(b, 3), 0)), whole(2, W), whole(2, W), whole(2, W),
+        ),
+        out_shape=(
+            sds((3, D, W), F32), sds((2, W), F32), sds((W, D), F32), sds((D, F), F32), sds((1, F), F32),
+            sds((F, D), F32), sds((2, W), F32), sds((2, W), F32), sds((2, W), F32),
+        ),
+        compiler_params=pltpu.CompilerParams(vmem_limit_bytes=48 * 2**20),
+        name="unpack",
+    )(gall, gsm)
 
 
 def shards(tokens, segment_ids, out_cotangent, w_qkv, qv_bias, w_out, w_up, up_bias, w_down, add_bias, norm_gain, norm_bias):
-    c = lax.axis_index("tensor")
     D = tokens.shape[1]
-    hd = D // 2
+    FF = 2 * w_up.shape[2]
     S = segment_ids.shape[1]
-    seqs = tokens.shape[0] // S
-    seg = lax.dynamic_slice_in_dim(segment_ids, c * seqs, seqs, axis=0)
-    vec = jnp.concatenate([add_bias[0], norm_gain[0], norm_bias[0], jnp.zeros((2, D), F32)], axis=0)
-    qv = qv_bias[0].astype(F32)
-    bq = jnp.concatenate([qv[0], jnp.zeros((hd,), F32), qv[1]])
-    bq = jnp.broadcast_to(bq[None], (8, 3 * hd))
-    bu = jnp.broadcast_to(up_bias.astype(F32), (8, up_bias.shape[1]))
     grid = lax.axis_size("dp") == 2 * LINE
     lo, ig, gall, gsm = main_call(
-        tokens, out_cotangent, seg[:, :, None], seg[:, None, :],
-        w_qkv[0].reshape(D, 3 * hd), w_out[0], w_up[0], w_down[0], bq, bu, vec, S, grid,
+        grid, S, tokens, out_cotangent, segment_ids, w_qkv[0].transpose(1, 0, 2), qv_bias[0],
+        w_out[0], w_up[0], up_bias, w_down[0], add_bias[0], norm_gain[0], norm_bias[0],
     )
-    def own(v, size):
-        return lax.dynamic_slice_in_dim(v, c * size, size, axis=-1)
     if not grid:
         gall, gsm = lax.psum(gall, "dp"), lax.psum(gsm, "dp")
-    F = up_bias.shape[1]
-    block = gall.astype(F32).reshape(BUCKETS, 2, hd, hd)
-    gd = block[0:4].transpose(0, 2, 1, 3).reshape(F, D)
-    gu = block[4:8].reshape(4, D, hd).transpose(1, 0, 2).reshape(D, F)
-    gq = block[8:11].reshape(3, D, hd).transpose(1, 0, 2)
-    go = block[11].transpose(1, 0, 2).reshape(hd, D)
-    sq = own(gsm[0:3].reshape(-1), 3 * hd)
-    gqv = jnp.concatenate([sq[:hd], sq[2 * hd :]])
-    gub = own(gsm[3:7].reshape(-1), F)
-    gsv = own(gsm[8:14], hd)
+    gq, gqv, go, gu, gub, gd, ga, gg, gs = unpack_call(gall, gsm, D, FF)
     return (
-        lo[None], ig[None],
-        gq.reshape(1, D, 3, hd), gqv.reshape(1, 2, hd), go[None], gu[None], gub[None], gd[None],
-        gsv[None, 0:2], gsv[None, 2:4], gsv[None, 4:6],
+        lo[None], ig[None], gq.transpose(1, 0, 2)[None], gqv[None], go[None], gu[None], gub, gd[None],
+        ga[None], gg[None], gs[None],
     )
 
 

time: 330 us -> 263 us (0.80)
  local copies, waits for them, and re-layouts: 54.1 us -> 3.62 us
  Pallas kernels: 271 us -> 258 us
    another operation x4 -> x0, local copies, waits for them, and re-layouts: 17.8 us -> none  [the longest x1 7.16 us: shards(): gd[None]]
    transpose x3 -> x0, local copies, waits for them, and re-layouts: 14.2 us -> none  [the longest x1 7.49 us: shards(): gu = block[4:8].reshape(4, D, hd).transpose(1, 0, 2).reshape(D, F)]
    pallas_call x1 -> x2, Pallas kernels: 271 us -> 258 us  [the longest x1 246 us: main_call(): pl.pallas_call(partial(main_kernel, D, FF, S, grid), out_shape=(sds((rows...]
    slice x8 -> x0, local copies, waits for them, and re-layouts: 12.1 us -> none  [the longest x1 5.17 us: shards(): gd = block[0:4].transpose(0, 2, 1, 3).reshape(F, D)]
    broadcast_in_dim x9 -> x0, local copies, waits for them, and re-layouts: 3.95 us -> none  [the longest x2 0.86 us: shards(): seg[:, :, None]]
where the time goes in v3:
time: 263 us; the launch traced here: 262 us
  Pallas kernels  258 us (98%)
  local copies, waits for them, and re-layouts  3.62 us (1%)
    pallas_call x1, Pallas kernels, main_call(): pl.pallas_call(partial(main_kernel, D, FF, S, grid), out_shape=(sds((rows...  246 us
    pallas_call x1, Pallas kernels, unpack_call(): pl.pallas_call(partial(unpack_kernel, D), grid=(BUCKETS,), in_specs=[pl.B...  12.3 us

profile of v3, /device:TPU:0, one launch (start us, length us, event | category | flops | bytes accessed | tf_op | source)
XLA Modules:
  0.0 262.1 jit_solution(1164583011889069248)
XLA Ops:
  0.6 245.5 %layer_pass.1 = (bf16[512,768]{1,0:T(8,128)(2,1)}, f32[512,768]{1,0:T(8,128)}, bf16[9216,384]{1,0:T(8,128)(2,1)}, f32[16,768]{1,0:T(8,128)}) custom-call(bf16[512,768]{1,0:T(8,128)(2,1)} %tok.1, bf16[512,768]{1,0:T(8,128)(2,1)} %cot.1, s32[4,256]{1,0:T(4,128)} %seg.1, bf16[3,768,384]{2,1,0:T(8,128)(2,1)} %bitcast.24, bf16[2,384]{1,0:T(2,128)(2,1)} %bitcast.31, ...), custom_call_target="tpu_custom_call" | custom-call | tf_op jit(solution)/shard_map/layer_pass/pallas_call | solution.py:834
  246.2 0.0 copy-start
  246.2 0.8 copy-done
  247.0 0.0 copy-start.2
  247.0 12.3 %unpack.1 = (f32[3,768,384]{2,1,0:T(8,128)}, f32[2,384]{1,0:T(2,128)}, f32[384,768]{1,0:T(8,128)}, f32[768,1536]{1,0:T(8,128)}, f32[1,1536]{1,0:T(1,128)}, /*ind...) custom-call(bf16[9216,384]{1,0:T(8,128)(2,1)} %get-tuple-element.26.block, ...), custom_call_target="tpu_custom_call" | custom-call | tf_op jit(solution)/shard_map/unpack/pallas_call | solution.py:884
  259.3 0.0 copy-start.1
  259.3 0.0 copy-done.2
  259.3 0.9 copy.25
  260.2 0.8 copy-done.1
  261.0 1.1 copy.26
Async XLA Ops:
  246.2 0.8 copy-start
  247.0 12.3 %copy-start.2 = (bf16[512,768]{1,0:T(8,128)(2,1)S(1)}, bf16[512,768]{1,0:T(8,128)(2,1)}, u32[]{:S(2)}) copy-start(bf16[512,768]{1,0:T(8,128)(2,1)} %get-tuple-element.24) | copy-start | bytes 2359300
  259.3 1.7 copy-start.1

commit v4 on v3

--- a/solution.py
+++ b/solution.py
@@ -12,7 +12,8 @@
 masked_score = -1e30
 LINE = 4
 BUCKETS = 12
-A_ROWS = 512
+A_ROWS = (512,)
+MOST_A, MOST_B = 512, 256
 MESH = pl.DeviceIdType.MESH
 F32 = jnp.float32
 BF16 = jnp.bfloat16
@@ -54,14 +55,14 @@
 
 
 class Line:
-    def __init__(self, red, base, size, landing, sems):
-        self.red, self.base, self.size, self.landing, self.sems = red, base, size, landing, sems
+    def __init__(self, red, base, size, most, landing, sems):
+        self.red, self.base, self.size, self.most, self.landing, self.sems = red, base, size, most, landing, sems
 
     def own(self, b, j):
         return ds(self.base(b) + j * self.size, self.size, 16)
 
     def slot(self, b, j):
-        return ds((b * (LINE + 1) + j) * self.size, self.size, 16)
+        return ds(b * (LINE + 1) * self.most + j * self.size, self.size, 16)
 
     def sum_up(self, b, j):
         r = self.red
@@ -215,10 +216,14 @@
         self.above = (s, jnp.minimum(d + 2, 2 * LINE - 1), c)
         self.below = (s, jnp.maximum(d - 2, 0), c)
         self.beside = (s, d + 1 - 2 * self.y, c)
-        self.half = A_ROWS // 2
         self.D = D
-        self.a = Line(self, lambda b: b * D + self.y * self.half, self.half // LINE, LA, 0)
-        self.b = Line(self, lambda b: b * D + A_ROWS, (D - A_ROWS) // LINE, LB, 4 * LINE)
+        self.kinds = []
+        for a_rows in A_ROWS:
+            half = a_rows // 2
+            base = partial(lambda half, b: b * D + self.y * half, half)
+            a = Line(self, base, half // LINE, MOST_A // 2 // LINE, LA, 0)
+            base = partial(lambda a_rows, b: b * D + a_rows, a_rows)
+            self.kinds.append((half, a, Line(self, base, (D - a_rows) // LINE, MOST_B // LINE, LB, 4 * LINE)))
         z = self.z
         pair = z + 1 - 2 * (z % 2)
         far = (z + 2) % 4
@@ -256,28 +261,27 @@
         self.small_copy(k).wait()
         self.SM[...] += self.SML[k]
 
-    def give_side(self, b):
-        rows = ds(b * self.D + (1 - self.y) * self.half, self.half, 16)
-        return self.remote(self.G.at[rows], self.LA1.at[ds(b * self.half, self.half, 16)], b, 8 * LINE, self.beside)
-
-    def share_side(self, b):
-        rows = ds(b * self.D + self.y * self.half, self.half, 16)
+    def give_side(self, b, half):
+        rows = ds(b * self.D + (1 - self.y) * half, half, 16)
+        return self.remote(self.G.at[rows], self.LA1.at[ds(b * (MOST_A // 2), half, 16)], b, 8 * LINE, self.beside)
+
+    def share_side(self, b, half):
+        rows = ds(b * self.D + self.y * half, half, 16)
         return self.remote(self.out.at[rows], self.out.at[rows], b, 8 * LINE + 1, self.beside)
 
-    def swap(self, b):
-        size = self.b.size
-        return self.remote(self.G.at[self.b.own(b, self.z)], self.LS.at[ds(b * size, size, 16)], b, 8 * LINE + 2, self.beside)
-
-    def stage(self, k, b):
-        A, B = self.a, self.b
+    def swap(self, b, B):
+        return self.remote(self.G.at[B.own(b, self.z)], self.LS.at[ds(b * B.most, B.size, 16)], b, 8 * LINE + 2, self.beside)
+
+    def stage(self, k, b, kind):
+        half, A, B = kind
         if k == 0:
-            self.give_side(b).start()
+            self.give_side(b, half).start()
             B.begin(b)
         elif k == 1:
             B.pass_on(b, 0)
-            self.give_side(b).wait_recv()
-            rows = ds(b * self.D + self.y * self.half, self.half, 16)
-            land = ds(b * self.half, self.half, 16)
+            self.give_side(b, half).wait_recv()
+            rows = ds(b * self.D + self.y * half, half, 16)
+            land = ds(b * (MOST_A // 2), half, 16)
             self.G[rows, :] = (self.G[rows, :].astype(F32) + self.LA1[land, :].astype(F32)).astype(BF16)
             A.begin(b)
         elif k == 2:
@@ -285,14 +289,13 @@
             A.pass_on(b, 0)
         elif k == 3:
             B.finish_own(b)
-            self.swap(b).start()
+            self.swap(b, B).start()
             A.pass_on(b, 1)
         elif k == 4:
             A.finish_own(b)
             A.spread(b)
-            size = B.size
-            self.swap(b).wait()
-            rows, land = B.own(b, self.z), ds(b * size, size, 16)
+            self.swap(b, B).wait()
+            rows, land = B.own(b, self.z), ds(b * B.most, B.size, 16)
             self.G[rows, :] = (self.G[rows, :].astype(F32) + self.LS[land, :].astype(F32)).astype(BF16)
             B.spread(b)
         elif k <= 7:
@@ -300,25 +303,28 @@
             B.spread_on(b, k - 4)
             if k == 7:
                 A.keep(b).wait()
-                self.share_side(b).start()
+                self.share_side(b, half).start()
         else:
-            self.share_side(b).wait_recv()
+            self.share_side(b, half).wait_recv()
 
     def slot(self, tau):
         for k in range(self.stages - 1, -1, -1):
             b = tau - k
-
-            @pl.when((b >= 0) & (b < BUCKETS))
-            def _():
-                self.stage(k, b)
+            for i, kind in enumerate(self.kinds):
+                @pl.when((b >= 0) & (b < BUCKETS) & (b % len(self.kinds) == i))
+                def _():
+                    self.stage(k, b, kind)
 
     def drain(self):
         def one(b, _):
-            self.a.drain(b)
-            self.b.drain(b)
-            self.give_side(b).wait_send()
-            self.share_side(b).wait_send()
-            self.b.keep(b).wait()
+            for i, (half, A, B) in enumerate(self.kinds):
+                @pl.when(b % len(self.kinds) == i)
+                def _():
+                    A.drain(b)
+                    B.drain(b)
+                    self.give_side(b, half).wait_send()
+                    self.share_side(b, half).wait_send()
+                    B.keep(b).wait()
             return 0
         lax.fori_loop(0, BUCKETS, one, 0)
 
@@ -328,7 +334,7 @@
     tok, cot, seg, wq_in, qv_in, wo_in, wu_in, ub_in, wd_in, add_in, gain, shift,
     lo, ig, gall, gsm,
     wq, wo, wu, wd, bq, bu,
-    X, QKV, O, N1, N2, Hr, U, GP, R, DST, dB, dA, dOs, dQKV,
+    X, QKV, O, N1, N2, Hr, U, GP, R, dB, dA, dOs, dQKV,
     r1s, r2s, Hf, Zf, bias, dY, YB, IGB, IGF,
     sq, su, sv, SM, SML, G, LA1, LA, LB, LS,
     lsem, wsend, wrecv, rsend, rrecv, gsend, grecv, osem, ssend, srecv, asend, arecv, csem,
@@ -424,7 +430,7 @@
             finish(near, rows, n * gain[which : which + 1, :] + shift[which : which + 1, :])
             return 0
 
-        lax.fori_loop(0, S // 32, norm_rows, 0, unroll=4)
+        lax.fori_loop(0, S // 32, norm_rows, 0, unroll=True)
 
     def forward(t, m):
         rows = ds(m * S, S)
@@ -447,25 +453,27 @@
             QKV[rows, cols] = (mm(X[rows, :], wq[:, cols]) + bq[0:1, cols]).astype(BF16)
             return 0
 
-        lax.fori_loop(0, 3 * D // 256, qkv_tile, 0, unroll=3)
+        lax.fori_loop(0, 3 * D // 256, qkv_tile, 0, unroll=True)
 
         def attend(p, _):
             qc, kc, vc = pair_columns(p)
             q2, k2, v2 = QKV[rows, qc], QKV[rows, kc], QKV[rows, vc]
-            vt = v2.T
             weights = ds((m * pairs + p) * S, S)
             outs = []
-            for h, mask in enumerate((first_scaled, second_scaled)):
+            for h, (mask, half) in enumerate(((first_scaled, first_half), (second_scaled, second_half))):
                 kh = k2 * mask
+                shares = []
                 for part in range(0, S, 128):
                     st = mm_nt(kh, q2[part : part + 128, :]) + bias[m, :, part : part + 128]
                     e = jnp.exp(st - jnp.max(st, axis=0, keepdims=True))
-                    R[weights, h * S + part : h * S + part + 128] = (e * (1.0 / jnp.sum(e, axis=0, keepdims=True))).astype(BF16)
-                outs.append(mm(vt[h * HEAD_DIM : (h + 1) * HEAD_DIM], R[weights, h * S : (h + 1) * S]))
-            O[rows, ds(p * 128, 128)] = jnp.concatenate(outs, axis=0).T.astype(BF16)
-            return 0
-
-        lax.fori_loop(0, pairs, attend, 0, unroll=2)
+                    share = (e * (1.0 / jnp.sum(e, axis=0, keepdims=True))).astype(BF16)
+                    R[weights, h * S + part : h * S + part + 128] = share
+                    shares.append(share)
+                outs.append(mm_tn(jnp.concatenate(shares, axis=1), v2 * half))
+            O[rows, ds(p * 128, 128)] = (outs[0] + outs[1]).astype(BF16)
+            return 0
+
+        lax.fori_loop(0, pairs, attend, 0, unroll=True)
 
         @pl.when(t == 0)
         def _():
@@ -491,12 +499,14 @@
 
         def up_tile(i, _):
             cols = ds(i * 256, 256)
-            u, slope = gelu_and_slope(mm(Hr[rows, :], wu[:, cols]) + bu[0:1, cols])
-            U[rows, cols] = u.astype(BF16)
-            GP[rows, cols] = slope.astype(BF16)
-            return 0
-
-        lax.fori_loop(0, FF // 256, up_tile, 0, unroll=4)
+            g = mm(Hr[rows, :], wu[:, cols])
+            for j in range(0, S, 32):
+                u, slope = gelu_and_slope(g[j : j + 32] + bu[0:1, cols])
+                U[ds(m * S + j, 32), cols] = u.astype(BF16)
+                GP[ds(m * S + j, 32), cols] = slope.astype(BF16)
+            return 0
+
+        lax.fori_loop(0, FF // 256, up_tile, 0, unroll=True)
 
         @pl.when(t == 0)
         def _():
@@ -529,7 +539,7 @@
             low[rows, :] = dz.astype(BF16)
             return sums[0] + eights(dz), sums[1] + eights(dy * n), sums[2] + eights(dy)
 
-        sums = lax.fori_loop(0, S // 32, back_rows, (jnp.zeros((8, D), F32),) * 3, unroll=2)
+        sums = lax.fori_loop(0, S // 32, back_rows, (jnp.zeros((8, D), F32),) * 3, unroll=4)
         for i in range(3):
             sv[2 * i + which] += sums[i]
 
@@ -553,7 +563,7 @@
             GP[rows, cols] = dg.astype(BF16)
             return 0
 
-        lax.fori_loop(0, FF // 256, down_back, 0, unroll=4)
+        lax.fori_loop(0, FF // 256, down_back, 0, unroll=True)
         last(0)
 
         def up_back(i, _):
@@ -579,15 +589,15 @@
             do2 = dOs[:, ds(p * 128, 128)]
             kt = k2.T
             weights = ds((m * pairs + p) * S, S)
-            turn = p % 2
+            parts = []
             for h, half in enumerate((first_half, second_half)):
                 vh = v2 * half
                 for part in range(0, S, 128):
                     cols = slice(h * S + part, h * S + part + 128)
                     drt = mm_nt(vh, do2[part : part + 128, :])
                     rf = R[weights, cols].astype(F32)
-                    DST[turn, :, cols] = (rf * (drt - jnp.sum(rf * drt, axis=0, keepdims=True))).astype(BF16)
-            dst = DST[turn]
+                    parts.append((rf * (drt - jnp.sum(rf * drt, axis=0, keepdims=True))).astype(BF16))
+            dst = jnp.concatenate(parts, axis=1)
             dk = mm(dst, jnp.concatenate([q2 * first_scaled, q2 * second_scaled], axis=0))
             dv = mm(R[weights, :], jnp.concatenate([do2 * first_half, do2 * second_half], axis=0))
             dqt = [mm(kt[h * HEAD_DIM : (h + 1) * HEAD_DIM], dst[:, h * S : (h + 1) * S]) for h in range(2)]
@@ -600,7 +610,7 @@
             sq[:, vc] += eights(dvb.astype(F32))
             return 0
 
-        lax.fori_loop(0, pairs, attend_back, 0, unroll=2)
+        lax.fori_loop(0, pairs, attend_back, 0, unroll=True)
         last(3)
 
         def in_back(i, _):
@@ -733,39 +743,41 @@
     small_core = pltpu.make_async_remote_copy(SM, SML.at[0], ssend.at[0], srecv.at[0], device_id=core_peer, device_id_type=MESH)
     small_core.start()
 
-    def keep_up(i, _):
-        keep("up", i)
+    def keep_rest(i, _):
+        @pl.when(i < 2)
+        def _():
+            keep("up", 2 * i)
+            keep("up", 2 * i + 1)
+
+        @pl.when(i == 0)
+        def _():
+            give("qkv", 0)
+            give("qkv", 1)
+
+        @pl.when(i == 1)
+        def _():
+            give("qkv", 2)
+            give("out", 0)
+
+        @pl.when(i == 2)
+        def _():
+            keep("qkv", 0)
+            keep("qkv", 1)
+
+        @pl.when(i == 3)
+        def _():
+            keep("qkv", 2)
+            keep("out", 0)
+
         slot(4 + i)
-
-        @pl.when(i < 3)
-        def _():
-            give("qkv", i)
-
-        @pl.when(i == 3)
-        def _():
-            give("out", 0)
-
         return 0
 
-    lax.fori_loop(0, 4, keep_up, 0)
+    lax.fori_loop(0, 4, keep_rest, 0)
     small_core.wait()
     SM[...] += SML[0]
     if grid:
         ring.small_start(1)
 
-    def keep_rest(i, _):
-        @pl.when(i < 3)
-        def _():
-            keep("qkv", i)
-
-        @pl.when(i == 3)
-        def _():
-            keep("out", 0)
-
-        slot(8 + i)
-        return 0
-
-    lax.fori_loop(0, 4, keep_rest, 0)
     if grid:
         def last_slot(tau, _):
             slot(tau)
@@ -773,10 +785,10 @@
 
         ring.small_finish(1)
         ring.small_start(2)
-        lax.fori_loop(12, 14, last_slot, 0)
+        lax.fori_loop(8, 10, last_slot, 0)
         ring.small_finish(2)
         ring.small_start(3)
-        lax.fori_loop(14, BUCKETS + ring.stages - 1, last_slot, 0)
+        lax.fori_loop(10, BUCKETS + ring.stages - 1, last_slot, 0)
         ring.small_finish(3)
         ring.drain()
     else:
@@ -816,16 +828,16 @@
     vm_spec = pl.BlockSpec(memory_space=pltpu.VMEM)
     sds = jax.ShapeDtypeStruct
     V, DMA = pltpu.VMEM, pltpu.SemaphoreType.DMA
-    line_a, line_b = A_ROWS // 2 // LINE, (D - A_ROWS) // LINE
+    line_a, line_b = MOST_A // 2 // LINE, MOST_B // LINE
     scratch = [
         V((D, 2 * hq), BF16), V((D, D), BF16), V((D, FF), BF16), V((FF, D), BF16), V((8, 2 * hq), F32), V((8, FF), F32),
         V((rows, D), BF16), V((rows, 3 * D), BF16), V((rows, D), BF16), V((rows, D), BF16), V((rows, D), BF16), V((rows, D), BF16),
-        V((rows, FF), BF16), V((rows, FF), BF16), V((2 * (D // 128) * S, 2 * S), BF16), V((2, S, 2 * S), BF16),
+        V((rows, FF), BF16), V((rows, FF), BF16), V((2 * (D // 128) * S, 2 * S), BF16),
         V((rows, D), BF16), V((rows, D), BF16), V((S, D), BF16), V((rows, 3 * D), BF16),
         V((rows, 128), F32), V((rows, 128), F32), V((S, D), F32), V((S, D), F32), V((2, S, S), F32),
         V((rows, D), BF16), V((rows, D), BF16), V((rows, D), BF16), V((rows, D), F32),
         V((8, 2 * hq), F32), V((8, FF), F32), V((6, 8, D), F32), V((16, D), F32), V((4, 16, D), F32),
-        V((BUCKETS * D, hd), BF16), V((BUCKETS * A_ROWS // 2, hd), BF16), V((BUCKETS * line_a * (LINE + 1), hd), BF16),
+        V((BUCKETS * D, hd), BF16), V((BUCKETS * MOST_A // 2, hd), BF16), V((BUCKETS * line_a * (LINE + 1), hd), BF16),
         V((BUCKETS * line_b * (LINE + 1), hd), BF16), V((BUCKETS * line_b, hd), BF16),
         DMA((8,)), DMA((8,)), DMA((8,)), DMA((2,)), DMA((2,)),
         DMA((BUCKETS, 2)), DMA((BUCKETS, 2)), DMA((6,)), DMA((4,)), DMA((4,)),
@@ -842,59 +854,59 @@
     )(tok, cot, seg, wq, qv, wo, wu, ub, wd, add, gain, shift)
 
 
-def unpack_kernel(D, block, sums, gq, gqv, go, gu, gub, gd, ga, gg, gs):
-    b = pl.program_id(0)
+def unpack_kernel(D, FF, gall, sums, gq, gqv, go, gu, gub, gd, ga, gg, gs, low, wide, in_sem, out_sem):
     c = lax.axis_index("tensor")
     W = D // 2
-
-    @pl.when(b < 4)
-    def _():
-        for q in range(2):
-            gd[:, q * W : (q + 1) * W] = block[q * W : (q + 1) * W, :].astype(F32)
-
-    @pl.when((b >= 4) & (b < 8))
-    def _():
-        gu[...] = block[...].astype(F32)
-
-    @pl.when((b >= 8) & (b < 11))
-    def _():
-        gq[0] = block[...].astype(F32)
-
-    @pl.when(b == 11)
-    def _():
-        for q in range(2):
-            go[:, q * W : (q + 1) * W] = block[q * W : (q + 1) * W, :].astype(F32)
-        own = ds(c * W, W)
-        gqv[0:1, :] = sums[pl.ds(c, 1), own]
-        gqv[1:2, :] = sums[pl.ds(1 + c, 1), own]
-        for i in range(2):
-            gub[:, i * D : (i + 1) * D] = sums[pl.ds(3 + 2 * c + i, 1), :]
-            ga[i : i + 1, :] = sums[8 + i : 9 + i, own]
-            gg[i : i + 1, :] = sums[10 + i : 11 + i, own]
-            gs[i : i + 1, :] = sums[12 + i : 13 + i, own]
+    reads = [pltpu.make_async_copy(gall.at[b * D : (b + 1) * D], low.at[b], in_sem.at[b]) for b in range(BUCKETS)]
+    for read in reads:
+        read.start()
+    writes = []
+    for b in range(BUCKETS):
+        if b < 4 or b == 11:
+            rows = wide.at[b]
+            place = gd.at[b * W : (b + 1) * W, :] if b < 4 else go
+            parts = [(rows.at[q * W : (q + 1) * W], place.at[:, q * W : (q + 1) * W]) for q in range(2)]
+        elif b < 8:
+            parts = [(wide.at[b], gu.at[:, (b - 4) * W : (b - 3) * W])]
+        else:
+            parts = [(wide.at[b], gq.at[b - 8])]
+        writes.append([pltpu.make_async_copy(src, dst, out_sem.at[b, q]) for q, (src, dst) in enumerate(parts)])
+    own = ds(c * W, W)
+    gqv[0:1, :] = sums[pl.ds(c, 1), own]
+    gqv[1:2, :] = sums[pl.ds(1 + c, 1), own]
+    for i in range(2):
+        gub[:, i * D : (i + 1) * D] = sums[pl.ds(3 + 2 * c + i, 1), :]
+        ga[i : i + 1, :] = sums[8 + i : 9 + i, own]
+        gg[i : i + 1, :] = sums[10 + i : 11 + i, own]
+        gs[i : i + 1, :] = sums[12 + i : 13 + i, own]
+    for b in range(BUCKETS):
+        reads[b].wait()
+        wide[b] = low[b].astype(F32)
+        for copy in writes[b]:
+            copy.start()
+    for copies in writes:
+        for copy in copies:
+            copy.wait()
 
 
 def unpack_call(gall, gsm, D, FF):
     W, F = D // 2, FF // 2
     sds = jax.ShapeDtypeStruct
-
-    def whole(*shape):
-        return pl.BlockSpec(shape, lambda b: (0,) * len(shape))
-
+    any_spec = pl.BlockSpec(memory_space=pl.ANY)
+    vm_spec = pl.BlockSpec(memory_space=pltpu.VMEM)
     return pl.pallas_call(
-        partial(unpack_kernel, D),
-        grid=(BUCKETS,),
-        in_specs=[pl.BlockSpec((D, W), lambda b: (b, 0)), whole(16, D)],
-        out_specs=(
-            pl.BlockSpec((1, D, W), lambda b: (jnp.clip(b - 8, 0, 2), 0, 0)), whole(2, W), whole(W, D),
-            pl.BlockSpec((D, W), lambda b: (0, jnp.clip(b - 4, 0, 3))), whole(1, F),
-            pl.BlockSpec((W, D), lambda b: (jnp.minimum(b, 3), 0)), whole(2, W), whole(2, W), whole(2, W),
-        ),
+        partial(unpack_kernel, D, FF),
+        in_specs=[any_spec, vm_spec],
+        out_specs=(any_spec, vm_spec, any_spec, any_spec, vm_spec, any_spec, vm_spec, vm_spec, vm_spec),
         out_shape=(
             sds((3, D, W), F32), sds((2, W), F32), sds((W, D), F32), sds((D, F), F32), sds((1, F), F32),
             sds((F, D), F32), sds((2, W), F32), sds((2, W), F32), sds((2, W), F32),
         ),
-        compiler_params=pltpu.CompilerParams(vmem_limit_bytes=48 * 2**20),
+        scratch_shapes=[
+            pltpu.VMEM((BUCKETS, D, W), BF16), pltpu.VMEM((BUCKETS, D, W), F32),
+            pltpu.SemaphoreType.DMA((BUCKETS,)), pltpu.SemaphoreType.DMA((BUCKETS, 2)),
+        ],
+        compiler_params=pltpu.CompilerParams(vmem_limit_bytes=60 * 2**20),
         name="unpack",
     )(gall, gsm)
 

time: 263 us -> 248 us (0.943)
  Pallas kernels: 258 us -> 244 us
    pallas_call x1, Pallas kernels: 246 us -> 235 us  [main_call(): pl.pallas_call(partial(main_kernel, D, FF, S, grid), out_shape=(sds((rows...]
    pallas_call x1, Pallas kernels: 12.3 us -> 8.49 us  [unpack_call(): pl.pallas_call(partial(unpack_kernel, D, FF), in_specs=[any_spec, vm_spec...]
where the time goes in v4:
time: 248 us; the launch traced here: 247 us
  Pallas kernels  244 us (98%)
  local copies, waits for them, and re-layouts  2.82 us (1%)
    pallas_call x1, Pallas kernels, main_call(): pl.pallas_call(partial(main_kernel, D, FF, S, grid), out_shape=(sds((rows...  235 us
    pallas_call x1, Pallas kernels, unpack_call(): pl.pallas_call(partial(unpack_kernel, D, FF), in_specs=[any_spec, vm_spec...  8.49 us

profile of v4, /device:TPU:0, one launch (start us, length us, event | category | flops | bytes accessed | tf_op | source)
XLA Modules:
  0.0 247.4 jit_solution(9247324791601379401)
XLA Ops:
  0.6 235.4 %layer_pass.1 = (bf16[512,768]{1,0:T(8,128)(2,1)}, f32[512,768]{1,0:T(8,128)}, bf16[9216,384]{1,0:T(8,128)(2,1)}, f32[16,768]{1,0:T(8,128)}) custom-call(bf16[512,768]{1,0:T(8,128)(2,1)} %tok.1, bf16[512,768]{1,0:T(8,128)(2,1)} %cot.1, s32[4,256]{1,0:T(4,128)} %seg.1, bf16[3,768,384]{2,1,0:T(8,128)(2,1)} %bitcast.24, bf16[2,384]{1,0:T(2,128)(2,1)} %bitcast.31, ...), custom_call_target="tpu_custom_call" | custom-call | tf_op jit(solution)/shard_map/layer_pass/pallas_call | solution.py:846
  236.0 0.0 copy-start.1
  236.1 8.5 %unpack.1 = (f32[3,768,384]{2,1,0:T(8,128)}, f32[2,384]{1,0:T(2,128)}, f32[384,768]{1,0:T(8,128)}, f32[768,1536]{1,0:T(8,128)}, f32[1,1536]{1,0:T(1,128)}, /*ind...) custom-call(bf16[9216,384]{1,0:T(8,128)(2,1)} %get-tuple-element.26.gall, ...), custom_call_target="tpu_custom_call" | custom-call | tf_op jit(solution)/shard_map/unpack/pallas_call | solution.py:897
  244.6 0.0 copy-start
  244.6 0.0 copy-done.1
  244.6 0.9 copy.25
  245.5 0.8 copy-done
  246.2 1.1 copy.26
Async XLA Ops:
  236.0 8.5 %copy-start.1 = (bf16[512,768]{1,0:T(8,128)(2,1)S(1)}, bf16[512,768]{1,0:T(8,128)(2,1)}, u32[]{:S(2)}) copy-start(bf16[512,768]{1,0:T(8,128)(2,1)} %get-tuple-element.24) | copy-start | bytes 2359300
  244.6 1.7 copy-start

commit v5 on v4

--- a/solution.py
+++ b/solution.py
@@ -308,7 +308,7 @@
             self.share_side(b, half).wait_recv()
 
     def slot(self, tau):
-        for k in range(self.stages - 1, -1, -1):
+        for k in (7, 0, 6, 4, 3, 5, 2, 1, 8):
             b = tau - k
             for i, kind in enumerate(self.kinds):
                 @pl.when((b >= 0) & (b < BUCKETS) & (b % len(self.kinds) == i))
@@ -406,19 +406,20 @@
                 local[i].wait()
             remote[i].wait_recv()
 
-    def relay(m):
-        rows = ds(m * S, S)
-        return pltpu.make_async_remote_copy(YB.at[rows], X.at[rows], rsend.at[m], rrecv.at[m], device_id=x_peer, device_id_type=MESH)
+    def relay(m, part):
+        rows = ds(m * S + part * (S // 2), S // 2)
+        sem = 2 * m + part
+        return pltpu.make_async_remote_copy(YB.at[rows], X.at[rows], rsend.at[sem], rrecv.at[sem], device_id=x_peer, device_id_type=MESH)
 
     def relay_back(m):
         rows = ds(m * S, S)
-        return pltpu.make_async_remote_copy(IGB.at[rows], dY.at[rows], rsend.at[m], rrecv.at[m], device_id=x_peer, device_id_type=MESH)
+        return pltpu.make_async_remote_copy(IGB.at[rows], dY.at[rows], rsend.at[2 * m], rrecv.at[2 * m], device_id=x_peer, device_id_type=MESH)
 
     def pair_columns(p):
         base = (p // lo_pairs) * half_q + (p % lo_pairs) * 128
         return ds(base, 128), ds(base + half_d, 128), ds(base + 2 * half_d, 128)
 
-    def normed(m, which, N, rs, finish):
+    def normed(m, which, N, rs, finish, sent=None):
         def norm_rows(j, _):
             near, rows = ds(j * 32, 32), ds(m * S + j * 32, 32)
             z = Zf[near, :]
@@ -430,7 +431,10 @@
             finish(near, rows, n * gain[which : which + 1, :] + shift[which : which + 1, :])
             return 0
 
-        lax.fori_loop(0, S // 32, norm_rows, 0, unroll=True)
+        for part in range(2):
+            lax.fori_loop(part * S // 64, (part + 1) * S // 64, norm_rows, 0, unroll=True)
+            if sent is not None:
+                sent(part)
 
     def forward(t, m):
         rows = ds(m * S, S)
@@ -446,7 +450,8 @@
 
         @pl.when(s == 1)
         def _():
-            relay(m).wait_recv()
+            relay(m, 0).wait_recv()
+            relay(m, 1).wait_recv()
 
         def qkv_tile(i, _):
             cols = ds(i * 256, 256)
@@ -522,12 +527,13 @@
         def second_done(near, rows, y):
             YB[rows, :] = y.astype(BF16)
 
-        normed(m, 1, N2, r2s, second_done)
+        def send(part):
+            @pl.when(s == 0)
+            def _():
+                relay(m, part).start()
+
+        normed(m, 1, N2, r2s, second_done, send)
         pltpu.make_async_copy(YB.at[rows], lo.at[rows], osem.at[m]).start()
-
-        @pl.when(s == 0)
-        def _():
-            relay(m).start()
 
     def norm_back(m, which, get, N, rs, low):
         def back_rows(j, sums):
@@ -812,7 +818,8 @@
     @pl.when(s == 0)
     def _():
         for m in range(2):
-            relay(m).wait_send()
+            relay(m, 0).wait_send()
+            relay(m, 1).wait_send()
 
     @pl.when(s == 1)
     def _():
@@ -839,7 +846,7 @@
         V((8, 2 * hq), F32), V((8, FF), F32), V((6, 8, D), F32), V((16, D), F32), V((4, 16, D), F32),
         V((BUCKETS * D, hd), BF16), V((BUCKETS * MOST_A // 2, hd), BF16), V((BUCKETS * line_a * (LINE + 1), hd), BF16),
         V((BUCKETS * line_b * (LINE + 1), hd), BF16), V((BUCKETS * line_b, hd), BF16),
-        DMA((8,)), DMA((8,)), DMA((8,)), DMA((2,)), DMA((2,)),
+        DMA((8,)), DMA((8,)), DMA((8,)), DMA((4,)), DMA((4,)),
         DMA((BUCKETS, 2)), DMA((BUCKETS, 2)), DMA((6,)), DMA((4,)), DMA((4,)),
         DMA((BUCKETS, 8 * LINE + 3)), DMA((BUCKETS, 8 * LINE + 3)), DMA((BUCKETS, 2)),
     ]
@@ -854,12 +861,14 @@
     )(tok, cot, seg, wq, qv, wo, wu, ub, wd, add, gain, shift)
 
 
-def unpack_kernel(D, FF, gall, sums, gq, gqv, go, gu, gub, gd, ga, gg, gs, low, wide, in_sem, out_sem):
+def unpack_kernel(D, FF, gall, sums, lo, ig, gq, gqv, go, gu, gub, gd, ga, gg, gs, lo_out, ig_out, low, wide, lo_held, ig_held, in_sem, out_sem, pass_sem):
     c = lax.axis_index("tensor")
     W = D // 2
     reads = [pltpu.make_async_copy(gall.at[b * D : (b + 1) * D], low.at[b], in_sem.at[b]) for b in range(BUCKETS)]
-    for read in reads:
-        read.start()
+    held = [pltpu.make_async_copy(src, dst, pass_sem.at[i]) for i, (src, dst) in enumerate(((lo, lo_held), (ig, ig_held)))]
+    passed = [pltpu.make_async_copy(src, dst, pass_sem.at[2 + i]) for i, (src, dst) in enumerate(((lo_held, lo_out), (ig_held, ig_out)))]
+    for copy in held + reads:
+        copy.start()
     writes = []
     for b in range(BUCKETS):
         if b < 4 or b == 11:
@@ -879,36 +888,39 @@
         ga[i : i + 1, :] = sums[8 + i : 9 + i, own]
         gg[i : i + 1, :] = sums[10 + i : 11 + i, own]
         gs[i : i + 1, :] = sums[12 + i : 13 + i, own]
+    for read, write in zip(held, passed):
+        read.wait()
+        write.start()
     for b in range(BUCKETS):
         reads[b].wait()
         wide[b] = low[b].astype(F32)
         for copy in writes[b]:
             copy.start()
-    for copies in writes:
+    for copies in writes + [passed]:
         for copy in copies:
             copy.wait()
 
 
-def unpack_call(gall, gsm, D, FF):
+def unpack_call(gall, gsm, lo, ig, D, FF):
     W, F = D // 2, FF // 2
     sds = jax.ShapeDtypeStruct
     any_spec = pl.BlockSpec(memory_space=pl.ANY)
     vm_spec = pl.BlockSpec(memory_space=pltpu.VMEM)
     return pl.pallas_call(
         partial(unpack_kernel, D, FF),
-        in_specs=[any_spec, vm_spec],
-        out_specs=(any_spec, vm_spec, any_spec, any_spec, vm_spec, any_spec, vm_spec, vm_spec, vm_spec),
+        in_specs=[any_spec, vm_spec, any_spec, any_spec],
+        out_specs=(any_spec, vm_spec, any_spec, any_spec, vm_spec, any_spec, vm_spec, vm_spec, vm_spec, any_spec, any_spec),
         out_shape=(
             sds((3, D, W), F32), sds((2, W), F32), sds((W, D), F32), sds((D, F), F32), sds((1, F), F32),
-            sds((F, D), F32), sds((2, W), F32), sds((2, W), F32), sds((2, W), F32),
+            sds((F, D), F32), sds((2, W), F32), sds((2, W), F32), sds((2, W), F32), sds(lo.shape, lo.dtype), sds(ig.shape, ig.dtype),
         ),
         scratch_shapes=[
-            pltpu.VMEM((BUCKETS, D, W), BF16), pltpu.VMEM((BUCKETS, D, W), F32),
-            pltpu.SemaphoreType.DMA((BUCKETS,)), pltpu.SemaphoreType.DMA((BUCKETS, 2)),
+            pltpu.VMEM((BUCKETS, D, W), BF16), pltpu.VMEM((BUCKETS, D, W), F32), pltpu.VMEM(lo.shape, lo.dtype), pltpu.VMEM(ig.shape, ig.dtype),
+            pltpu.SemaphoreType.DMA((BUCKETS,)), pltpu.SemaphoreType.DMA((BUCKETS, 2)), pltpu.SemaphoreType.DMA((4,)),
         ],
         compiler_params=pltpu.CompilerParams(vmem_limit_bytes=60 * 2**20),
         name="unpack",
-    )(gall, gsm)
+    )(gall, gsm, lo, ig)
 
 
 def shards(tokens, segment_ids, out_cotangent, w_qkv, qv_bias, w_out, w_up, up_bias, w_down, add_bias, norm_gain, norm_bias):
@@ -922,7 +934,7 @@
     )
     if not grid:
         gall, gsm = lax.psum(gall, "dp"), lax.psum(gsm, "dp")
-    gq, gqv, go, gu, gub, gd, ga, gg, gs = unpack_call(gall, gsm, D, FF)
+    gq, gqv, go, gu, gub, gd, ga, gg, gs, lo, ig = unpack_call(gall, gsm, lo, ig, D, FF)
     return (
         lo[None], ig[None], gq.transpose(1, 0, 2)[None], gqv[None], go[None], gu[None], gub, gd[None],
         ga[None], gg[None], gs[None],

time: 248 us -> 241 us (0.972)
  Pallas kernels: 244 us -> 240 us
  local copies, waits for them, and re-layouts: 2.82 us -> 0 us
    pallas_call x1, Pallas kernels: 235 us -> 230 us  [main_call(): pl.pallas_call(partial(main_kernel, D, FF, S, grid), out_shape=(sds((rows...]
    unnamed x6 -> x0, local copies, waits for them, and re-layouts: 2.82 us -> none
where the time goes in v5:
time: 241 us
  Pallas kernels  240 us (100%)
    pallas_call x1, Pallas kernels, main_call(): pl.pallas_call(partial(main_kernel, D, FF, S, grid), out_shape=(sds((rows...  230 us
    pallas_call x1, Pallas kernels, unpack_call(): pl.pallas_call(partial(unpack_kernel, D, FF), in_specs=[any_spec, vm_spec...  10.8 us

profile of v5, /device:TPU:0, one launch (start us, length us, event | category | flops | bytes accessed | tf_op | source)
XLA Modules:
  0.0 241.2 jit_solution(11002675971386203550)
XLA Ops:
  0.6 229.6 %layer_pass.1 = (bf16[512,768]{1,0:T(8,128)(2,1)}, f32[512,768]{1,0:T(8,128)}, bf16[9216,384]{1,0:T(8,128)(2,1)}, f32[16,768]{1,0:T(8,128)}) custom-call(bf16[512,768]{1,0:T(8,128)(2,1)} %tok.1, bf16[512,768]{1,0:T(8,128)(2,1)} %cot.1, s32[4,256]{1,0:T(4,128)} %seg.1, bf16[3,768,384]{2,1,0:T(8,128)(2,1)} %bitcast.24, bf16[2,384]{1,0:T(2,128)(2,1)} %bitcast.29, ...), custom_call_target="tpu_custom_call" | custom-call | tf_op jit(solution)/shard_map/layer_pass/pallas_call | solution.py:853
  230.2 10.8 %unpack.1 = (f32[3,768,384]{2,1,0:T(8,128)}, f32[2,384]{1,0:T(2,128)}, f32[384,768]{1,0:T(8,128)}, f32[768,1536]{1,0:T(8,128)}, f32[1,1536]{1,0:T(1,128)}, /*ind...) custom-call(bf16[9216,384]{1,0:T(8,128)(2,1)} %get-tuple-element.26., ...), custom_call_target="tpu_custom_call" | custom-call | tf_op jit(solution)/shard_map/unpack/pallas_call | solution.py:909

commit v6 on v5

--- a/solution.py
+++ b/solution.py
@@ -12,6 +12,7 @@
 masked_score = -1e30
 LINE = 4
 BUCKETS = 12
+LENT, GUEST, GUEST_TURN = 4, 12, 8
 A_ROWS = (512,)
 MOST_A, MOST_B = 512, 256
 MESH = pl.DeviceIdType.MESH
@@ -207,8 +208,8 @@
 class Reduction:
     stages = 9
 
-    def __init__(self, D, s, d, c, G, out, LA1, LA, LB, LS, SM, SML, asend, arecv, ssend, srecv, csem):
-        self.out, self.csem = out, csem
+    def __init__(self, D, s, d, c, G, out, LA1, LA, LB, LS, SM, SML, asend, arecv, ssend, srecv, csem, xsend, xrecv):
+        self.out, self.csem, self.xsend, self.xrecv = out, csem, xsend, xrecv
         self.G, self.LA1, self.LS, self.SM, self.SML = G, LA1, LS, SM, SML
         self.asend, self.arecv, self.ssend, self.srecv = asend, arecv, ssend, srecv
         self.z, self.y = d // 2, d % 2
@@ -307,26 +308,67 @@
         else:
             self.share_side(b, half).wait_recv()
 
+    def turns(self):
+        return jnp.where(self.s == 0, BUCKETS - 1, BUCKETS + 1)
+
+    def bucket(self, turn):
+        lender = turn + jnp.where(turn >= LENT, 1, 0)
+        keeper = jnp.where(turn == GUEST_TURN, GUEST, turn - jnp.where(turn > GUEST_TURN, 1, 0))
+        return jnp.where(self.s == 0, lender, keeper)
+
+    def lend(self):
+        src, dst = self.G.at[LENT * self.D : (LENT + 1) * self.D], self.G.at[GUEST * self.D : (GUEST + 1) * self.D]
+        return pltpu.make_async_remote_copy(src, dst, self.xsend.at[0], self.xrecv.at[0], device_id=(1 - self.s, self.d, self.c), device_id_type=MESH)
+
+    def give_back(self):
+        src, dst = self.out.at[GUEST * self.D : (GUEST + 1) * self.D], self.out.at[LENT * self.D : (LENT + 1) * self.D]
+        return pltpu.make_async_remote_copy(src, dst, self.xsend.at[1], self.xrecv.at[1], device_id=(1 - self.s, self.d, self.c), device_id_type=MESH)
+
     def slot(self, tau):
         for k in (7, 0, 6, 4, 3, 5, 2, 1, 8):
-            b = tau - k
-            for i, kind in enumerate(self.kinds):
-                @pl.when((b >= 0) & (b < BUCKETS) & (b % len(self.kinds) == i))
+            turn = tau - k
+            b = self.bucket(turn)
+            if k == 0:
+                @pl.when((self.s == 1) & (turn == GUEST_TURN))
                 def _():
-                    self.stage(k, b, kind)
+                    self.lend().wait_recv()
+
+            @pl.when((turn >= 0) & (turn < self.turns()))
+            def _():
+                self.stage(k, b, self.kinds[0])
+
+    def guest_done(self):
+        @pl.when(self.s == 1)
+        def _():
+            self.kinds[0][2].keep(GUEST).wait()
+            self.give_back().start()
 
     def drain(self):
-        def one(b, _):
-            for i, (half, A, B) in enumerate(self.kinds):
-                @pl.when(b % len(self.kinds) == i)
-                def _():
-                    A.drain(b)
-                    B.drain(b)
-                    self.give_side(b, half).wait_send()
-                    self.share_side(b, half).wait_send()
-                    B.keep(b).wait()
-            return 0
-        lax.fori_loop(0, BUCKETS, one, 0)
+        half, A, B = self.kinds[0]
+
+        def one(turn, _):
+            b = self.bucket(turn)
+            A.drain(b)
+            B.drain(b)
+            self.give_side(b, half).wait_send()
+            self.share_side(b, half).wait_send()
+
+            @pl.when(b != GUEST)
+            def _():
+                B.keep(b).wait()
+
+            return 0
+
+        lax.fori_loop(0, self.turns(), one, 0)
+
+        @pl.when(self.s == 0)
+        def _():
+            self.lend().wait_send()
+            self.give_back().wait_recv()
+
+        @pl.when(self.s == 1)
+        def _():
+            self.give_back().wait_send()
 
 
 def main_kernel(
@@ -337,7 +379,7 @@
     X, QKV, O, N1, N2, Hr, U, GP, R, dB, dA, dOs, dQKV,
     r1s, r2s, Hf, Zf, bias, dY, YB, IGB, IGF,
     sq, su, sv, SM, SML, G, LA1, LA, LB, LS,
-    lsem, wsend, wrecv, rsend, rrecv, gsend, grecv, osem, ssend, srecv, asend, arecv, csem,
+    lsem, wsend, wrecv, rsend, rrecv, gsend, grecv, osem, ssend, srecv, asend, arecv, csem, xsend, xrecv,
 ):
     s = lax.axis_index("section")
     d = lax.axis_index("dp")
@@ -353,7 +395,7 @@
     pl.semaphore_signal(barrier, inc=1, device_id=core_peer, device_id_type=MESH)
     pl.semaphore_signal(barrier, inc=1, device_id=x_peer, device_id_type=MESH)
     if grid:
-        ring = Reduction(D, s, d, c, G, gall, LA1, LA, LB, LS, SM, SML, asend, arecv, ssend, srecv, csem)
+        ring = Reduction(D, s, d, c, G, gall, LA1, LA, LB, LS, SM, SML, asend, arecv, ssend, srecv, csem, xsend, xrecv)
         ring.greet(barrier)
 
     weights = [(wq_in.at[j], wq.at[:, ds(c * half_q + j * half_d, half_d)]) for j in range(3)] + [
@@ -755,6 +797,11 @@
             keep("up", 2 * i)
             keep("up", 2 * i + 1)
 
+        if grid:
+            @pl.when((i == 0) & (s == 0))
+            def _():
+                ring.lend().start()
+
         @pl.when(i == 0)
         def _():
             give("qkv", 0)
@@ -794,11 +841,13 @@
         lax.fori_loop(8, 10, last_slot, 0)
         ring.small_finish(2)
         ring.small_start(3)
-        lax.fori_loop(10, BUCKETS + ring.stages - 1, last_slot, 0)
+        lax.fori_loop(10, GUEST_TURN + ring.stages, last_slot, 0)
+        ring.guest_done()
+        lax.fori_loop(GUEST_TURN + ring.stages, ring.turns() + ring.stages - 1, last_slot, 0)
         ring.small_finish(3)
         ring.drain()
     else:
-        result = pltpu.make_async_copy(G, gall, osem.at[4])
+        result = pltpu.make_async_copy(G.at[0 : BUCKETS * D], gall.at[0 : BUCKETS * D], osem.at[4])
         result.start()
         result.wait()
     small_result = pltpu.make_async_copy(SM, gsm, osem.at[5])
@@ -835,6 +884,7 @@
     vm_spec = pl.BlockSpec(memory_space=pltpu.VMEM)
     sds = jax.ShapeDtypeStruct
     V, DMA = pltpu.VMEM, pltpu.SemaphoreType.DMA
+    slots = BUCKETS + 1
     line_a, line_b = MOST_A // 2 // LINE, MOST_B // LINE
     scratch = [
         V((D, 2 * hq), BF16), V((D, D), BF16), V((D, FF), BF16), V((FF, D), BF16), V((8, 2 * hq), F32), V((8, FF), F32),
@@ -844,15 +894,15 @@
         V((rows, 128), F32), V((rows, 128), F32), V((S, D), F32), V((S, D), F32), V((2, S, S), F32),
         V((rows, D), BF16), V((rows, D), BF16), V((rows, D), BF16), V((rows, D), F32),
         V((8, 2 * hq), F32), V((8, FF), F32), V((6, 8, D), F32), V((16, D), F32), V((4, 16, D), F32),
-        V((BUCKETS * D, hd), BF16), V((BUCKETS * MOST_A // 2, hd), BF16), V((BUCKETS * line_a * (LINE + 1), hd), BF16),
-        V((BUCKETS * line_b * (LINE + 1), hd), BF16), V((BUCKETS * line_b, hd), BF16),
+        V((slots * D, hd), BF16), V((slots * MOST_A // 2, hd), BF16), V((slots * line_a * (LINE + 1), hd), BF16),
+        V((slots * line_b * (LINE + 1), hd), BF16), V((slots * line_b, hd), BF16),
         DMA((8,)), DMA((8,)), DMA((8,)), DMA((4,)), DMA((4,)),
         DMA((BUCKETS, 2)), DMA((BUCKETS, 2)), DMA((6,)), DMA((4,)), DMA((4,)),
-        DMA((BUCKETS, 8 * LINE + 3)), DMA((BUCKETS, 8 * LINE + 3)), DMA((BUCKETS, 2)),
+        DMA((slots, 8 * LINE + 3)), DMA((slots, 8 * LINE + 3)), DMA((slots, 2)), DMA((2,)), DMA((2,)),
     ]
     return pl.pallas_call(
         partial(main_kernel, D, FF, S, grid),
-        out_shape=(sds((rows, D), BF16), sds((rows, D), F32), sds((BUCKETS * D, hd), BF16), sds((16, D), F32)),
+        out_shape=(sds((rows, D), BF16), sds((rows, D), F32), sds(((BUCKETS + 1) * D, hd), BF16), sds((16, D), F32)),
         in_specs=[any_spec, any_spec, vm_spec, any_spec, vm_spec, any_spec, any_spec, vm_spec, any_spec, vm_spec, vm_spec, vm_spec],
         out_specs=(any_spec,) * 4,
         scratch_shapes=scratch,
@@ -933,7 +983,7 @@
         w_out[0], w_up[0], up_bias, w_down[0], add_bias[0], norm_gain[0], norm_bias[0],
     )
     if not grid:
-        gall, gsm = lax.psum(gall, "dp"), lax.psum(gsm, "dp")
+        gall, gsm = lax.psum(gall[: BUCKETS * D], "dp"), lax.psum(gsm, "dp")
     gq, gqv, go, gu, gub, gd, ga, gg, gs, lo, ig = unpack_call(gall, gsm, lo, ig, D, FF)
     return (
         lo[None], ig[None], gq.transpose(1, 0, 2)[None], gqv[None], go[None], gu[None], gub, gd[None],

time: 241 us -> 238 us (0.988)
  the two profiles are of different devices: /device:TPU:0 before, /device:TPU:6 now
where the time goes in v6:
time: 238 us; the launch traced here: 237 us
  Pallas kernels  237 us (100%)
    pallas_call x1, Pallas kernels, main_call(): pl.pallas_call(partial(main_kernel, D, FF, S, grid), out_shape=(sds((rows...  226 us
    pallas_call x1, Pallas kernels, unpack_call(): pl.pallas_call(partial(unpack_kernel, D, FF), in_specs=[any_spec, vm_spec...  10.8 us

profile of v6, /device:TPU:6, one launch (start us, length us, event | category | flops | bytes accessed | tf_op | source)
XLA Modules:
  0.0 237.5 jit_solution(7293934926963262674)
XLA Ops:
  0.6 225.8 %layer_pass.1 = (bf16[512,768]{1,0:T(8,128)(2,1)}, f32[512,768]{1,0:T(8,128)}, bf16[9984,384]{1,0:T(8,128)(2,1)}, f32[16,768]{1,0:T(8,128)}) custom-call(bf16[512,768]{1,0:T(8,128)(2,1)} %tok.1, bf16[512,768]{1,0:T(8,128)(2,1)} %cot.1, s32[4,256]{1,0:T(4,128)} %seg.1, bf16[3,768,384]{2,1,0:T(8,128)(2,1)} %bitcast.24, bf16[2,384]{1,0:T(2,128)(2,1)} %bitcast.29, ...), custom_call_target="tpu_custom_call" | custom-call | tf_op jit(solution)/shard_map/layer_pass/pallas_call | solution.py:903
  226.5 10.8 %unpack.1 = (f32[3,768,384]{2,1,0:T(8,128)}, f32[2,384]{1,0:T(2,128)}, f32[384,768]{1,0:T(8,128)}, f32[768,1536]{1,0:T(8,128)}, f32[1,1536]{1,0:T(1,128)}, /*ind...) custom-call(bf16[9984,384]{1,0:T(8,128)(2,1)} %get-tuple-element.26., ...), custom_call_target="tpu_custom_call" | custom-call | tf_op jit(solution)/shard_map/unpack/pallas_call | solution.py:959

commit v7 on v6

--- a/solution.py
+++ b/solution.py
@@ -325,7 +325,7 @@
         return pltpu.make_async_remote_copy(src, dst, self.xsend.at[1], self.xrecv.at[1], device_id=(1 - self.s, self.d, self.c), device_id_type=MESH)
 
     def slot(self, tau):
-        for k in (7, 0, 6, 4, 3, 5, 2, 1, 8):
+        for k in (7, 0, 6, 5, 4, 3, 2, 1, 8):
             turn = tau - k
             b = self.bucket(turn)
             if k == 0:
@@ -682,8 +682,9 @@
 
     def grad_tiles(k, kind, i):
         if kind == "down":
-            left = U[:, ds(k * half_f + i * W, W, 128)].T
-            return [mm(left, dB[:, q * W : (q + 1) * W]) for q in range(2)]
+            left = U[:, ds(k * half_f + i * W, W, 128)]
+            whole = mm_tn(left, dB[...])
+            return [whole[:, q * W : (q + 1) * W] for q in range(2)]
         if kind == "out":
             return [across(1, k * half_d, W, dA[:, q * W : (q + 1) * W]) for q in range(2)]
         cols = ds(k * (half_f if kind == "up" else half_q) + i * W, W, 128)

time: 238 us -> 234 us (0.983)
  the two profiles are of different devices: /device:TPU:6 before, /device:TPU:0 now
where the time goes in v7:
time: 234 us; the launch traced here: 231 us
  Pallas kernels  230 us (98%)
    pallas_call x1, Pallas kernels, main_call(): pl.pallas_call(partial(main_kernel, D, FF, S, grid), out_shape=(sds((rows...  220 us
    pallas_call x1, Pallas kernels, unpack_call(): pl.pallas_call(partial(unpack_kernel, D, FF), in_specs=[any_spec, vm_spec...  10.8 us

profile of v7, /device:TPU:0, one launch (start us, length us, event | category | flops | bytes accessed | tf_op | source)
XLA Modules:
  0.0 231.2 jit_solution(6266549822157648094)
XLA Ops:
  0.6 219.6 %layer_pass.1 = (bf16[512,768]{1,0:T(8,128)(2,1)}, f32[512,768]{1,0:T(8,128)}, bf16[9984,384]{1,0:T(8,128)(2,1)}, f32[16,768]{1,0:T(8,128)}) custom-call(bf16[512,768]{1,0:T(8,128)(2,1)} %tok.1, bf16[512,768]{1,0:T(8,128)(2,1)} %cot.1, s32[4,256]{1,0:T(4,128)} %seg.1, bf16[3,768,384]{2,1,0:T(8,128)(2,1)} %bitcast.24, bf16[2,384]{1,0:T(2,128)(2,1)} %bitcast.29, ...), custom_call_target="tpu_custom_call" | custom-call | tf_op jit(solution)/shard_map/layer_pass/pallas_call | solution.py:904
  220.2 10.8 %unpack.1 = (f32[3,768,384]{2,1,0:T(8,128)}, f32[2,384]{1,0:T(2,128)}, f32[384,768]{1,0:T(8,128)}, f32[768,1536]{1,0:T(8,128)}, f32[1,1536]{1,0:T(1,128)}, /*ind...) custom-call(bf16[9984,384]{1,0:T(8,128)(2,1)} %get-tuple-element.26., ...), custom_call_target="tpu_custom_call" | custom-call | tf_op jit(solution)/shard_map/unpack/pallas_call | solution.py:960
